TPU v7x, 32 devices: a whole 2x2x4 slice. The times are simulated.
32 devices in a mesh: seq: 4 (over z), batch: 8 (over y, x, core).
Axes of the slice: x: 2, y: 2, z: 4, core: 2. Of those that a mesh axis runs over, the one named last changes fastest.
Arguments:
- image: bfloat16 [8, 128, 32, 512], P('batch', 'seq'), may hold values from -64 to 64
- tile_map: int32 [8, 128, 32], P('batch', 'seq'), may hold values from 0 to 1003, as said below
- out_grad: bfloat16 [8, 128, 32, 512], P('batch', 'seq'), may hold values from -6 to 6
- conv_weight: bfloat16 [2, 3, 3, 512, 512], replicated, may hold values from -0.09375 to 0.09375
- conv_bias: bfloat16 [2, 512], replicated, may hold values from -1.75 to 1.75
- norm_gain: bfloat16 [3, 512], replicated, may hold values from 0.5 to 1.5
- norm_shift: bfloat16 [3, 512], replicated, may hold values from -2.5 to 2.5
- qk_weight: bfloat16 [2, 512, 512], replicated, may hold values from -0.375 to 0.375
- value_weight: bfloat16 [512, 512], replicated, may hold values from -0.25 to 0.25
- proj_weight: bfloat16 [512, 512], replicated, may hold values from -1 to 1
- qv_bias: bfloat16 [2, 512], replicated, may hold values from -1.75 to 1.75
- proj_bias: bfloat16 [512], replicated, may hold values from -1.75 to 1.75
Outputs:
- output: bfloat16 [8, 128, 32, 512], P('batch', 'seq')
- image_grad: bfloat16 [8, 128, 32, 512], P('batch', 'seq')
- conv_weight_grad: float32 [2, 3, 3, 512, 512], replicated
- conv_bias_grad: float32 [2, 512], replicated
- norm_gain_grad: float32 [3, 512], replicated
- norm_shift_grad: float32 [3, 512], replicated
- qk_weight_grad: float32 [2, 512, 512], replicated
- value_weight_grad: float32 [512, 512], replicated
- proj_weight_grad: float32 [512, 512], replicated
- qv_bias_grad: float32 [2, 512], replicated
- proj_bias_grad: float32 [512], replicated
Inputs may be any that keep to these rules, and one draw needn't show every extreme that they name: `tile_map`: tile ids label regions of a canvas: each tile is one region of pixels, and distinct tiles of a canvas have distinct ids.
All inputs are finite; a program needn't handle non-finite values.
Results may differ from a plain program's by a relative error of at most 0.017.
The roundings to bfloat16 on the way count: a program that leaves them out, or rounds other values in their place, can miss the bound.
Values may be sent and summed in bfloat16 or wider, within the bound.
No kernel may reach another device: no remote copies, remote signals or barrier semaphores. Data moves between devices by JAX's collectives and lax.ppermute only.
A program may use at most 256 MiB of HBM per device.

v0:
```python
import jax
import jax.numpy as jnp
from jax import lax
from jax.sharding import PartitionSpec as P

GROUPS = 32


EPSILON = 1e-06
MASKED_SCORE = -1e30


def padded_2(x, sides, width):
    for axis, dim in sides:
        devices, length = (lax.axis_size(axis), x.shape[dim])
        up = [(i, (i + 1) % devices) for i in range(devices - 1)]
        down = [(j, i) for i, j in up]
        last = lax.slice_in_dim(x, length - width, length, axis=dim)
        leading = lax.slice_in_dim(x, 0, width, axis=dim)
        before = lax.ppermute(last, axis, up)
        after = lax.ppermute(leading, axis, down)
        x = jnp.concatenate([before, x, after], axis=dim)
    return x


def inner_rows(left, right):
    return lax.dot_general(
        left, right, (((0,), (0,)), ((), ())), preferred_element_type=jnp.float32
    )


def across_rows(left, right):
    return lax.dot_general(
        left, right, (((1,), (1,)), ((), ())), preferred_element_type=jnp.float32
    )


def swish_slope(pre_act):
    sigmoid = jax.nn.sigmoid(pre_act)
    return (pre_act * sigmoid, sigmoid * (1.0 + pre_act * (1.0 - sigmoid)))


def group_stats(grouped, group_count):
    group_mean = lax.psum(jnp.sum(grouped, axis=(0, 2)), "seq") / group_count
    centered = grouped - group_mean[None, :, None]
    group_var = lax.psum(jnp.sum(centered * centered, axis=(0, 2)), "seq") / group_count
    return (group_mean, lax.rsqrt(group_var + EPSILON))


def norm_forward(values, gain, shift, group_count):
    pixel_rows, channels = values.shape
    grouped = values.reshape(pixel_rows, GROUPS, channels // GROUPS)
    group_mean, inverse = group_stats(grouped, group_count)
    normal_form = ((grouped - group_mean[None, :, None]) * inverse[None, :, None]).reshape(
        pixel_rows, channels
    )
    return (normal_form, inverse, normal_form * gain + shift)


def norm_backward(upstream, normal_form, inverse, gain, group_count):
    pixel_rows, channels = upstream.shape
    hat_grad = (upstream * gain).reshape(pixel_rows, GROUPS, channels // GROUPS)
    hat_rows = normal_form.reshape(pixel_rows, GROUPS, channels // GROUPS)
    first_sum, second_sum = lax.psum(
        (jnp.sum(hat_grad, axis=(0, 2)), jnp.sum(hat_grad * hat_rows, axis=(0, 2))), "seq"
    )
    input_grad = inverse[None, :, None] * (
        hat_grad
        - (first_sum / group_count)[None, :, None]
        - hat_rows * (second_sum / group_count)[None, :, None]
    )
    return (
        input_grad.reshape(pixel_rows, channels),
        jnp.sum(upstream * normal_form, axis=0),
        jnp.sum(upstream, axis=0),
    )


def gather_taps(padded, tap_masks):
    band_rows, canvas_width = (tap_masks.shape[1], tap_masks.shape[2])
    widened = jnp.pad(padded, ((0, 0), (1, 1), (0, 0)))
    columns = [
        widened[row_off : row_off + band_rows, col_off : col_off + canvas_width]
        * tap_masks[row_off * 3 + col_off][:, :, None]
        for row_off in range(3)
        for col_off in range(3)
    ]
    return jnp.stack(columns, 2).reshape(band_rows * canvas_width, -1)


def conv_forward(field, weight_flat, tap_masks):
    padded = padded_2(field, (("seq", 0),), 1)
    tap_rows = gather_taps(padded, tap_masks)
    return (tap_rows, jnp.dot(tap_rows, weight_flat, preferred_element_type=jnp.float32))


def conv_back(grad_field, weight_back, tap_masks):
    padded = padded_2(grad_field, (("seq", 0),), 1)
    tap_rows = gather_taps(padded, tap_masks)
    return jnp.dot(tap_rows, weight_back, preferred_element_type=jnp.float32)


def body(
    image,
    tile_map,
    out_grad,
    conv_weight,
    conv_bias,
    norm_gain,
    norm_shift,
    qk_weight,
    value_weight,
    proj_weight,
    qv_bias,
    proj_bias,
):
    band_rows, canvas_width, channels = (image.shape[1], image.shape[2], image.shape[3])
    pixel_rows = band_rows * canvas_width
    group_count = float(pixel_rows * lax.axis_size("seq") * (channels // GROUPS))
    score_scale = channels ** (-0.5)
    own_tiles = tile_map[0]
    whole_tiles = lax.all_gather(own_tiles, "seq", axis=0, tiled=True)
    framed = jnp.pad(whole_tiles, 1, constant_values=-1)
    first_row = lax.axis_index("seq") * band_rows
    near_tiles = lax.dynamic_slice(
        framed, (first_row, jnp.int32(0)), (band_rows + 2, canvas_width + 2)
    )
    tap_masks = jnp.stack(
        [
            near_tiles[row_off : row_off + band_rows, col_off : col_off + canvas_width] == own_tiles
            for row_off in range(3)
            for col_off in range(3)
        ]
    ).astype(jnp.bfloat16)
    gains = norm_gain.astype(jnp.float32)
    shifts = norm_shift.astype(jnp.float32)
    biases = conv_bias.astype(jnp.float32)
    weight_one = conv_weight[0].reshape(9 * channels, channels)
    weight_two = conv_weight[1].reshape(9 * channels, channels)
    inputs = image[0].astype(jnp.float32).reshape(pixel_rows, channels)
    first_hat, first_scale, first_pre = norm_forward(inputs, gains[0], shifts[0], group_count)
    first_act, first_slope = swish_slope(first_pre)
    first_taps, first_conv = conv_forward(
        first_act.astype(jnp.bfloat16).reshape(band_rows, canvas_width, channels),
        weight_one,
        tap_masks,
    )
    middle = first_conv + biases[0]
    second_hat, second_scale, second_pre = norm_forward(middle, gains[1], shifts[1], group_count)
    second_act, second_slope = swish_slope(second_pre)
    second_taps, second_conv = conv_forward(
        second_act.astype(jnp.bfloat16).reshape(band_rows, canvas_width, channels),
        weight_two,
        tap_masks,
    )
    residual = inputs + second_conv + biases[1]
    third_hat, third_scale, third_pre = norm_forward(residual, gains[2], shifts[2], group_count)
    normed = third_pre.astype(jnp.bfloat16)
    bias_rows = qv_bias.astype(jnp.float32)
    queries = (
        jnp.dot(normed, qk_weight[0], preferred_element_type=jnp.float32) + bias_rows[0]
    ).astype(jnp.bfloat16)
    key_rows = jnp.dot(normed, qk_weight[1], preferred_element_type=jnp.float32).astype(
        jnp.bfloat16
    )
    value_rows = (
        jnp.dot(normed, value_weight, preferred_element_type=jnp.float32) + bias_rows[1]
    ).astype(jnp.bfloat16)
    own_flat = own_tiles.reshape(pixel_rows)
    all_flat = whole_tiles.reshape(-1)
    row_max = jnp.full((pixel_rows,), MASKED_SCORE, jnp.float32)
    key_piece = lax.all_gather(key_rows, "seq", axis=0, tiled=True)
    value_piece = lax.all_gather(value_rows, "seq", axis=0, tiled=True)
    allowed = own_flat[:, None] == all_flat[None, :]
    scores = jnp.where(allowed, across_rows(queries, key_piece) * score_scale, MASKED_SCORE)
    newest = jnp.maximum(row_max, jnp.max(scores, axis=1))
    weights = jnp.where(allowed, jnp.exp(scores - newest[:, None]), 0.0)
    row_sum = jnp.sum(weights, axis=1)
    weighted = jnp.dot(
        weights.astype(jnp.bfloat16), value_piece, preferred_element_type=jnp.float32
    )
    row_max, row_sum, weighted = (newest, row_sum, weighted)
    attended = weighted / row_sum[:, None]
    log_total = row_max + jnp.log(row_sum)
    attended_b = attended.astype(jnp.bfloat16)
    result = (
        residual
        + jnp.dot(attended_b, proj_weight, preferred_element_type=jnp.float32)
        + proj_bias.astype(jnp.float32)
    )
    cotangent = out_grad[0].reshape(pixel_rows, channels)
    cot_float = cotangent.astype(jnp.float32)
    proj_grad = inner_rows(attended_b, cotangent)
    proj_bias_rows = jnp.sum(cot_float, axis=0)[None, :]
    grad_att = across_rows(cotangent, proj_weight).astype(jnp.bfloat16)
    all_keys, all_values = (
        lax.all_gather(key_rows, "seq", axis=0, tiled=True),
        lax.all_gather(value_rows, "seq", axis=0, tiled=True),
    )
    allowed = own_flat[:, None] == all_flat[None, :]
    scores = across_rows(queries, all_keys) * score_scale
    attention = jnp.where(allowed, jnp.exp(scores - log_total[:, None]), 0.0)
    prob_grad = across_rows(grad_att, all_values)
    row_delta = jnp.sum(attention * prob_grad, axis=1)
    score_grad = (attention * (prob_grad - row_delta[:, None])).astype(jnp.bfloat16)
    grad_query = (
        jnp.dot(score_grad, all_keys, preferred_element_type=jnp.float32) * score_scale
    ).astype(jnp.bfloat16)
    attention_b = attention.astype(jnp.bfloat16)
    key_part = inner_rows(score_grad, queries) * score_scale
    value_part = inner_rows(attention_b, grad_att)
    pair_sums = lax.psum_scatter(
        jnp.concatenate([key_part, value_part], axis=1).astype(jnp.bfloat16),
        "seq",
        scatter_dimension=0,
        tiled=True,
    ).astype(jnp.float32)
    grad_key = pair_sums[:, :channels].astype(jnp.bfloat16)
    grad_value = pair_sums[:, channels:].astype(jnp.bfloat16)
    qk_rows = jnp.concatenate(
        [inner_rows(normed, grad_query), inner_rows(normed, grad_key)], axis=0
    )
    value_grad = inner_rows(normed, grad_value)
    qv_rows = jnp.stack(
        [
            jnp.sum(grad_query.astype(jnp.float32), axis=0),
            jnp.sum(grad_value.astype(jnp.float32), axis=0),
        ]
    )
    normed_grad = (
        across_rows(grad_query, qk_weight[0])
        + across_rows(grad_key, qk_weight[1])
        + across_rows(grad_value, value_weight)
    )
    third_grad, third_gain, third_shift = norm_backward(
        normed_grad, third_hat, third_scale, gains[2], group_count
    )
    residual_grad = cot_float + third_grad
    conv_grad_two = residual_grad.astype(jnp.bfloat16)
    bias_two = jnp.sum(residual_grad, axis=0)
    weight_two_grad = inner_rows(second_taps, conv_grad_two)
    back_two = jnp.swapaxes(conv_weight[1][::-1, ::-1], 2, 3).reshape(9 * channels, channels)
    act_two_grad = conv_back(
        conv_grad_two.reshape(band_rows, canvas_width, channels), back_two, tap_masks
    )
    middle_grad, second_gain, second_shift = norm_backward(
        act_two_grad * second_slope, second_hat, second_scale, gains[1], group_count
    )
    conv_grad_one = middle_grad.astype(jnp.bfloat16)
    bias_one = jnp.sum(middle_grad, axis=0)
    weight_one_grad = inner_rows(first_taps, conv_grad_one)
    back_one = jnp.swapaxes(conv_weight[0][::-1, ::-1], 2, 3).reshape(9 * channels, channels)
    act_one_grad = conv_back(
        conv_grad_one.reshape(band_rows, canvas_width, channels), back_one, tap_masks
    )
    input_grad, first_gain, first_shift = norm_backward(
        act_one_grad * first_slope, first_hat, first_scale, gains[0], group_count
    )
    image_grad = (
        (residual_grad + input_grad)
        .astype(jnp.bfloat16)
        .reshape(1, band_rows, canvas_width, channels)
    )
    conv_rows = jnp.concatenate([weight_one_grad, weight_two_grad], axis=0)
    bias_pair = jnp.stack([bias_one, bias_two])
    gain_rows = jnp.stack([first_gain, second_gain, third_gain])
    shift_rows = jnp.stack([first_shift, second_shift, third_shift])
    summed = lax.psum(
        (
            conv_rows,
            bias_pair,
            gain_rows,
            shift_rows,
            qk_rows,
            value_grad,
            proj_grad,
            qv_rows,
            proj_bias_rows,
        ),
        ("seq", "batch"),
    )
    output = result.astype(jnp.bfloat16).reshape(1, band_rows, canvas_width, channels)
    return (
        output,
        image_grad,
        summed[0].reshape(2, 3, 3, channels, channels),
        summed[1],
        summed[2],
        summed[3],
        summed[4].reshape(2, channels, channels),
        summed[5],
        summed[6],
        summed[7],
        summed[8].reshape(channels),
    )


def solution(mesh):
    in_specs = (
        P("batch", "seq", None, None),
        P("batch", "seq", None),
        P("batch", "seq", None, None),
        P(),
        P(),
        P(),
        P(),
        P(),
        P(),
        P(),
        P(),
        P(),
    )
    out_specs = (
        P("batch", "seq", None, None),
        P("batch", "seq", None, None),
        P(),
        P(),
        P(),
        P(),
        P(),
        P(),
        P(),
        P(),
        P(),
    )
    return jax.shard_map(body, mesh=mesh, in_specs=in_specs, out_specs=out_specs, check_vma=False)
```

profile of v0, /device:TPU:0, one launch (start us, length us, event | category | flops | bytes accessed | tf_op | source)
XLA Modules:
  0.0 1138.0 jit_solution(11943703197432542081)
XLA Ops:
  10.6 13.5 %psum.147 = f32[32]{0:T(128)S(1)} all-reduce(f32[32]{0:T(128)S(1)} %reduce_sum.256), channel_id=1, replica_groups=mesh['seq'=4,'batch'=8] {'seq'}, use_global_device_ids=true, to_apply=%region_2.3 | all-reduce | flops 32 | bytes 256 | tf_op jit(solution)/shard_map/psum | solution.py:44
  43.3 13.2 %all-gather = s32[1,128,32]{2,1,0:T(8,128)S(1)} all-gather(s32[1,32,32]{2,1,0:T(8,128)S(1)} %copy-done.18), channel_id=2, replica_groups=mesh['seq'=4,'batch'=8] {'seq'}, dimensions={1}, use_global_device_ids=true | all-gather | bytes 20480 | tf_op jit(solution)/shard_map/all_gather | solution.py:122
  71.6 30.9 %copy.29 = bf16[32,32,9,512]{3,2,1,0:T(8,128)(2,1)S(1)} copy(bf16[32,32,9,512]{3,1,0,2:T(8,128)(2,1)S(1)} %fusion.116) | data formatting | bytes 18874368 | tf_op jit(solution)/shard_map/stack | solution.py:88
  102.5 17.5 %copy.35 = bf16[128,8,9,512]{3,1,2,0:T(8,128)(2,1)S(1)} copy(bf16[128,8,9,512]{3,2,1,0:T(8,128)(2,1)S(1)} %bitcast.414) | data formatting | bytes 18874368
  126.6 21.4 %psum.149 = f32[32]{0:T(128)S(1)} all-reduce(f32[32]{0:T(128)S(1)} %reduce_sum.265), channel_id=1, replica_groups=mesh['seq'=4,'batch'=8] {'seq'}, use_global_device_ids=true, to_apply=%region_8.9 | all-reduce | flops 32 | bytes 256 | tf_op jit(solution)/shard_map/psum | solution.py:44
  173.2 30.9 %copy.30 = bf16[32,32,9,512]{3,2,1,0:T(8,128)(2,1)S(1)} copy(bf16[32,32,9,512]{3,1,0,2:T(8,128)(2,1)S(1)} %fusion.98) | data formatting | bytes 18874368 | tf_op jit(solution)/shard_map/stack | solution.py:88
  204.1 17.5 %copy.36 = bf16[128,8,9,512]{3,1,2,0:T(8,128)(2,1)S(1)} copy(bf16[128,8,9,512]{3,2,1,0:T(8,128)(2,1)S(1)} %bitcast.415) | data formatting | bytes 18874368
  228.2 11.6 %psum.151 = f32[32]{0:T(128)S(1)} all-reduce(f32[32]{0:T(128)S(1)} %reduce_sum.323), channel_id=1, replica_groups=mesh['seq'=4,'batch'=8] {'seq'}, use_global_device_ids=true, to_apply=%region_14.15 | all-reduce | flops 32 | bytes 256 | tf_op jit(solution)/shard_map/psum | solution.py:44
  263.2 70.9 %all-gather.4.cloned.1.call-done = bf16[4096,512]{1,0:T(8,128)(2,1)} async-done(((bf16[1024,512]{1,0:T(8,128)(2,1)}), bf16[4096,512]{1,0:T(8,128)(2,1)}) %all-gather.4.cloned.1.call-update) | async-done | bytes 4194320 | tf_op jit(solution)/shard_map/all_gather | solution.py:172
  355.9 59.7 %all-gather.6.cloned.1.call-done = bf16[4096,512]{1,0:T(8,128)(2,1)} async-done(((bf16[1024,512]{1,0:T(8,128)(2,1)}), bf16[4096,512]{1,0:T(8,128)(2,1)}) %all-gather.6.cloned.1.call-update) | async-done | bytes 4194320 | tf_op jit(solution)/shard_map/all_gather | solution.py:173
  415.6 13.6 %multiply_reduce_fusion = (f32[1024]{0:T(1024)S(1)}, f32[1024,4096]{1,0:T(8,128)}) fusion(f32[1024]{0:T(1024)S(1)} %log_add_fusion, f32[1024,4096]{1,0:T(8,128)} %copy-done.1, s32[4096]{0:T(1024)S(1)} %eq.62, s32[1024]{0:T(1024)S(1)} %eq.60, bf16[1024,512]{1,0:T(8,128)(2,1)} %convolution_convert_fusion, bf16[4096,512]{1,0:T(8,128)(2,1)} %all-gather.6.cloned.1.call-done), kind=kOutput, calls=%fused_computation.5 | convolution fusion | flops 4320132096 | bytes 38825984 | tf_op jit(solution)/shard_map/dot_general | solution.py:33
  429.1 12.5 %multiply_convert_fusion = bf16[1024,4096]{1,0:T(8,128)(2,1)S(1)} fusion(f32[1024,4096]{1,0:T(8,128)} %get-tuple-element.82, f32[1024]{0:T(1024)S(1)} %get-tuple-element.81, f32[1024]{0:T(1024)S(1)} %log_add_fusion, f32[1024,4096]{1,0:T(8,128)} %copy-done.1, s32[4096]{0:T(1024)S(1)} %eq.62, s32[1024]{0:T(1024)S(1)} %eq.60), kind=kLoop, calls=%fused_computation.4 | loop fusion | flops 29360128 | bytes 41971712 | tf_op jit(solution)/shard_map/convert_element_type | solution.py:205
  498.9 103.6 %reduce-scatter.2.cloned.1.call-done = bf16[1024,1024]{0,1:T(8,128)(2,1)} async-done(((bf16[4096,1024]{0,1:T(8,128)(2,1)}), bf16[1024,1024]{0,1:T(8,128)(2,1)}) %reduce-scatter.2.cloned.1.call-update) | async-done | bytes 2097168 | tf_op jit(solution)/shard_map/reduce_scatter | solution.py:212
  609.1 11.4 all-reduce.9
  624.9 11.4 fusion.172
  650.8 30.9 %copy.31 = bf16[32,32,9,512]{3,2,1,0:T(8,128)(2,1)S(1)} copy(bf16[32,32,9,512]{3,1,0,2:T(8,128)(2,1)S(1)} %fusion.80) | data formatting | bytes 18874368 | tf_op jit(solution)/shard_map/stack | solution.py:88
  681.8 17.5 %copy.37 = bf16[128,8,9,512]{3,1,2,0:T(8,128)(2,1)S(1)} copy(bf16[128,8,9,512]{3,2,1,0:T(8,128)(2,1)S(1)} %bitcast.416) | data formatting | bytes 18874368
  729.6 11.2 pad_maximum_fusion
  765.7 30.9 %copy.33 = bf16[32,32,9,512]{3,2,1,0:T(8,128)(2,1)S(1)} copy(bf16[32,32,9,512]{3,1,0,2:T(8,128)(2,1)S(1)} %fusion.62) | data formatting | bytes 18874368 | tf_op jit(solution)/shard_map/stack | solution.py:88
  796.8 17.5 %copy.38 = bf16[128,8,9,512]{3,1,2,0:T(8,128)(2,1)S(1)} copy(bf16[128,8,9,512]{3,2,1,0:T(8,128)(2,1)S(1)} %bitcast.417) | data formatting | bytes 18874368
  821.9 12.1 %all-reduce.7 = (f32[32]{0:T(128)S(1)}, f32[32]{0:T(128)S(1)}) all-reduce(f32[32]{0:T(128)S(1)} %reduce_sum.346, f32[32]{0:T(128)S(1)} %reduce_sum.343), channel_id=1, replica_groups=mesh['seq'=4,'batch'=8] {'seq'}, use_global_device_ids=true, to_apply=%region_39.40 | all-reduce | flops 64 | bytes 512 | tf_op jit(solution)/shard_map/psum | solution.py:64
  834.4 41.1 %all-reduce.5 = (f32[2,512]{1,0:T(2,128)}, f32[3,512]{1,0:T(4,128)}, f32[3,512]{1,0:T(4,128)}, f32[2,512]{1,0:T(2,128)}, f32[512]{0:T(512)}) all-reduce(f32[2,512]{1,0:T(2,128)S(1)} %pad_maximum_fusion.13, f32[3,512]{1,0:T(4,128)S(1)} %pad_maximum_fusion.11, ...), channel_id=1, replica_groups=mesh['seq'=4,'batch'=8] {'seq','batch'}, use_global_device_ids=true, to_apply=%region_43.44 | all-reduce | flops 5632 | bytes 45056 | tf_op jit(solution)/shard_map/psum | solution.py:268
  879.4 232.4 %all-reduce.12.cloned.1.call-done = (f32[2,3,3,512,512]{4,3,2,1,0:T(8,128)}, f32[2,512,512]{2,1,0:T(8,128)}, f32[512,512]{1,0:T(8,128)}, f32[512,512]{1,0:T(8,128)}) async-done(((f32[2,3,3,512,512]{4,3,2,1,0:T(8,128)}, f32[2,512,512]{2,1,0:T(8,128)}, f32[512,512]{1,0:T(8,128)}, f32[512,512]{1,0:T(8,128)}), (f32[2,3,3,512,512]{4,3,2,1,0:T(8,128)}, f32[2,512,512]{2,1,0:T(8,128)}, f32[512,512]{1,0:T(8,128)}, ...) | async-done | bytes 23068688 | tf_op jit(solution)/shard_map/psum | solution.py:268
  1111.8 15.0 %copy.83 = f32[2,3,3,512,512]{4,3,2,1,0:T(8,128)} copy(f32[2,3,3,512,512]{4,3,2,1,0:T(8,128)} %get-tuple-element.94) | data formatting | bytes 37748736
  (362 shorter events, 274.5 us)
Async XLA Ops:
  7.2 246.6 %copy-start = (bf16[512,512]{1,0:T(8,128)(2,1)S(1)}, bf16[512,512]{1,0:T(8,128)(2,1)}, u32[]{:S(2)}) copy-start(bf16[512,512]{1,0:T(8,128)(2,1)} %param.20) | copy-start | bytes 1572868
  7.2 326.9 %all-gather.4.cloned.1.call-start = ((), (), s32[]{:S(2)}) async-start(), calls=%async_computation.1 | async-start | bytes 5242880 | tf_op jit(solution)/shard_map/all_gather | solution.py:172
  8.1 150.8 %copy-start.63 = (f32[1,512]{1,0:T(1,128)}, f32[1,512]{1,0:T(1,128)S(1)}, u32[]{:S(2)}) copy-start(f32[1,512]{1,0:T(1,128)S(1)} %get-tuple-element.70) | copy-start | bytes 6148
  8.9 150.0 %copy-start.59 = (f32[1,512]{1,0:T(1,128)}, f32[1,512]{1,0:T(1,128)S(1)}, u32[]{:S(2)}) copy-start(f32[1,512]{1,0:T(1,128)S(1)} %get-tuple-element.67) | copy-start | bytes 6148
  36.6 30.1 %collective-permute-start.1 = (bf16[1,32,512]{2,1,0:T(8,128)(2,1)S(1)}, bf16[1,32,512]{2,1,0:T(8,128)(2,1)S(1)}, u32[]{:S(2)}, u32[]{:S(2)}) collective-permute-start(bf16[1,32,512]{2,1,0:T(8,128)(2,1)S(1)} %get-tuple-element.55), channel_id=1, source_target_pairs={{8,0},{16,8},{24,16},{9,1},{17,9},{25,17},{10,2},{18,10},{26,18},{... | collective-permute-start | bytes 98312 | tf_op jit(solution)/shard_map/ppermute | solution.py:21
  38.0 28.7 %collective-permute-start = (bf16[1,32,512]{2,1,0:T(8,128)(2,1)S(1)}, bf16[1,32,512]{2,1,0:T(8,128)(2,1)S(1)}, u32[]{:S(2)}, u32[]{:S(2)}) collective-permute-start(bf16[1,32,512]{2,1,0:T(8,128)(2,1)S(1)} %get-tuple-element.54), channel_id=1, source_target_pairs={{0,8},{8,16},{16,24},{1,9},{9,17},{17,25},{2,10},{10,18},{18,26},{... | collective-permute-start | bytes 98312 | tf_op jit(solution)/shard_map/ppermute | solution.py:20
  57.5 112.0 %copy-start.43 = (bf16[32,32]{1,0:T(8,128)(2,1)}, bf16[32,32]{1,0:T(8,128)(2,1)S(1)}, u32[]{:S(2)}) copy-start(bf16[32,32]{1,0:T(8,128)(2,1)S(1)} %get-tuple-element.64) | copy-start | bytes 6148
  57.5 112.3 %copy-start.41 = (bf16[32,32]{1,0:T(8,128)(2,1)}, bf16[32,32]{1,0:T(8,128)(2,1)S(1)}, u32[]{:S(2)}) copy-start(bf16[32,32]{1,0:T(8,128)(2,1)S(1)} %get-tuple-element.63) | copy-start | bytes 6148
  57.5 112.6 %copy-start.39 = (bf16[32,32]{1,0:T(8,128)(2,1)}, bf16[32,32]{1,0:T(8,128)(2,1)S(1)}, u32[]{:S(2)}) copy-start(bf16[32,32]{1,0:T(8,128)(2,1)S(1)} %get-tuple-element.62) | copy-start | bytes 6148
  57.5 113.2 %copy-start.37 = (bf16[32,32]{1,0:T(8,128)(2,1)}, bf16[32,32]{1,0:T(8,128)(2,1)S(1)}, u32[]{:S(2)}) copy-start(bf16[32,32]{1,0:T(8,128)(2,1)S(1)} %get-tuple-element.61) | copy-start | bytes 6148
  57.5 113.5 %copy-start.35 = (bf16[32,32]{1,0:T(8,128)(2,1)}, bf16[32,32]{1,0:T(8,128)(2,1)S(1)}, u32[]{:S(2)}) copy-start(bf16[32,32]{1,0:T(8,128)(2,1)S(1)} %get-tuple-element.60) | copy-start | bytes 6148
  57.5 113.8 %copy-start.33 = (bf16[32,32]{1,0:T(8,128)(2,1)}, bf16[32,32]{1,0:T(8,128)(2,1)S(1)}, u32[]{:S(2)}) copy-start(bf16[32,32]{1,0:T(8,128)(2,1)S(1)} %get-tuple-element.59) | copy-start | bytes 6148
  57.5 114.4 %copy-start.31 = (bf16[32,32]{1,0:T(8,128)(2,1)}, bf16[32,32]{1,0:T(8,128)(2,1)S(1)}, u32[]{:S(2)}) copy-start(bf16[32,32]{1,0:T(8,128)(2,1)S(1)} %get-tuple-element.58) | copy-start | bytes 6148
  57.5 114.7 %copy-start.29 = (bf16[32,32]{1,0:T(8,128)(2,1)}, bf16[32,32]{1,0:T(8,128)(2,1)S(1)}, u32[]{:S(2)}) copy-start(bf16[32,32]{1,0:T(8,128)(2,1)S(1)} %get-tuple-element.57) | copy-start | bytes 6148
  57.6 115.0 %copy-start.27 = (bf16[32,32]{1,0:T(8,128)(2,1)}, bf16[32,32]{1,0:T(8,128)(2,1)S(1)}, u32[]{:S(2)}) copy-start(bf16[32,32]{1,0:T(8,128)(2,1)S(1)} %get-tuple-element.56) | copy-start | bytes 6148
  161.3 5.9 collective-permute-start.3
  162.6 6.1 collective-permute-start.2
  253.7 161.8 %all-gather.6.cloned.1.call-start = ((), (), s32[]{:S(2)}) async-start(), calls=%async_computation.2 | async-start | bytes 5242880 | tf_op jit(solution)/shard_map/all_gather | solution.py:173
  256.8 345.7 %reduce-scatter.2.cloned.1.call-start = ((), (), s32[]{:S(2)}) async-start(), calls=%async_computation.3 | async-start | bytes 10485760 | tf_op jit(solution)/shard_map/reduce_scatter | solution.py:212
  459.4 652.4 %all-reduce.12.cloned.1.call-start = ((), (), s32[]{:S(2)}) async-start(), calls=%async_computation.4 | async-start | bytes 46137344 | tf_op jit(solution)/shard_map/psum | solution.py:268
  636.3 9.9 collective-permute-start.5
  637.6 8.6 collective-permute-start.4
  753.3 6.7 collective-permute-start.7
  754.6 6.8 collective-permute-start.6
  (67 other events, 910.5 us)
Sparse Core Ops, SparseCore 0:
  253.9 80.1 all-gather.3
  336.2 79.2 all-gather.5
  459.5 142.9 reduce-scatter.1
  741.0 370.7 all-reduce.11
where the time goes:
time: 1140 us
  waiting for transfers between devices  470 us (41%)
  local copies, waits for them, and re-layouts  258 us (23%)
  blocking collectives  158 us (14%)
  matrix products  129 us (11%)
  other arithmetic  82.5 us (7%)
  starting transfers between devices  24 us (2%)
  between operations  15.5 us (1%)
    psum x1, waiting for transfers between devices, body(): lax.psum((conv_rows, bias_pair, gain_rows, shift_rows, qk_rows, value_gra...  232 us
    another operation x4, local copies, waits for them, and re-layouts, gather_taps(): return jnp.stack(columns, 2).reshape(band_rows * canvas_width, -1)  124 us
    reduce_scatter x1, waiting for transfers between devices, body(): lax.psum_scatter(jnp.concatenate([key_part, value_part], axis=1).astype(j...  104 us
    unnamed x166, local copies, waits for them, and re-layouts  98.5 us
    all_gather x1, waiting for transfers between devices, body(): key_piece = lax.all_gather(key_rows, 'seq', axis=0, tiled=True)  70.9 us
    all_gather x1, waiting for transfers between devices, body(): value_piece = lax.all_gather(value_rows, 'seq', axis=0, tiled=True)  59.7 us
    psum x3, blocking collectives, group_stats(): group_mean = lax.psum(jnp.sum(grouped, axis=(0, 2)), 'seq') / group_count  46.4 us
    psum x1, blocking collectives, body(): lax.psum((conv_rows, bias_pair, gain_rows, shift_rows, qk_rows, value_gra...  41.1 us
  transfers between devices with their start and end apart: 12, of which 7 were waited for; matrix products, arithmetic and copies ran while one was open for 14% of the time, Pallas kernels for 0%

commit v1 on v0

v1 whole, which is shorter than its diff:
```python
import functools

import jax
import jax.numpy as jnp
from jax import lax
from jax.experimental import pallas as pl
from jax.experimental.pallas import tpu as pltpu
from jax.sharding import PartitionSpec as P

GROUPS = 32
EPSILON = 1e-06
MASKED_SCORE = -1e30
F32 = jnp.float32
BF16 = jnp.bfloat16
MIB = 1024 * 1024
PIECES = 32


def params(mib):
    return pltpu.CompilerParams(vmem_limit_bytes=mib * MIB)


def shape(dims, dtype):
    return jax.ShapeDtypeStruct(dims, dtype)


SMEM = pl.BlockSpec(memory_space=pltpu.SMEM)


def whole(*dims):
    return pl.BlockSpec(dims, lambda *_: (0,) * len(dims))


def group_sum(row):
    channels = row.shape[1]
    lane = lax.broadcasted_iota(jnp.int32, row.shape, 1)
    step = 1
    while step < channels // GROUPS:
        ahead = pltpu.roll(row, channels - step, 1)
        behind = pltpu.roll(row, step, 1)
        row = row + jnp.where((lane & step) == 0, ahead, behind)
        step *= 2
    return row


def rows_of(*parts):
    channels = parts[0].shape[1]
    line = lax.broadcasted_iota(jnp.int32, (8, channels), 0)
    out = jnp.zeros((8, channels), F32)
    for i, part in enumerate(parts):
        out = jnp.where(line == i, jnp.broadcast_to(part, (8, channels)), out)
    return out


def eight(row):
    return jnp.broadcast_to(row, (8, row.shape[1]))


def local_stats(values, channels, pixels):
    count = float(pixels * (channels // GROUPS))
    mean = group_sum(eight(jnp.sum(values, axis=0, keepdims=True)))[0:1] / count
    centered = values - mean
    square = group_sum(eight(jnp.sum(centered * centered, axis=0, keepdims=True)))[0:1]
    return mean, square


def joined_stats(own, near, cross, pair, pixels):
    bands = [own[0:2], near[32:34], cross[32:34], pair[0:2]]
    channels = bands[0].shape[1]
    count = float(pixels * (channels // GROUPS))
    mean = (bands[0][0:1] + bands[1][0:1] + bands[2][0:1] + bands[3][0:1]) * 0.25
    total = 0.0
    for band in bands:
        gap = band[0:1] - mean
        total = total + band[1:2] + count * gap * gap
    return mean, lax.rsqrt(total / (4.0 * count) + EPSILON)


def joined_sums(own, near, cross, pair, pixels):
    bands = [own[0:2], near[32:34], cross[32:34], pair[0:2]]
    channels = bands[0].shape[1]
    count = 4.0 * float(pixels * (channels // GROUPS))
    sums = (bands[0] + bands[1]) + (bands[2] + bands[3])
    return sums[0:1] / count, sums[1:2] / count


def sigmoid(values):
    return 0.5 * jnp.tanh(0.5 * values) + 0.5


def edges_out(side_ref, out_ref, near_ref, cross_ref, stats):
    pixels = out_ref.shape[0]
    side = side_ref[0]
    last = pixels - 32
    near_ref[0:32, :] = out_ref[pl.ds(pl.multiple_of(last * (1 - side), 32), 32), :].astype(F32)
    cross_ref[0:32, :] = out_ref[pl.ds(pl.multiple_of(last * side, 32), 32), :].astype(F32)
    near_ref[32:40, :] = stats
    cross_ref[32:40, :] = stats


def columns_of(frame, shifted, rows):
    for b in range(3):
        shifted[b] = frame[7 + b : 7 + b + rows, :].astype(BF16)


def masked(values, mask):
    channels = values.shape[1]
    return [values[:, i * 128 : (i + 1) * 128] * mask for i in range(channels // 128)]


def tap_rows(shifted, mask_ref, start, count, row):
    parts = []
    for b in range(3):
        block = shifted[b, pl.ds(pl.multiple_of(row * 32 + start, 32), count), :]
        parts += masked(block, mask_ref[b, start : start + count, :])
    return parts


def first_kernel(image_ref, tiles_ref, side_ref, near_ref, cross_ref, stats_ref):
    pixels, channels = image_ref.shape
    mean, square = local_stats(image_ref[...].astype(F32), channels, pixels)
    stats = rows_of(mean, square, tiles_ref[0:1], tiles_ref[1:2])
    stats_ref[...] = stats
    edges_out(side_ref, image_ref, near_ref, cross_ref, stats)


def mask_kernel(where_ref, own_ref, near_ref, cross_ref, pair_ref, mask_ref, column_ref, row_ref, frame):
    side, first, last = where_ref[0], where_ref[1], where_ref[2]

    def line(ref, base):
        return jnp.concatenate([ref[base + 2 : base + 3, :], ref[base + 3 : base + 4, :]], axis=1)

    own, near, cross, pair = line(own_ref, 0), line(near_ref, 32), line(cross_ref, 32), line(pair_ref, 0)
    pixels = own.shape[1]
    row_ref[...] = jnp.concatenate([own, pair, near, cross], axis=1)

    def upright(row):
        return jnp.transpose(jnp.broadcast_to(row, (128, row.shape[1])))

    column = upright(own)
    column_ref[...] = column
    above = jnp.where(side == 0, cross[:, pixels - 128 :], near[:, pixels - 128 :])
    below = jnp.where(side == 0, near[:, :128], cross[:, :128])
    outside = jnp.full((32, 128), -1.0, F32)
    frame[0:8, :] = jnp.zeros((8, 128), F32)
    frame[8:40, :] = jnp.where(first == 1, outside, upright(above)[96:128, :])
    frame[40 : 40 + pixels, :] = column
    frame[40 + pixels : 72 + pixels, :] = jnp.where(last == 1, outside, upright(below)[0:32, :])
    frame[72 + pixels : 80 + pixels, :] = jnp.zeros((8, 128), F32)
    place = lax.broadcasted_iota(jnp.int32, (pixels, 128), 0) & 31
    for a in range(3):
        for b in range(3):
            start = 8 + a * 32 + b - 1
            same = frame[start : start + pixels, :] == column
            if b == 0:
                same = same & (place > 0)
            if b == 2:
                same = same & (place < 31)
            mask_ref[a * 3 + b] = jnp.where(same, 1.0, 0.0).astype(BF16)


def conv_kernel(
    side_ref, x_ref, near_ref, cross_ref, pair_ref, stats_ref, rows_ref, mask_ref, weight_ref, skip_ref,
    out_ref, act_ref, near_out, cross_out, stats_out, frame, shifted,
):
    row = pl.program_id(0)
    pixels, channels = x_ref.shape

    @pl.when(row == 0)
    def _():
        mean, inverse = joined_stats(stats_ref[...], near_ref[...], cross_ref[...], pair_ref[...], pixels)
        scale, shift, bias = rows_ref[0:1, :], rows_ref[1:2, :], rows_ref[2:3, :]

        def act(values):
            pre = (values - mean) * inverse * scale + shift
            return pre * sigmoid(pre)

        side = side_ref[0]
        near, cross = near_ref[0:32, :], cross_ref[0:32, :]
        frame[0:8, :] = jnp.zeros((8, channels), F32)
        frame[8:40, :] = act(jnp.where(side == 0, cross, near))
        frame[40 : 40 + pixels, :] = act(x_ref[...].astype(F32))
        frame[40 + pixels : 72 + pixels, :] = act(jnp.where(side == 0, near, cross))
        frame[72 + pixels : 80 + pixels, :] = jnp.zeros((8, channels), F32)
        columns_of(frame, shifted, pixels + 64)
        act_ref[...] = shifted[1, 32 : 32 + pixels, :]
        start = jnp.broadcast_to(bias, (pixels, channels))
        if skip_ref is not None:
            start = start + skip_ref[...].astype(F32)
        out_ref[...] = start

    weight = weight_ref[...].reshape(3 * channels, channels)
    for i in range(pixels // 256):
        taps = jnp.concatenate(tap_rows(shifted, mask_ref, i * 256, 256, row), axis=1)
        out_ref[i * 256 : (i + 1) * 256, :] += jnp.dot(taps, weight, preferred_element_type=F32)

    @pl.when(row == 2)
    def _():
        mean, square = local_stats(out_ref[...], channels, pixels)
        stats = rows_of(mean, square)
        stats_out[...] = stats
        edges_out(side_ref, out_ref, near_out, cross_out, stats)


def normed_kernel(x_ref, near_ref, cross_ref, pair_ref, stats_ref, rows_ref, out_ref):
    pixels = x_ref.shape[0]
    mean, inverse = joined_stats(stats_ref[...], near_ref[...], cross_ref[...], pair_ref[...], pixels)
    out_ref[...] = ((x_ref[...] - mean) * inverse * rows_ref[0:1, :] + rows_ref[1:2, :]).astype(BF16)


def nn(left, right):
    return jnp.dot(left, right, preferred_element_type=F32)


def nt(left, right):
    return lax.dot_general(left, right, (((1,), (1,)), ((), ())), preferred_element_type=F32)


def project_kernel(transposed, *refs):
    blocks, (matrix_ref, bias_ref, out_ref) = refs[:4], refs[4:]
    pixels = blocks[0].shape[0]
    product = nt if transposed else nn
    for i, block in enumerate(blocks):
        values = product(block[...], matrix_ref[...])
        out_ref[i * pixels : (i + 1) * pixels, :] = (values + bias_ref[0:1, :]).astype(BF16)


def attend_kernel(
    own_ref, pair_ref, near_ref, cross_ref, grad_ref, qk_ref, value_ref, bias_ref, column_ref, row_ref,
    attended_ref, query_grad_ref, totals_ref, keys, values,
):
    pixels, channels = own_ref.shape
    scale = channels ** (-0.5)
    for i, block in enumerate((own_ref, pair_ref, near_ref, cross_ref)):
        rows = block[...]
        keys[i * pixels : (i + 1) * pixels, :] = nn(rows, qk_ref[1]).astype(BF16)
        values[i * pixels : (i + 1) * pixels, :] = (nn(rows, value_ref[...]) + bias_ref[1:2, :]).astype(BF16)

    def step(i, carry):
        part = pl.ds(pl.multiple_of(i * 256, 256), 256)
        queries = (nn(own_ref[part, :], qk_ref[0]) + bias_ref[0:1, :]).astype(BF16)
        scores = nt(queries, keys[...]) * scale
        scores = jnp.where(column_ref[part, 0:1] == row_ref[...], scores, MASKED_SCORE)
        top = jnp.max(scores, axis=1, keepdims=True)
        weights = jnp.exp(scores - top)
        total = jnp.sum(weights, axis=1, keepdims=True)
        attended = nn(weights.astype(BF16), values[...]) / total
        attended_ref[part, :] = attended.astype(BF16)
        upstream = grad_ref[part, :]
        delta = jnp.sum(attended * upstream.astype(F32), axis=1, keepdims=True)
        prob_grad = nt(upstream, values[...])
        score_grad = (weights * (1.0 / total) * (prob_grad - delta)).astype(BF16)
        query_grad_ref[part, :] = (nn(score_grad, keys[...]) * scale).astype(BF16)
        log_total = jnp.transpose(jnp.broadcast_to(top + jnp.log(total), (256, 128)))
        turned = jnp.transpose(jnp.broadcast_to(delta, (256, 128)))
        totals_ref[i, 0:1, :] = log_total[0:1, :]
        totals_ref[i, 1:2, :] = turned[0:1, :]
        totals_ref[i, 2:8, :] = jnp.zeros((6, 256), F32)
        return carry

    lax.fori_loop(0, pixels // 256, step, 0)


def out_kernel(attended_ref, residual_ref, matrix_ref, bias_ref, out_ref):
    out_ref[...] = (residual_ref[...] + nn(attended_ref[...], matrix_ref[...]) + bias_ref[0:1, :]).astype(BF16)


def norm_back_sums(upstream, hat, gain):
    outer = jnp.sum(upstream * hat, axis=0, keepdims=True)
    inner = jnp.sum(upstream, axis=0, keepdims=True)
    first = group_sum(eight(inner * gain))[0:1]
    second = group_sum(eight(outer * gain))[0:1]
    return rows_of(outer, inner), rows_of(first, second)


def key_kernel(
    side_ref, own_ref, queries_ref, grads_ref, query_grad_ref, qk_ref, value_ref, bias_ref,
    totals_own, totals_pair, totals_near, totals_cross, column_ref, row_ref,
    residual_ref, stats_ref, near_ref, cross_ref, pair_ref, rows_ref,
    key_grad_ref, value_grad_ref, normed_grad_ref, near_out, cross_out, stats_out, sums_out,
    keys, values, key_sum, value_sum,
):
    pixels, channels = own_ref.shape
    scale = channels ** (-0.5)
    keys[...] = nn(own_ref[...], qk_ref[1]).astype(BF16)
    values[...] = (nn(own_ref[...], value_ref[...]) + bias_ref[1:2, :]).astype(BF16)
    key_sum[...] = jnp.zeros_like(key_sum)
    value_sum[...] = jnp.zeros_like(value_sum)
    blocks = pixels // 256
    for group, totals in enumerate((totals_own, totals_pair, totals_near, totals_cross)):

        def step(i, carry, group=group, totals=totals):
            part = pl.ds(pl.multiple_of(group * pixels + i * 256, 256), 256)
            queries, upstream = queries_ref[part, :], grads_ref[part, :]
            scores = nt(keys[...], queries) * scale
            weights = jnp.exp(scores - totals[i, 0:1, :])
            weights = jnp.where(column_ref[:, 0:1] == row_ref[group * blocks + i, 0:1, :], weights, 0.0)
            value_sum[...] += nn(weights.astype(BF16), upstream)
            prob_grad = nt(values[...], upstream)
            score_grad = (weights * (prob_grad - totals[i, 1:2, :])).astype(BF16)
            key_sum[...] += nn(score_grad, queries)
            return carry

        lax.fori_loop(0, blocks, step, 0)
    key_grad = (key_sum[...] * scale).astype(BF16)
    value_grad = value_sum[...].astype(BF16)
    key_grad_ref[...] = key_grad
    value_grad_ref[...] = value_grad
    normed_grad = nt(query_grad_ref[...], qk_ref[0]) + nt(key_grad, qk_ref[1]) + nt(value_grad, value_ref[...])
    normed_grad_ref[...] = normed_grad
    mean, inverse = joined_stats(stats_ref[...], near_ref[...], cross_ref[...], pair_ref[...], pixels)
    hat = (residual_ref[...] - mean) * inverse
    sums, groups = norm_back_sums(normed_grad, hat, rows_ref[0:1, :])
    sums_out[...] = sums
    stats_out[...] = groups
    edges_out(side_ref, normed_grad_ref, near_out, cross_out, groups)


def scatter_pieces(place_ref, product, tap, first_ref, second_ref):
    rows, channels = product.shape
    half, height = channels // 2, rows // PIECES
    for j in range(PIECES):
        piece = product[j * height : (j + 1) * height, :].astype(BF16)
        first_ref[j ^ place_ref[0], tap] = piece[:, :half]
        second_ref[j ^ place_ref[1], tap] = piece[:, half:]


def tn(left, right):
    return lax.dot_general(left, right, (((0,), (0,)), ((), ())), preferred_element_type=F32)


def matrix_kernel(
    place_ref, normed_ref, query_grad_ref, key_grad_ref, value_grad_ref, attended_ref, cotangent_ref,
    first_ref, second_ref, sums_ref, turned,
):
    turned[...] = jnp.transpose(normed_ref[...])
    for tap, ref in enumerate((query_grad_ref, key_grad_ref, value_grad_ref)):
        scatter_pieces(place_ref, nn(turned[...], ref[...]), tap, first_ref, second_ref)
    turned[...] = jnp.transpose(attended_ref[...])
    scatter_pieces(place_ref, nn(turned[...], cotangent_ref[...]), 3, first_ref, second_ref)
    total = [
        jnp.sum(ref[...].astype(F32), axis=0, keepdims=True)
        for ref in (query_grad_ref, value_grad_ref, cotangent_ref)
    ]
    sums_ref[...] = rows_of(*total)


def weight_grad_kernel(
    with_cotangent, place_ref, side_ref, x_ref, x_near, x_cross, stats_ref, near_ref, cross_ref, pair_ref,
    g_ref, g_near, g_cross, g_pair, g_stats, rows_ref, act_ref, mask_ref, *rest,
):
    if with_cotangent:
        cot_ref, first_ref, second_ref, shifted, sums_ref, own_ref, frame, turned = rest
    else:
        first_ref, second_ref, shifted, sums_ref, frame, turned = rest
    row = pl.program_id(0)
    pixels, channels = x_ref.shape

    @pl.when(row == 0)
    def _():
        mean, inverse = joined_stats(stats_ref[...], near_ref[...], cross_ref[...], pair_ref[...], pixels)
        mean_h, mean_hx = joined_sums(g_stats[...], g_near[...], g_cross[...], g_pair[...], pixels)
        gain = rows_ref[0:1, :]
        side = side_ref[0]

        def back(grad, values):
            hat = (values - mean) * inverse
            return inverse * (grad * gain - mean_h - hat * mean_hx)

        def pick(near, cross):
            return jnp.where(side == 0, cross, near), jnp.where(side == 0, near, cross)

        g_above, g_below = pick(g_near[0:32, :], g_cross[0:32, :])
        x_above, x_below = pick(x_near[0:32, :], x_cross[0:32, :])
        above, below = back(g_above, x_above), back(g_below, x_below)
        own = back(g_ref[...], x_ref[...])
        if with_cotangent:
            c_above, c_below = pick(x_near[32:64, :], x_cross[32:64, :])
            above, below = above + c_above, below + c_below
            own = own + cot_ref[...].astype(F32)
            own_ref[...] = own
        sums_ref[...] = rows_of(jnp.sum(own, axis=0, keepdims=True))
        frame[0:8, :] = jnp.zeros((8, channels), F32)
        frame[8:40, :] = above
        frame[40 : 40 + pixels, :] = own
        frame[40 + pixels : 72 + pixels, :] = below
        frame[72 + pixels : 80 + pixels, :] = jnp.zeros((8, channels), F32)
        columns_of(frame, shifted, pixels + 64)
        turned[...] = jnp.transpose(act_ref[...])

    for b in range(3):
        block = shifted[b, pl.ds(pl.multiple_of(row * 32, 32), pixels), :]
        block = jnp.concatenate(masked(block, mask_ref[b]), axis=1)
        product = nn(turned[...], block)
        scatter_pieces(place_ref, product, 8 - row * 3 - b, first_ref, second_ref)


def conv_back_kernel(
    side_ref, shifted, mask_ref, weight_ref, x_ref, stats_ref, near_ref, cross_ref, pair_ref, rows_ref,
    out_ref, near_out, cross_out, stats_out, sums_out,
):
    row = pl.program_id(0)
    pixels, channels = x_ref.shape

    @pl.when(row == 0)
    def _():
        out_ref[...] = jnp.zeros_like(out_ref)

    weight = jnp.concatenate([weight_ref[2 - b] for b in range(3)], axis=1)
    for i in range(pixels // 256):
        taps = jnp.concatenate(tap_rows(shifted, mask_ref, i * 256, 256, row), axis=1)
        out_ref[i * 256 : (i + 1) * 256, :] += nt(taps, weight)

    @pl.when(row == 2)
    def _():
        mean, inverse = joined_stats(stats_ref[...], near_ref[...], cross_ref[...], pair_ref[...], pixels)
        gain, shift = rows_ref[0:1, :], rows_ref[1:2, :]
        hat = (x_ref[...].astype(F32) - mean) * inverse
        pre = hat * gain + shift
        gate = sigmoid(pre)
        upstream = out_ref[...] * (gate * (1.0 + pre * (1.0 - gate)))
        out_ref[...] = upstream
        sums, groups = norm_back_sums(upstream, hat, gain)
        sums_out[...] = sums
        stats_out[...] = groups
        edges_out(side_ref, out_ref, near_out, cross_out, groups)


def last_kernel(
    g_ref, g_near, g_cross, g_pair, g_stats, x_ref, stats_ref, near_ref, cross_ref, pair_ref, rows_ref, add_ref, out_ref
):
    pixels = x_ref.shape[0]
    mean, inverse = joined_stats(stats_ref[...], near_ref[...], cross_ref[...], pair_ref[...], pixels)
    mean_h, mean_hx = joined_sums(g_stats[...], g_near[...], g_cross[...], g_pair[...], pixels)
    hat = (x_ref[...].astype(F32) - mean) * inverse
    grad = inverse * (g_ref[...] * rows_ref[0:1, :] - mean_h - hat * mean_hx)
    out_ref[...] = (add_ref[...] + grad).astype(BF16)


def unpack_kernel(place_ref, first_ref, second_ref, *rest):
    out_ref = rest[-1]
    height, half = first_ref.shape[2], first_ref.shape[3]
    for j in range(PIECES):
        lines = slice(j * height, (j + 1) * height)
        out_ref[0, lines, :half] = first_ref[j ^ place_ref[0], 0].astype(F32)
        out_ref[0, lines, half:] = second_ref[j ^ place_ref[1], 0].astype(F32)


def body(
    image,
    tile_map,
    out_grad,
    conv_weight,
    conv_bias,
    norm_gain,
    norm_shift,
    qk_weight,
    value_weight,
    proj_weight,
    qv_bias,
    proj_bias,
):
    band, width, channels = image.shape[1], image.shape[2], image.shape[3]
    pixels = band * width
    lanes = lax.axis_size("batch")
    devices = 4 * lanes

    def turned(flat):
        s, b = flat // lanes, flat % lanes
        core, high = b % 2, s // 2
        return (core * 2 + s % 2) * lanes + (b - core + high)

    def xored(flat, bits):
        return flat ^ bits

    def permute(x, to):
        return lax.ppermute(x, ("seq", "batch"), [(i, to(i)) for i in range(devices)])

    near_bit, pair_bit = lanes, 1

    def to_near(i):
        return i ^ near_bit

    def to_pair(i):
        return i ^ pair_bit

    def to_cross(i):
        return i ^ (near_bit | pair_bit)

    def meet(near, cross, stats):
        return permute(near, to_near), permute(cross, to_cross), permute(stats, to_pair)

    seq, lane = lax.axis_index("seq"), lax.axis_index("batch")
    core, low, high = lane % 2, seq % 2, seq // 2
    side = low.astype(jnp.int32).reshape(1)
    spot = jnp.stack([low, ((low == 0) & (core == 0)), ((low == 1) & (core == 1))]).astype(jnp.int32)
    x_bit, y_bit = (lane // 2) % 2, (lane // 4) % 2
    tail = low * 2 + high
    place = jnp.stack(
        [core * 16 + x_bit * 8 + y_bit * 4 + tail, core * 16 + y_bit * 8 + x_bit * 4 + tail]
    ).astype(jnp.int32)

    def block8(*rows):
        rows = [r.astype(F32).reshape(1, channels) for r in rows]
        return jnp.concatenate(rows + [jnp.zeros((8 - len(rows), channels), F32)], axis=0)

    norm_rows = [block8(norm_gain[i], norm_shift[i], conv_bias[min(i, 1)]) for i in range(3)]
    bias_rows = block8(qv_bias[0], qv_bias[1], proj_bias, jnp.zeros((channels,), F32))

    row_f32 = shape((40, channels), F32)
    stat_f32 = shape((8, channels), F32)
    field_f32 = shape((pixels, channels), F32)
    field_b16 = shape((pixels, channels), BF16)
    field = whole(pixels, channels)
    edge = whole(40, channels)
    stat = whole(8, channels)

    image_flat = image.reshape(pixels, channels)
    cot_flat = out_grad.reshape(pixels, channels)
    tiles = tile_map.astype(F32).reshape(2, pixels // 2)
    x = permute(image_flat, turned)
    near0, cross0, stats0 = pl.pallas_call(
        first_kernel,
        in_specs=[field, whole(2, pixels // 2), SMEM],
        out_specs=[edge, edge, stat],
        out_shape=[row_f32, row_f32, stat_f32],
        grid=(1,),
        compiler_params=params(16),
        name="first",
    )(image_flat, tiles, side)
    own0 = permute(stats0, turned)
    pair0 = permute(stats0, lambda i: to_pair(turned(i)))
    near0 = permute(near0, lambda i: to_near(turned(i)))
    cross0 = permute(cross0, lambda i: to_cross(turned(i)))
    masks, column_tiles, row_tiles = pl.pallas_call(
        mask_kernel,
        in_specs=[SMEM, stat, edge, edge, stat],
        out_specs=[whole(9, pixels, 128), whole(pixels, 128), whole(1, 4 * pixels)],
        out_shape=[shape((9, pixels, 128), BF16), shape((pixels, 128), F32), shape((1, 4 * pixels), F32)],
        scratch_shapes=[pltpu.VMEM((pixels + 80, 128), F32)],
        grid=(1,),
        compiler_params=params(24),
        name="masks",
    )(spot, own0, near0, cross0, pair0)

    cotangent = permute(cot_flat, turned)

    mask_block = pl.BlockSpec((3, pixels, 128), lambda i: (i, 0, 0))

    def conv(x, met, stats, rows, index, skip, name):
        near, cross, pair = met
        specs = [
            SMEM, field, edge, edge, stat, stat, stat, mask_block,
            pl.BlockSpec((None, 1, 3, channels, channels), lambda i: (index, i, 0, 0, 0)),
        ]
        operands = [side, x, near, cross, pair, stats, rows, masks, conv_weight]
        kernel = conv_kernel
        if skip is None:

            def kernel(*refs):
                return conv_kernel(*refs[:9], None, *refs[9:])
        else:
            specs.append(field)
            operands.append(skip)
        return pl.pallas_call(
            kernel,
            in_specs=specs,
            out_specs=[field, field, edge, edge, stat],
            out_shape=[field_f32, field_b16, row_f32, row_f32, stat_f32],
            scratch_shapes=[pltpu.VMEM((pixels + 80, channels), F32), pltpu.VMEM((3, pixels + 64, channels), BF16)],
            grid=(3,),
            compiler_params=params(40),
            name=name,
        )(*operands)

    met0 = (near0, cross0, pair0)
    middle, act_one, near1, cross1, stats1 = conv(x, met0, own0, norm_rows[0], 0, None, "conv_one")
    met1 = meet(near1, cross1, stats1)
    residual, act_two, near2, cross2, stats2 = conv(middle, met1, stats1, norm_rows[1], 1, x, "conv_two")
    met2 = meet(near2, cross2, stats2)

    normed = pl.pallas_call(
        normed_kernel,
        in_specs=[field, edge, edge, stat, stat, stat],
        out_specs=field,
        out_shape=field_b16,
        grid=(1,),
        compiler_params=params(16),
        name="normed",
    )(residual, *met2, stats2, norm_rows[2])

    normed_near = permute(normed, to_near)
    normed_pair = permute(normed, to_pair)
    normed_cross = permute(normed_near, to_pair)
    cot_near = permute(cotangent, to_near)
    cot_pair = permute(cotangent, to_pair)
    cot_cross = permute(cot_near, to_pair)

    def project(blocks, matrix, bias, transposed, name):
        return pl.pallas_call(
            functools.partial(project_kernel, transposed),
            in_specs=[field] * 4 + [whole(channels, channels), stat],
            out_specs=whole(4 * pixels, channels),
            out_shape=shape((4 * pixels, channels), BF16),
            grid=(1,),
            compiler_params=params(32),
            name=name,
        )(*blocks, matrix, bias)

    zero_rows = jnp.zeros((8, channels), F32)
    all_grads = project((cotangent, cot_pair, cot_near, cot_cross), proj_weight, zero_rows, True, "grad_att")

    totals_shape = shape((pixels // 256, 8, 256), F32)
    totals_spec = whole(pixels // 256, 8, 256)
    attended, query_grad, totals = pl.pallas_call(
        attend_kernel,
        in_specs=[field] * 5
        + [whole(2, channels, channels), whole(channels, channels), stat, whole(pixels, 128), whole(1, 4 * pixels)],
        out_specs=[field, field, totals_spec],
        out_shape=[field_b16, field_b16, totals_shape],
        scratch_shapes=[pltpu.VMEM((4 * pixels, channels), BF16)] * 2,
        grid=(1,),
        compiler_params=params(56),
        name="attend",
    )(normed, normed_pair, normed_near, normed_cross, all_grads, qk_weight, value_weight, bias_rows, column_tiles, row_tiles)

    totals_pair, totals_near, totals_cross = (permute(totals, to) for to in (to_pair, to_near, to_cross))
    cot32 = cotangent.astype(F32)
    cot_top, cot_bottom = cot32[:32], cot32[pixels - 32 :]
    near_edge = jnp.where(low == 0, cot_bottom, cot_top)
    cross_edge = jnp.where(low == 0, cot_top, cot_bottom)
    edge_near = permute(near_edge, to_near)
    edge_cross = permute(cross_edge, to_cross)
    wide_near = jnp.concatenate([met2[0][:32], edge_near], axis=0)
    wide_cross = jnp.concatenate([met2[1][:32], edge_cross], axis=0)

    all_queries = project((normed, normed_pair, normed_near, normed_cross), qk_weight[0], bias_rows, False, "queries")
    output = pl.pallas_call(
        out_kernel,
        in_specs=[field, field, whole(channels, channels), stat],
        out_specs=field,
        out_shape=field_b16,
        grid=(1,),
        compiler_params=params(16),
        name="output",
    )(attended, residual, proj_weight, block8(proj_bias))
    output = permute(output, turned)

    blocks = pixels // 256
    key_grad, value_grad, normed_grad, near3, cross3, stats3, sums3 = pl.pallas_call(
        key_kernel,
        in_specs=[SMEM, field, whole(4 * pixels, channels), whole(4 * pixels, channels), field]
        + [whole(2, channels, channels), whole(channels, channels), stat]
        + [totals_spec] * 4
        + [whole(pixels, 128), whole(4 * blocks, 1, 256), field, stat, edge, edge, stat, stat],
        out_specs=[field, field, field, edge, edge, stat, stat],
        out_shape=[field_b16, field_b16, field_f32, row_f32, row_f32, stat_f32, stat_f32],
        scratch_shapes=[pltpu.VMEM((pixels, channels), BF16)] * 2 + [pltpu.VMEM((pixels, channels), F32)] * 2,
        grid=(1,),
        compiler_params=params(56),
        name="key_value_grad",
    )(
        side, normed, all_queries, all_grads, query_grad, qk_weight, value_weight, bias_rows,
        totals, totals_pair, totals_near, totals_cross, column_tiles, row_tiles.reshape(4 * blocks, 1, 256),
        residual, stats2, *met2, norm_rows[2],
    )
    met3 = meet(near3, cross3, stats3)

    def piece_shapes(taps):
        dims = (PIECES, taps, channels // PIECES, channels // 2)
        return [whole(*dims)] * 2, [shape(dims, BF16)] * 2

    specs, shapes = piece_shapes(4)
    matrix_first, matrix_second, matrix_sums = pl.pallas_call(
        matrix_kernel,
        in_specs=[SMEM] + [field] * 6,
        out_specs=specs + [stat],
        out_shape=shapes + [stat_f32],
        scratch_shapes=[pltpu.VMEM((channels, pixels), BF16)],
        grid=(1,),
        compiler_params=params(32),
        name="matrix_grad",
    )(place, normed, query_grad, key_grad, value_grad, attended, cotangent)

    def weight_grad(x, x_near, x_cross, stats, met, grad, grad_met, grad_stats, rows, act, cot, name):
        specs, shapes = piece_shapes(9)
        wide = whole(x_near.shape[0], channels)
        extra_in, extra_out = ([field], [field]) if cot is not None else ([], [])
        near, cross, pair = met
        g_near, g_cross, g_pair = grad_met
        spread = (3, pixels + 64, channels)
        return pl.pallas_call(
            functools.partial(weight_grad_kernel, cot is not None),
            in_specs=[SMEM, SMEM, field, wide, wide, stat, edge, edge, stat, field, edge, edge, stat, stat, stat, field, mask_block]
            + extra_in,
            out_specs=specs + [whole(*spread), stat] + extra_out,
            out_shape=shapes + [shape(spread, BF16), stat_f32] + ([field_f32] if extra_out else []),
            scratch_shapes=[pltpu.VMEM((pixels + 80, channels), F32), pltpu.VMEM((channels, pixels), BF16)],
            grid=(3,),
            compiler_params=params(56),
            name=name,
        )(
            place, side, x, x_near, x_cross, stats, near, cross, pair, grad, g_near, g_cross, g_pair, grad_stats,
            rows, act, masks, *([cot] if cot is not None else []),
        )

    def conv_back(shifted, index, x, stats, met, rows, name):
        return pl.pallas_call(
            conv_back_kernel,
            in_specs=[
                SMEM, whole(3, pixels + 64, channels), mask_block,
                pl.BlockSpec((None, None, 3, channels, channels), lambda i: (index, 2 - i, 0, 0, 0)),
                field, stat, edge, edge, stat, stat,
            ],
            out_specs=[field, edge, edge, stat, stat],
            out_shape=[field_f32, row_f32, row_f32, stat_f32, stat_f32],
            grid=(3,),
            compiler_params=params(40),
            name=name,
        )(side, shifted, masks, conv_weight, x, stats, *met, rows)

    two_first, two_second, shifted_two, bias_two, residual_grad = weight_grad(
        residual, wide_near, wide_cross, stats2, met2, normed_grad, met3, stats3, norm_rows[2], act_two, cotangent,
        "weight_two_grad",
    )
    grad_two, near4, cross4, stats4, sums4 = conv_back(shifted_two, 1, middle, stats1, met1, norm_rows[1], "conv_two_back")
    met4 = meet(near4, cross4, stats4)
    one_first, one_second, shifted_one, bias_one = weight_grad(
        middle, met1[0], met1[1], stats1, met1, grad_two, met4, stats4, norm_rows[1], act_one, None, "weight_one_grad"
    )
    grad_one, near5, cross5, stats5, sums5 = conv_back(shifted_one, 0, x, own0, met0, norm_rows[0], "conv_one_back")
    met5 = meet(near5, cross5, stats5)
    image_grad = pl.pallas_call(
        last_kernel,
        in_specs=[field, edge, edge, stat, stat, field, stat, edge, edge, stat, stat, field],
        out_specs=field,
        out_shape=field_b16,
        grid=(1,),
        compiler_params=params(32),
        name="image_grad",
    )(grad_one, *met5, stats5, x, own0, *met0, norm_rows[0], residual_grad)
    image_grad = permute(image_grad, turned)

    far_bit = 2 * lanes
    orders = ((1, 2, 4, near_bit, far_bit), (1, 4, 2, near_bit, far_bit))
    others = []
    bit = 8
    while bit < lanes:
        others.append(bit)
        bit *= 2

    def swap(x, bit):
        return permute(x, lambda i: i ^ bit)

    def total(pieces, order):
        for bit in order:
            half = pieces.shape[0] // 2
            coming = swap(pieces[half:], bit)
            pieces = (pieces[:half].astype(F32) + coming.astype(F32)).astype(BF16)
        for bit in others:
            pieces = (pieces.astype(F32) + swap(pieces, bit).astype(F32)).astype(BF16)
        for bit in order[::-1]:
            pieces = jnp.concatenate([pieces, swap(pieces, bit)], axis=0)
        return pieces

    matrix_parts = total(matrix_first, orders[0]), total(matrix_second, orders[1])
    two_parts = total(two_first, orders[0]), total(two_second, orders[1])
    one_parts = total(one_first, orders[0]), total(one_second, orders[1])

    def unpack(parts, taps, slots, base, into, name):
        block = pl.BlockSpec((PIECES, 1, channels // PIECES, channels // 2), lambda i: (0, i, 0, 0))
        extra = [] if into is None else [into]
        return pl.pallas_call(
            unpack_kernel,
            in_specs=[SMEM, block, block] + [pl.BlockSpec(memory_space=pl.ANY)] * len(extra),
            out_specs=pl.BlockSpec((1, channels, channels), lambda i: (base + i, 0, 0)),
            out_shape=shape((slots, channels, channels), F32),
            grid=(taps,),
            input_output_aliases={3: 0} if extra else {},
            compiler_params=params(16),
            name=name,
        )(place, *parts, *extra)

    matrices = unpack(matrix_parts, 4, 4, 0, None, "unpack_matrices")
    weights = unpack(two_parts, 9, 18, 9, None, "unpack_two")
    weights = unpack(one_parts, 9, 18, 0, weights, "unpack_one")

    small = jnp.concatenate(
        [bias_one[:1], bias_two[:1], sums5[:1], sums4[:1], sums3[:1], sums5[1:2], sums4[1:2], sums3[1:2], matrix_sums[:3]]
        + [jnp.zeros((5, channels), F32)],
        axis=0,
    )
    bit = 1
    while bit < devices:
        small = small + swap(small, bit)
        bit *= 2

    return (
        output.reshape(1, band, width, channels),
        image_grad.reshape(1, band, width, channels),
        weights.reshape(2, 3, 3, channels, channels),
        small[0:2],
        small[2:5],
        small[5:8],
        matrices[0:2],
        matrices[2],
        matrices[3],
        small[8:10],
        small[10],
    )


def solution(mesh):
    split = P("batch", "seq", None, None)
    in_specs = (split, P("batch", "seq", None), split) + (P(),) * 9
    out_specs = (split, split) + (P(),) * 9
    return jax.shard_map(body, mesh=mesh, in_specs=in_specs, out_specs=out_specs, check_vma=False)
```

time: 1140 us -> 555 us (0.49)
  waiting for transfers between devices: 470 us -> 187 us
  local copies, waits for them, and re-layouts: 258 us -> 41.4 us
  Pallas kernels: 0 us -> 178 us
  blocking collectives: 158 us -> 0 us
  matrix products: 129 us -> 0 us
  starting transfers between devices: 24 us -> 126 us
  other arithmetic: 82.5 us -> 10.7 us
  between operations: 15.5 us -> 3.03 us
    psum x1 -> x0, waiting for transfers between devices: 232 us -> none  [body(): lax.psum((conv_rows, bias_pair, gain_rows, shift_rows, qk_rows, value_gra...]
    ppermute x8 -> x99, waiting for transfers between devices: 3.67 us -> 187 us  [permute(): lax.ppermute(x, ('seq', 'batch'), [(i, to(i)) for i in range(devices)])]
    pallas_call x0 -> x19, Pallas kernels: none -> 178 us  [the longest x1 43.6 us: body(): pl.pallas_call(key_kernel, in_specs=[SMEM, field, whole(4 * pixels, chann...]
    psum x10 -> x0, blocking collectives: 145 us -> none  [the longest x3 46.4 us: group_stats(): group_mean = lax.psum(jnp.sum(grouped, axis=(0, 2)), 'seq') / group_count]
    all_gather x2 -> x0, waiting for transfers between devices: 131 us -> none  [the longest x1 70.9 us: body(): key_piece = lax.all_gather(key_rows, 'seq', axis=0, tiled=True)]
    dot_general x24 -> x0, matrix products: 129 us -> none  [the longest x8 39.6 us: inner_rows(): lax.dot_general(left, right, (((0,), (0,)), ((), ())), preferred_element_...]
    another operation x4 -> x1, local copies, waits for them, and re-layouts: 124 us -> 0.01 us  [gather_taps(): return jnp.stack(columns, 2).reshape(band_rows * canvas_width, -1)]
    reduce_scatter x1 -> x0, waiting for transfers between devices: 104 us -> none  [body(): lax.psum_scatter(jnp.concatenate([key_part, value_part], axis=1).astype(j...]
  transfers between devices with their start and end apart: 12 -> 99, of which waited for: 7 -> 51; matrix products, arithmetic and copies ran while one was open for 14% -> 5% of each run, Pallas kernels for 0% -> 23%
where the time goes in v1:
time: 555 us; the launch traced here: 545 us
  waiting for transfers between devices  187 us (34%)
  Pallas kernels  178 us (32%)
  starting transfers between devices  126 us (23%)
  local copies, waits for them, and re-layouts  41.4 us (7%)
  other arithmetic  10.7 us (2%)
    ppermute x99, waiting for transfers between devices, permute(): lax.ppermute(x, ('seq', 'batch'), [(i, to(i)) for i in range(devices)])  187 us
    ppermute x99, starting transfers between devices, permute(): lax.ppermute(x, ('seq', 'batch'), [(i, to(i)) for i in range(devices)])  126 us
    pallas_call x1, Pallas kernels, body(): pl.pallas_call(key_kernel, in_specs=[SMEM, field, whole(4 * pixels, chann...  43.6 us
    pallas_call x1, Pallas kernels, body(): pl.pallas_call(attend_kernel, in_specs=[field] * 5 + [whole(2, channels,...  31.4 us
    pallas_call x2, Pallas kernels, weight_grad(): pl.pallas_call(functools.partial(weight_grad_kernel, cot is not None), in...  29.3 us
    unnamed x190, local copies, waits for them, and re-layouts  27.2 us
    pallas_call x2, Pallas kernels, conv(): pl.pallas_call(kernel, in_specs=specs, out_specs=[field, field, edge, edg...  22.7 us
    pallas_call x2, Pallas kernels, conv_back(): pl.pallas_call(conv_back_kernel, in_specs=[SMEM, whole(3, pixels + 64, ch...  21.1 us
  transfers between devices with their start and end apart: 99, of which 51 were waited for; matrix products, arithmetic and copies ran while one was open for 5% of the time, Pallas kernels for 23%

profile of v1, /device:TPU:0, one launch (start us, length us, event | category | flops | bytes accessed | tf_op | source)
XLA Modules:
  0.0 545.2 jit_solution(7065128833831367921)
XLA Ops:
  0.6 9.5 %collective-permute-start = (bf16[1024,512]{1,0:T(8,128)(2,1)}, bf16[1024,512]{1,0:T(8,128)(2,1)}, u32[]{:S(2)}, u32[]{:S(2)}) collective-permute-start(bf16[1024,512]{1,0:T(8,128)(2,1)} %bitcast.19), channel_id=1, source_target_pairs={{0,0},{1,16},{2,2},{3,18},{4,4},{5,20},{6,6},{7,22},{8,8},{9,24},{... | collective-permute-start | bytes 3145736 | tf_op jit(solution)/shard_map/ppermute | solution.py:477
  21.3 33.5 %collective-permute-start.2 = (f32[40,512]{1,0:T(8,128)S(1)}, f32[40,512]{1,0:T(8,128)S(1)}, u32[]{:S(2)}, u32[]{:S(2)}) collective-permute-start(f32[40,512]{1,0:T(8,128)S(1)} %get-tuple-element.60), channel_id=1, source_target_pairs={{0,9},{1,25},{2,11},{3,27},{4,13},{5,29},{6,15},{7,31},{8,1},{9,17... | collective-permute-start | bytes 245768 | tf_op jit(solution)/shard_map/ppermute | solution.py:477
  54.9 5.4 collective-permute-done.2.cross_ref.refs_3_
  62.8 11.7 %conv_one.1 = (f32[1024,512]{1,0:T(8,128)S(1)}, bf16[1024,512]{1,0:T(8,128)(2,1)S(1)}, f32[40,512]{1,0:T(8,128)S(1)}, f32[40,512]{1,0:T(8,128)S(1)}, f32[8,512]{1,0:T(8,128)S(1)}) custom-call(s32[1]{0:T(128)} %bitcast.side_ref.refs_0_, bf16[1024,512]{1,0:T(8,128)(2,1)} %collective-permute-done.refs_1_.skip_ref.x_ref, ...), custom_call_target="tpu_custom_call" | custom-call | tf_op jit(solution)/shard_map/conv_one/pallas_call | solution.py:565
  79.5 11.0 %conv_two.1 = (f32[1024,512]{1,0:T(8,128)S(1)}, bf16[1024,512]{1,0:T(8,128)(2,1)S(1)}, f32[40,512]{1,0:T(8,128)S(1)}, f32[40,512]{1,0:T(8,128)S(1)}, f32[8,512]{1,0:T(8,128)S(1)}) custom-call(s32[1]{0:T(128)} %bitcast.side_ref.refs_0_, f32[1024,512]{1,0:T(8,128)S(1)} %get-tuple-element.63.x_ref, f32[40,512]{1,0:T(8,128)S(1)} %collective-permute-done.5.near_ref.x_near, ...), custom_call_target="tpu_custom_call" | custom-call | tf_op jit(solution)/shard_map/conv_two/pallas_call | solution.py:565
  100.2 20.1 %collective-permute-done.16.refs_2_ = bf16[1024,512]{1,0:T(8,128)(2,1)} collective-permute-done((bf16[1024,512]{1,0:T(8,128)(2,1)S(1)}, bf16[1024,512]{1,0:T(8,128)(2,1)}, u32[]{:S(2)}, u32[]{:S(2)}) %collective-permute-start.16) | collective-permute-done | bytes 1048608 | tf_op jit(solution)/shard_map/ppermute | solution.py:477
  120.9 21.6 %collective-permute-done.12.near_ref.refs_2_ = bf16[1024,512]{1,0:T(8,128)(2,1)S(1)} collective-permute-done((bf16[1024,512]{1,0:T(8,128)(2,1)S(1)}, bf16[1024,512]{1,0:T(8,128)(2,1)S(1)}, u32[]{:S(2)}, u32[]{:S(2)}) %collective-permute-start.12) | collective-permute-done | bytes 1048608 | tf_op jit(solution)/shard_map/ppermute | solution.py:477
  156.9 31.4 %attend.1 = (bf16[1024,512]{1,0:T(8,128)(2,1)}, bf16[1024,512]{1,0:T(8,128)(2,1)}, f32[4,8,256]{2,1,0:T(8,128)}) custom-call(bf16[1024,512]{1,0:T(8,128)(2,1)} %copy-done.6, bf16[1024,512]{1,0:T(8,128)(2,1)} %collective-permute-done.11.pair_ref.refs_1_, bf16[1024,512]{1,0:T(8,128)(2,1)} %copy-done.13, ...), custom_call_target="tpu_custom_call" | custom-call | tf_op jit(solution)/shard_map/attend/pallas_call | solution.py:615
  198.0 43.6 %key_value_grad.1 = (bf16[1024,512]{1,0:T(8,128)(2,1)}, bf16[1024,512]{1,0:T(8,128)(2,1)}, f32[1024,512]{1,0:T(8,128)}, f32[40,512]{1,0:T(8,128)}, f32[40,512]{1...) custom-call(s32[1]{0:T(128)} %bitcast.side_ref.refs_0_, bf16[1024,512]{1,0:T(8,128)(2,1)} %copy-done.6, ...), custom_call_target="tpu_custom_call" | custom-call | tf_op jit(solution)/shard_map/key_value_grad/pallas_call | solution.py:650
  254.0 15.3 %weight_two_grad.1 = (bf16[32,9,16,256]{3,2,1,0:T(8,128)(2,1)}, bf16[32,9,16,256]{3,2,1,0:T(8,128)(2,1)}, bf16[3,1088,512]{2,1,0:T(8,128)(2,1)}, f32[8,512]{1,0:T(8,128)}, f32[1024,512]{1,0:T(8,128)}) custom-call(s32[2]{0:T(128)} %copy-done.56, s32[1]{0:T(128)} %bitcast.side_ref.refs_0_, f32[1024,512]{1,0:T(8,128)} %copy-done.4, ...), custom_call_target="tpu_custom_call" | custom-call | tf_op jit(solution)/shard_map/weight_two_grad/pallas_call | solution.py:692
  271.2 10.3 %conv_two_back.1 = (f32[1024,512]{1,0:T(8,128)S(1)}, f32[40,512]{1,0:T(8,128)S(1)}, f32[40,512]{1,0:T(8,128)S(1)}, f32[8,512]{1,0:T(8,128)S(1)}, f32[8,512]{1,0:T(8,128)S(1)}) custom-call(s32[1]{0:T(128)} %bitcast.side_ref.refs_0_, bf16[3,1088,512]{2,1,0:T(8,128)(2,1)S(1)} %copy-done.18, bf16[9,1024,128]{2,1,0:T(8,128)(2,1)S(1)} %copy-done.1, ...), custom_call_target="tpu_custom_call" | custom-call | tf_op jit(solution)/shard_map/conv_two_back/pallas_call | solution.py:708
  290.0 14.0 %weight_one_grad.1 = (bf16[32,9,16,256]{3,2,1,0:T(8,128)(2,1)}, bf16[32,9,16,256]{3,2,1,0:T(8,128)(2,1)}, bf16[3,1088,512]{2,1,0:T(8,128)(2,1)}, f32[8,512]{1,0:T(8,128)}) custom-call(s32[2]{0:T(128)} %copy-done.56, s32[1]{0:T(128)} %bitcast.side_ref.refs_0_, f32[1024,512]{1,0:T(8,128)} %copy-done.9, f32[40,512]{1,0:T(8,128)} %copy-done.30, ...), custom_call_target="tpu_custom_call" | custom-call | tf_op jit(solution)/shard_map/weight_one_grad/pallas_call | solution.py:692
  306.0 10.8 %conv_one_back.1 = (f32[1024,512]{1,0:T(8,128)S(1)}, f32[40,512]{1,0:T(8,128)S(1)}, f32[40,512]{1,0:T(8,128)S(1)}, f32[8,512]{1,0:T(8,128)S(1)}, f32[8,512]{1,0:T(8,128)S(1)}) custom-call(s32[1]{0:T(128)} %bitcast.side_ref.refs_0_, bf16[3,1088,512]{2,1,0:T(8,128)(2,1)S(1)} %copy-done.19, bf16[9,1024,128]{2,1,0:T(8,128)(2,1)S(1)} %copy-done.2, ...), custom_call_target="tpu_custom_call" | custom-call | tf_op jit(solution)/shard_map/conv_one_back/pallas_call | solution.py:708
  403.6 8.9 %collective-permute-done.65 = bf16[8,9,16,256]{3,2,1,0:T(8,128)(2,1)S(1)} collective-permute-done((bf16[8,9,16,256]{3,2,1,0:T(8,128)(2,1)S(1)}, bf16[8,9,16,256]{3,2,1,0:T(8,128)(2,1)S(1)}, u32[]{:S(2)}, u32[]{:S(2)}) %collective-permute-start.65) | collective-permute-done | bytes 589856 | tf_op jit(solution)/shard_map/ppermute | solution.py:477
  415.0 9.2 %collective-permute-done.45 = bf16[8,9,16,256]{3,2,1,0:T(8,128)(2,1)S(1)} collective-permute-done((bf16[8,9,16,256]{3,2,1,0:T(8,128)(2,1)S(1)}, bf16[8,9,16,256]{3,2,1,0:T(8,128)(2,1)S(1)}, u32[]{:S(2)}, u32[]{:S(2)}) %collective-permute-start.45) | collective-permute-done | bytes 589856 | tf_op jit(solution)/shard_map/ppermute | solution.py:477
  429.7 5.4 collective-permute-done.66
  446.7 7.1 %collective-permute-done.68 = bf16[1,9,16,256]{3,2,1,0:T(8,128)(2,1)S(1)} collective-permute-done((bf16[1,9,16,256]{3,2,1,0:T(8,128)(2,1)S(1)}, bf16[1,9,16,256]{3,2,1,0:T(8,128)(2,1)S(1)}, u32[]{:S(2)}, u32[]{:S(2)}) %collective-permute-start.68) | collective-permute-done | bytes 73760 | tf_op jit(solution)/shard_map/ppermute | solution.py:477
  453.9 7.7 %collective-permute-done.58 = bf16[1,9,16,256]{3,2,1,0:T(8,128)(2,1)S(1)} collective-permute-done((bf16[1,9,16,256]{3,2,1,0:T(8,128)(2,1)S(1)}, bf16[1,9,16,256]{3,2,1,0:T(8,128)(2,1)S(1)}, u32[]{:S(2)}, u32[]{:S(2)}) %collective-permute-start.58) | collective-permute-done | bytes 73760 | tf_op jit(solution)/shard_map/ppermute | solution.py:477
  473.8 5.3 collective-permute-done.49
  479.2 5.5 %collective-permute-done.39 = bf16[1,9,16,256]{3,2,1,0:T(8,128)(2,1)S(1)} collective-permute-done((bf16[1,9,16,256]{3,2,1,0:T(8,128)(2,1)S(1)}, bf16[1,9,16,256]{3,2,1,0:T(8,128)(2,1)S(1)}, u32[]{:S(2)}, u32[]{:S(2)}) %collective-permute-start.39) | collective-permute-done | bytes 73760 | tf_op jit(solution)/shard_map/ppermute | solution.py:477
  492.6 5.6 %collective-permute-done.61 = bf16[4,9,16,256]{3,2,1,0:T(8,128)(2,1)S(1)} collective-permute-done((bf16[4,9,16,256]{3,2,1,0:T(8,128)(2,1)S(1)}, bf16[4,9,16,256]{3,2,1,0:T(8,128)(2,1)S(1)}, u32[]{:S(2)}, u32[]{:S(2)}) %collective-permute-start.61) | collective-permute-done | bytes 294944 | tf_op jit(solution)/shard_map/ppermute | solution.py:477
  500.9 7.3 %collective-permute-done.41 = bf16[4,9,16,256]{3,2,1,0:T(8,128)(2,1)S(1)} collective-permute-done((bf16[4,9,16,256]{3,2,1,0:T(8,128)(2,1)S(1)}, bf16[4,9,16,256]{3,2,1,0:T(8,128)(2,1)S(1)}, u32[]{:S(2)}, u32[]{:S(2)}) %collective-permute-start.41) | collective-permute-done | bytes 294944 | tf_op jit(solution)/shard_map/ppermute | solution.py:477
  530.6 6.0 %unpack_two.1.rest_0_ = f32[18,512,512]{2,1,0:T(8,128)} custom-call(s32[2]{0:T(128)S(1)} %copy-done.57, bf16[32,9,16,256]{3,2,1,0:T(8,128)(2,1)S(1)} %constant_dynamic-update-slice_fusion.27.first_ref, bf16[32,9,16,256]{3,2,1,0:T(8,128)(2,1)S(1)} %constant_dynamic-update-slice_fusion.38.second_ref), custom_call_target="tpu_custom_call" | custom-call | tf_op jit(solution)/shard_map/unpack_two/pallas_call | solution.py:773
  536.8 6.0 %unpack_one.1 = f32[18,512,512]{2,1,0:T(8,128)} custom-call(s32[2]{0:T(128)S(1)} %copy-done.57, bf16[32,9,16,256]{3,2,1,0:T(8,128)(2,1)S(1)} %constant_dynamic-update-slice_fusion.5.first_ref, bf16[32,9,16,256]{3,2,1,0:T(8,128)(2,1)S(1)} %constant_dynamic-update-slice_fusion.16.second_ref, ...), custom_call_target="tpu_custom_call", output_to_operand_aliasing={{}: (3, {})} | custom-call | tf_op jit(solution)/shard_map/unpack_one/pallas_call | solution.py:773
  (513 shorter events, 229.8 us)
Async XLA Ops:
  0.6 62.2 %collective-permute-start = (bf16[1024,512]{1,0:T(8,128)(2,1)}, bf16[1024,512]{1,0:T(8,128)(2,1)}, u32[]{:S(2)}, u32[]{:S(2)}) collective-permute-start(bf16[1024,512]{1,0:T(8,128)(2,1)} %bitcast.19), channel_id=1, source_target_pairs={{0,0},{1,16},{2,2},{3,18},{4,4},{5,20},{6,6},{7,22},{8,8},{9,24},{... | collective-permute-start | bytes 3145736 | tf_op jit(solution)/shard_map/ppermute | solution.py:477
  10.2 82.7 %collective-permute-start.14 = (bf16[1024,512]{1,0:T(8,128)(2,1)}, bf16[1024,512]{1,0:T(8,128)(2,1)S(1)}, u32[]{:S(2)}, u32[]{:S(2)}) collective-permute-start(bf16[1024,512]{1,0:T(8,128)(2,1)} %bitcast.28), channel_id=1, source_target_pairs={{0,0},{1,16},{2,2},{3,18},{4,4},{5,20},{6,6},{7,22},{8,8},{9,24},{... | collective-permute-start | bytes 3145736 | tf_op jit(solution)/shard_map/ppermute | solution.py:477
  15.9 39.0 %collective-permute-start.3 = (f32[8,512]{1,0:T(8,128)S(1)}, f32[8,512]{1,0:T(8,128)S(1)}, u32[]{:S(2)}, u32[]{:S(2)}) collective-permute-start(f32[8,512]{1,0:T(8,128)S(1)} %get-tuple-element.61), channel_id=1, source_target_pairs={{0,1},{1,17},{2,3},{3,19},{4,5},{5,21},{6,7},{7,23},{8,9},{9,25},{... | collective-permute-start | bytes 49160 | tf_op jit(solution)/shard_map/ppermute | solution.py:477
  16.5 38.4 %collective-permute-start.1 = (f32[40,512]{1,0:T(8,128)S(1)}, f32[40,512]{1,0:T(8,128)S(1)}, u32[]{:S(2)}, u32[]{:S(2)}) collective-permute-start(f32[40,512]{1,0:T(8,128)S(1)} %get-tuple-element.59), channel_id=1, source_target_pairs={{0,8},{1,24},{2,10},{3,26},{4,12},{5,28},{6,14},{7,30},{8,0},{9,16... | collective-permute-start | bytes 245768 | tf_op jit(solution)/shard_map/ppermute | solution.py:477
  21.3 39.0 %collective-permute-start.2 = (f32[40,512]{1,0:T(8,128)S(1)}, f32[40,512]{1,0:T(8,128)S(1)}, u32[]{:S(2)}, u32[]{:S(2)}) collective-permute-start(f32[40,512]{1,0:T(8,128)S(1)} %get-tuple-element.60), channel_id=1, source_target_pairs={{0,9},{1,25},{2,11},{3,27},{4,13},{5,29},{6,15},{7,31},{8,1},{9,17... | collective-permute-start | bytes 245768 | tf_op jit(solution)/shard_map/ppermute | solution.py:477
  92.9 27.5 %collective-permute-start.16 = (bf16[1024,512]{1,0:T(8,128)(2,1)S(1)}, bf16[1024,512]{1,0:T(8,128)(2,1)}, u32[]{:S(2)}, u32[]{:S(2)}) collective-permute-start(bf16[1024,512]{1,0:T(8,128)(2,1)S(1)} %collective-permute-done.14.refs_0_.rest_0_.cotangent_ref), channel_id=1, source_target_pairs={{0,8},{1,9},{2,10},{3,11},{4,12},{5,13},{6,14},{7,15},{8,0},{9,1},... | collective-permute-start | bytes 3145736 | tf_op jit(solution)/shard_map/ppermute | solution.py:477
  98.9 43.6 %collective-permute-start.12 = (bf16[1024,512]{1,0:T(8,128)(2,1)S(1)}, bf16[1024,512]{1,0:T(8,128)(2,1)S(1)}, u32[]{:S(2)}, u32[]{:S(2)}) collective-permute-start(bf16[1024,512]{1,0:T(8,128)(2,1)S(1)} %normed.1.own_ref.refs_0_.normed_ref), channel_id=1, source_target_pairs={{0,8},{1,9},{2,10},{3,11},{4,12},{5,13},{6,14},{7,15},{8,0},{9,1},... | collective-permute-start | bytes 3145736 | tf_op jit(solution)/shard_map/ppermute | solution.py:477
  99.2 51.4 %collective-permute-start.15 = (bf16[1024,512]{1,0:T(8,128)(2,1)S(1)}, bf16[1024,512]{1,0:T(8,128)(2,1)}, u32[]{:S(2)}, u32[]{:S(2)}) collective-permute-start(bf16[1024,512]{1,0:T(8,128)(2,1)S(1)} %collective-permute-done.14.refs_0_.rest_0_.cotangent_ref), channel_id=1, source_target_pairs={{0,1},{1,0},{2,3},{3,2},{4,5},{5,4},{6,7},{7,6},{8,9},{9,8},{10,11... | collective-permute-start | bytes 3145736 | tf_op jit(solution)/shard_map/ppermute | solution.py:477
  120.4 30.3 %collective-permute-start.17 = (bf16[1024,512]{1,0:T(8,128)(2,1)}, bf16[1024,512]{1,0:T(8,128)(2,1)}, u32[]{:S(2)}, u32[]{:S(2)}) collective-permute-start(bf16[1024,512]{1,0:T(8,128)(2,1)} %collective-permute-done.16.refs_2_), channel_id=1, source_target_pairs={{0,1},{1,0},{2,3},{3,2},{4,5},{5,4},{6,7},{7,6},{8,9},{9,8},{10,11... | collective-permute-start | bytes 3145736 | tf_op jit(solution)/shard_map/ppermute | solution.py:477
  120.4 36.5 %collective-permute-start.11 = (bf16[1024,512]{1,0:T(8,128)(2,1)S(1)}, bf16[1024,512]{1,0:T(8,128)(2,1)}, u32[]{:S(2)}, u32[]{:S(2)}) collective-permute-start(bf16[1024,512]{1,0:T(8,128)(2,1)S(1)} %normed.1.own_ref.refs_0_.normed_ref), channel_id=1, source_target_pairs={{0,1},{1,0},{2,3},{3,2},{4,5},{5,4},{6,7},{7,6},{8,9},{9,8},{10,11... | collective-permute-start | bytes 3145736 | tf_op jit(solution)/shard_map/ppermute | solution.py:477
  149.9 40.9 %collective-permute-start.20 = (f32[32,512]{1,0:T(8,128)S(1)}, f32[32,512]{1,0:T(8,128)S(1)}, u32[]{:S(2)}, u32[]{:S(2)}) collective-permute-start(f32[32,512]{1,0:T(8,128)S(1)} %get-tuple-element.121), channel_id=1, source_target_pairs={{0,9},{1,8},{2,11},{3,10},{4,13},{5,12},{6,15},{7,14},{8,1},{9,0},... | collective-permute-start | bytes 196616 | tf_op jit(solution)/shard_map/ppermute | solution.py:477
  252.5 95.0 %collective-permute-start.89 = (bf16[16,4,16,256]{3,2,1,0:T(8,128)(2,1)}, bf16[16,4,16,256]{3,2,1,0:T(8,128)(2,1)}, u32[]{:S(2)}, u32[]{:S(2)}) collective-permute-start(bf16[16,4,16,256]{3,2,1,0:T(8,128)(2,1)} %slice.355), channel_id=1, source_target_pairs={{0,1},{1,0},{2,3},{3,2},{4,5},{5,4},{6,7},{7,6},{8,9},{9,8},{10,11... | collective-permute-start | bytes 1572872 | tf_op jit(solution)/shard_map/ppermute | solution.py:477
  253.2 91.4 %collective-permute-start.79 = (bf16[16,4,16,256]{3,2,1,0:T(8,128)(2,1)}, bf16[16,4,16,256]{3,2,1,0:T(8,128)(2,1)}, u32[]{:S(2)}, u32[]{:S(2)}) collective-permute-start(bf16[16,4,16,256]{3,2,1,0:T(8,128)(2,1)} %slice.345), channel_id=1, source_target_pairs={{0,1},{1,0},{2,3},{3,2},{4,5},{5,4},{6,7},{7,6},{8,9},{9,8},{10,11... | collective-permute-start | bytes 1572872 | tf_op jit(solution)/shard_map/ppermute | solution.py:477
  340.6 50.1 %collective-permute-start.64 = (bf16[16,9,16,256]{3,2,1,0:T(8,128)(2,1)S(1)}, bf16[16,9,16,256]{3,2,1,0:T(8,128)(2,1)S(1)}, u32[]{:S(2)}, u32[]{:S(2)}) collective-permute-start(bf16[16,9,16,256]{3,2,1,0:T(8,128)(2,1)S(1)} %slice.323), channel_id=1, source_target_pairs={{0,1},{1,0},{2,3},{3,2},{4,5},{5,4},{6,7},{7,6},{8,9},{9,8},{10,11... | collective-permute-start | bytes 3538952 | tf_op jit(solution)/shard_map/ppermute | solution.py:477
  340.7 51.2 %collective-permute-start.54 = (bf16[16,9,16,256]{3,2,1,0:T(8,128)(2,1)S(1)}, bf16[16,9,16,256]{3,2,1,0:T(8,128)(2,1)S(1)}, u32[]{:S(2)}, u32[]{:S(2)}) collective-permute-start(bf16[16,9,16,256]{3,2,1,0:T(8,128)(2,1)S(1)} %slice.313), channel_id=1, source_target_pairs={{0,1},{1,0},{2,3},{3,2},{4,5},{5,4},{6,7},{7,6},{8,9},{9,8},{10,11... | collective-permute-start | bytes 3538952 | tf_op jit(solution)/shard_map/ppermute | solution.py:477
  344.6 48.4 %collective-permute-start.44 = (bf16[16,9,16,256]{3,2,1,0:T(8,128)(2,1)S(1)}, bf16[16,9,16,256]{3,2,1,0:T(8,128)(2,1)S(1)}, u32[]{:S(2)}, u32[]{:S(2)}) collective-permute-start(bf16[16,9,16,256]{3,2,1,0:T(8,128)(2,1)S(1)} %slice.303), channel_id=1, source_target_pairs={{0,1},{1,0},{2,3},{3,2},{4,5},{5,4},{6,7},{7,6},{8,9},{9,8},{10,11... | collective-permute-start | bytes 3538952 | tf_op jit(solution)/shard_map/ppermute | solution.py:477
  386.6 124.2 %collective-permute-start.18 = (bf16[1024,512]{1,0:T(8,128)(2,1)S(1)}, bf16[1024,512]{1,0:T(8,128)(2,1)S(1)}, u32[]{:S(2)}, u32[]{:S(2)}) collective-permute-start(bf16[1024,512]{1,0:T(8,128)(2,1)S(1)} %output.1), channel_id=1, source_target_pairs={{0,0},{1,16},{2,2},{3,18},{4,4},{5,20},{6,6},{7,22},{8,8},{9,24},{... | collective-permute-start | bytes 3145736 | tf_op jit(solution)/shard_map/ppermute | solution.py:477
  393.0 19.5 %collective-permute-start.65 = (bf16[8,9,16,256]{3,2,1,0:T(8,128)(2,1)S(1)}, bf16[8,9,16,256]{3,2,1,0:T(8,128)(2,1)S(1)}, u32[]{:S(2)}, u32[]{:S(2)}) collective-permute-start(bf16[8,9,16,256]{3,2,1,0:T(8,128)(2,1)S(1)} %slice.398), channel_id=1, source_target_pairs={{0,4},{1,5},{2,6},{3,7},{4,0},{5,1},{6,2},{7,3},{8,12},{9,13},{10,... | collective-permute-start | bytes 1769480 | tf_op jit(solution)/shard_map/ppermute | solution.py:477
  401.1 117.7 %collective-permute-start.33 = (bf16[1024,512]{1,0:T(8,128)(2,1)S(1)}, bf16[1024,512]{1,0:T(8,128)(2,1)S(1)}, u32[]{:S(2)}, u32[]{:S(2)}) collective-permute-start(bf16[1024,512]{1,0:T(8,128)(2,1)S(1)} %image_grad.1), channel_id=1, source_target_pairs={{0,0},{1,16},{2,2},{3,18},{4,4},{5,20},{6,6},{7,22},{8,8},{9,24},{... | collective-permute-start | bytes 3145736 | tf_op jit(solution)/shard_map/ppermute | solution.py:477
  402.2 22.0 %collective-permute-start.45 = (bf16[8,9,16,256]{3,2,1,0:T(8,128)(2,1)S(1)}, bf16[8,9,16,256]{3,2,1,0:T(8,128)(2,1)S(1)}, u32[]{:S(2)}, u32[]{:S(2)}) collective-permute-start(bf16[8,9,16,256]{3,2,1,0:T(8,128)(2,1)S(1)} %slice.382), channel_id=1, source_target_pairs={{0,4},{1,5},{2,6},{3,7},{4,0},{5,1},{6,2},{7,3},{8,12},{9,13},{10,... | collective-permute-start | bytes 1769480 | tf_op jit(solution)/shard_map/ppermute | solution.py:477
  413.4 21.6 %collective-permute-start.66 = (bf16[4,9,16,256]{3,2,1,0:T(8,128)(2,1)S(1)}, bf16[4,9,16,256]{3,2,1,0:T(8,128)(2,1)S(1)}, u32[]{:S(2)}, u32[]{:S(2)}) collective-permute-start(bf16[4,9,16,256]{3,2,1,0:T(8,128)(2,1)S(1)} %slice.400), channel_id=1, source_target_pairs={{0,2},{1,3},{2,0},{3,1},{4,6},{5,7},{6,4},{7,5},{8,10},{9,11},{10,... | collective-permute-start | bytes 884744 | tf_op jit(solution)/shard_map/ppermute | solution.py:477
  441.8 19.8 %collective-permute-start.47 = (bf16[2,9,16,256]{3,2,1,0:T(8,128)(2,1)S(1)}, bf16[2,9,16,256]{3,2,1,0:T(8,128)(2,1)S(1)}, u32[]{:S(2)}, u32[]{:S(2)}) collective-permute-start(bf16[2,9,16,256]{3,2,1,0:T(8,128)(2,1)S(1)} %slice.386), channel_id=1, source_target_pairs={{0,8},{1,9},{2,10},{3,11},{4,12},{5,13},{6,14},{7,15},{8,0},{9,1},... | collective-permute-start | bytes 442376 | tf_op jit(solution)/shard_map/ppermute | solution.py:477
  443.7 20.9 %collective-permute-start.37 = (bf16[2,9,16,256]{3,2,1,0:T(8,128)(2,1)S(1)}, bf16[2,9,16,256]{3,2,1,0:T(8,128)(2,1)S(1)}, u32[]{:S(2)}, u32[]{:S(2)}) collective-permute-start(bf16[2,9,16,256]{3,2,1,0:T(8,128)(2,1)S(1)} %slice.378), channel_id=1, source_target_pairs={{0,8},{1,9},{2,10},{3,11},{4,12},{5,13},{6,14},{7,15},{8,0},{9,1},... | collective-permute-start | bytes 442376 | tf_op jit(solution)/shard_map/ppermute | solution.py:477
  491.6 18.7 %collective-permute-start.51 = (bf16[4,9,16,256]{3,2,1,0:T(8,128)(2,1)S(1)}, bf16[4,9,16,256]{3,2,1,0:T(8,128)(2,1)S(1)}, u32[]{:S(2)}, u32[]{:S(2)}) collective-permute-start(bf16[4,9,16,256]{3,2,1,0:T(8,128)(2,1)S(1)} %pad_maximum_fusion.5), channel_id=1, source_target_pairs={{0,2},{1,3},{2,0},{3,1},{4,6},{5,7},{6,4},{7,5},{8,10},{9,11},{10,... | collective-permute-start | bytes 884744 | tf_op jit(solution)/shard_map/ppermute | solution.py:477
  (158 other events, 2145.3 us)

commit v2 on v1

v2 whole, which is shorter than its diff:
```python
import functools

import jax
import jax.numpy as jnp
from jax import lax
from jax.experimental import pallas as pl
from jax.experimental.pallas import tpu as pltpu
from jax.sharding import PartitionSpec as P

GROUPS = 32
EPSILON = 1e-06
MASKED_SCORE = -1e30
F32 = jnp.float32
BF16 = jnp.bfloat16
MIB = 1024 * 1024
PIECES = 32


def params(mib):
    return pltpu.CompilerParams(vmem_limit_bytes=mib * MIB)


def shape(dims, dtype):
    return jax.ShapeDtypeStruct(dims, dtype)


SMEM = pl.BlockSpec(memory_space=pltpu.SMEM)


def whole(*dims):
    return pl.BlockSpec(dims, lambda *_: (0,) * len(dims))


def group_sum(row):
    channels = row.shape[1]
    lane = lax.broadcasted_iota(jnp.int32, row.shape, 1)
    step = 1
    while step < channels // GROUPS:
        ahead = pltpu.roll(row, channels - step, 1)
        behind = pltpu.roll(row, step, 1)
        row = row + jnp.where((lane & step) == 0, ahead, behind)
        step *= 2
    return row


def rows_of(*parts):
    channels = parts[0].shape[1]
    line = lax.broadcasted_iota(jnp.int32, (8, channels), 0)
    out = jnp.zeros((8, channels), F32)
    for i, part in enumerate(parts):
        out = jnp.where(line == i, jnp.broadcast_to(part, (8, channels)), out)
    return out


def eight(row):
    return jnp.broadcast_to(row, (8, row.shape[1]))


def local_stats(values, channels, pixels):
    count = float(pixels * (channels // GROUPS))
    mean = group_sum(eight(jnp.sum(values, axis=0, keepdims=True)))[0:1] / count
    centered = values - mean
    square = group_sum(eight(jnp.sum(centered * centered, axis=0, keepdims=True)))[0:1]
    return mean, square


def joined_stats(own, near, cross, pair, pixels):
    bands = [own[0:2], near[32:34], cross[32:34], pair[0:2]]
    channels = bands[0].shape[1]
    count = float(pixels * (channels // GROUPS))
    mean = (bands[0][0:1] + bands[1][0:1] + bands[2][0:1] + bands[3][0:1]) * 0.25
    total = 0.0
    for band in bands:
        gap = band[0:1] - mean
        total = total + band[1:2] + count * gap * gap
    return mean, lax.rsqrt(total / (4.0 * count) + EPSILON)


def joined_sums(own, near, cross, pair, pixels):
    bands = [own[0:2], near[32:34], cross[32:34], pair[0:2]]
    channels = bands[0].shape[1]
    count = 4.0 * float(pixels * (channels // GROUPS))
    sums = (bands[0] + bands[1]) + (bands[2] + bands[3])
    return sums[0:1] / count, sums[1:2] / count


def sigmoid(values):
    return 0.5 * jnp.tanh(0.5 * values) + 0.5


def edges_out(side_ref, out_ref, near_ref, cross_ref, stats):
    pixels = out_ref.shape[0]
    side = side_ref[0]
    last = pixels - 32
    near_ref[0:32, :] = out_ref[pl.ds(pl.multiple_of(last * (1 - side), 32), 32), :].astype(F32)
    cross_ref[0:32, :] = out_ref[pl.ds(pl.multiple_of(last * side, 32), 32), :].astype(F32)
    near_ref[32:40, :] = stats
    cross_ref[32:40, :] = stats


def columns_of(frame, shifted, rows):
    for b in range(3):
        shifted[b] = frame[7 + b : 7 + b + rows, :].astype(BF16)


def masked(values, mask):
    channels = values.shape[1]
    return [values[:, i * 128 : (i + 1) * 128] * mask for i in range(channels // 128)]


def tap_rows(shifted, mask_ref, start, count, row):
    parts = []
    for b in range(3):
        block = shifted[b, pl.ds(pl.multiple_of(row * 32 + start, 32), count), :]
        parts += masked(block, mask_ref[b, start : start + count, :])
    return parts


def first_kernel(image_ref, tiles_ref, side_ref, near_ref, cross_ref, stats_ref):
    pixels, channels = image_ref.shape
    mean, square = local_stats(image_ref[...].astype(F32), channels, pixels)
    stats = rows_of(mean, square, tiles_ref[0:1], tiles_ref[1:2])
    stats_ref[...] = stats
    edges_out(side_ref, image_ref, near_ref, cross_ref, stats)


def mask_kernel(where_ref, own_ref, near_ref, cross_ref, pair_ref, mask_ref, column_ref, row_ref, frame):
    side, first, last = where_ref[0], where_ref[1], where_ref[2]

    def line(ref, base):
        return jnp.concatenate([ref[base + 2 : base + 3, :], ref[base + 3 : base + 4, :]], axis=1)

    own, near, cross, pair = line(own_ref, 0), line(near_ref, 32), line(cross_ref, 32), line(pair_ref, 0)
    pixels = own.shape[1]
    row_ref[...] = jnp.concatenate([own, pair, near, cross], axis=1)

    def upright(row):
        return jnp.transpose(jnp.broadcast_to(row, (128, row.shape[1])))

    column = upright(own)
    column_ref[...] = column
    above = jnp.where(side == 0, cross[:, pixels - 128 :], near[:, pixels - 128 :])
    below = jnp.where(side == 0, near[:, :128], cross[:, :128])
    outside = jnp.full((32, 128), -1.0, F32)
    frame[0:8, :] = jnp.zeros((8, 128), F32)
    frame[8:40, :] = jnp.where(first == 1, outside, upright(above)[96:128, :])
    frame[40 : 40 + pixels, :] = column
    frame[40 + pixels : 72 + pixels, :] = jnp.where(last == 1, outside, upright(below)[0:32, :])
    frame[72 + pixels : 80 + pixels, :] = jnp.zeros((8, 128), F32)
    place = lax.broadcasted_iota(jnp.int32, (pixels, 128), 0) & 31
    for a in range(3):
        for b in range(3):
            start = 8 + a * 32 + b - 1
            same = frame[start : start + pixels, :] == column
            if b == 0:
                same = same & (place > 0)
            if b == 2:
                same = same & (place < 31)
            mask_ref[a * 3 + b] = jnp.where(same, 1.0, 0.0).astype(BF16)


def conv_kernel(
    side_ref, x_ref, near_ref, cross_ref, pair_ref, stats_ref, rows_ref, mask_ref, weight_ref, skip_ref,
    out_ref, act_ref, near_out, cross_out, stats_out, frame, shifted,
):
    row = pl.program_id(0)
    pixels, channels = x_ref.shape

    @pl.when(row == 0)
    def _():
        mean, inverse = joined_stats(stats_ref[...], near_ref[...], cross_ref[...], pair_ref[...], pixels)
        scale, shift, bias = rows_ref[0:1, :], rows_ref[1:2, :], rows_ref[2:3, :]

        def act(values):
            pre = (values - mean) * inverse * scale + shift
            return pre * sigmoid(pre)

        side = side_ref[0]
        near, cross = near_ref[0:32, :], cross_ref[0:32, :]
        frame[0:8, :] = jnp.zeros((8, channels), F32)
        frame[8:40, :] = act(jnp.where(side == 0, cross, near))
        frame[40 : 40 + pixels, :] = act(x_ref[...].astype(F32))
        frame[40 + pixels : 72 + pixels, :] = act(jnp.where(side == 0, near, cross))
        frame[72 + pixels : 80 + pixels, :] = jnp.zeros((8, channels), F32)
        columns_of(frame, shifted, pixels + 64)
        act_ref[...] = shifted[1, 32 : 32 + pixels, :]
        start = jnp.broadcast_to(bias, (pixels, channels))
        if skip_ref is not None:
            start = start + skip_ref[...].astype(F32)
        out_ref[...] = start

    weight = weight_ref[...].reshape(3 * channels, channels)
    for i in range(pixels // 256):
        taps = jnp.concatenate(tap_rows(shifted, mask_ref, i * 256, 256, row), axis=1)
        out_ref[i * 256 : (i + 1) * 256, :] += jnp.dot(taps, weight, preferred_element_type=F32)

    @pl.when(row == 2)
    def _():
        mean, square = local_stats(out_ref[...], channels, pixels)
        stats = rows_of(mean, square)
        stats_out[...] = stats
        edges_out(side_ref, out_ref, near_out, cross_out, stats)


def normed_kernel(x_ref, near_ref, cross_ref, pair_ref, stats_ref, rows_ref, out_ref):
    pixels = x_ref.shape[0]
    mean, inverse = joined_stats(stats_ref[...], near_ref[...], cross_ref[...], pair_ref[...], pixels)
    out_ref[...] = ((x_ref[...] - mean) * inverse * rows_ref[0:1, :] + rows_ref[1:2, :]).astype(BF16)


def nn(left, right):
    return jnp.dot(left, right, preferred_element_type=F32)


def nt(left, right):
    return lax.dot_general(left, right, (((1,), (1,)), ((), ())), preferred_element_type=F32)


def early_kernel(
    own_ref, pair_ref, cot_own, cot_pair, qk_ref, value_ref, proj_ref, bias_ref, keys_ref, values_ref, queries_ref, grads_ref
):
    pixels = own_ref.shape[0]
    for i, (rows_ref, cot_ref) in enumerate(((own_ref, cot_own), (pair_ref, cot_pair))):
        part = slice(i * pixels, (i + 1) * pixels)
        rows = rows_ref[...]
        queries_ref[part, :] = (nn(rows, qk_ref[0]) + bias_ref[0:1, :]).astype(BF16)
        keys_ref[part, :] = nn(rows, qk_ref[1]).astype(BF16)
        values_ref[part, :] = (nn(rows, value_ref[...]) + bias_ref[1:2, :]).astype(BF16)
        grads_ref[part, :] = nt(cot_ref[...], proj_ref[...]).astype(BF16)


def attend_kernel(
    near_ref, cross_ref, keys_ref, values_ref, queries_ref, grads_ref, qk_ref, value_ref, bias_ref, column_ref, row_ref,
    attended_ref, query_grad_ref, totals_ref, far_keys, far_values,
):
    pixels, channels = near_ref.shape
    scale = channels ** (-0.5)
    for i, ref in enumerate((near_ref, cross_ref)):
        part = slice(i * pixels, (i + 1) * pixels)
        rows = ref[...]
        far_keys[part, :] = nn(rows, qk_ref[1]).astype(BF16)
        far_values[part, :] = (nn(rows, value_ref[...]) + bias_ref[1:2, :]).astype(BF16)
    block = totals_ref.shape[2]
    halves = ((keys_ref, values_ref, slice(0, 2 * pixels)), (far_keys, far_values, slice(2 * pixels, 4 * pixels)))

    def step(i, carry):
        part = pl.ds(pl.multiple_of(i * block, block), block)
        queries, upstream = queries_ref[part, :], grads_ref[part, :]
        column = column_ref[part, 0:1]
        scores = []
        for keys, _, span in halves:
            product = nt(queries, keys[...]) * scale
            scores.append(jnp.where(column == row_ref[:, span], product, MASKED_SCORE))
        top = jnp.maximum(*[jnp.max(s, axis=1, keepdims=True) for s in scores])
        weights = [jnp.exp(s - top) for s in scores]
        total = sum(jnp.sum(w, axis=1, keepdims=True) for w in weights)
        inverse = 1.0 / total
        attended = sum(nn(w.astype(BF16), values[...]) for w, (_, values, _) in zip(weights, halves)) * inverse
        attended_ref[part, :] = attended.astype(BF16)
        delta = jnp.sum(attended * upstream.astype(F32), axis=1, keepdims=True)
        query_grad = 0.0
        for w, (keys, values, _) in zip(weights, halves):
            prob_grad = nt(upstream, values[...])
            score_grad = (w * inverse * (prob_grad - delta)).astype(BF16)
            query_grad = query_grad + nn(score_grad, keys[...])
        query_grad_ref[part, :] = (query_grad * scale).astype(BF16)
        log_total = jnp.transpose(jnp.broadcast_to(top + jnp.log(total), (block, 128)))
        turned = jnp.transpose(jnp.broadcast_to(delta, (block, 128)))
        totals_ref[i, 0:1, :] = log_total[0:1, :]
        totals_ref[i, 1:2, :] = turned[0:1, :]
        totals_ref[i, 2:8, :] = jnp.zeros((6, block), F32)
        return carry

    lax.fori_loop(0, pixels // block, step, 0)


def out_kernel(attended_ref, residual_ref, matrix_ref, bias_ref, out_ref):
    out_ref[...] = (residual_ref[...] + nn(attended_ref[...], matrix_ref[...]) + bias_ref[0:1, :]).astype(BF16)


def norm_back_sums(upstream, hat, gain):
    outer = jnp.sum(upstream * hat, axis=0, keepdims=True)
    inner = jnp.sum(upstream, axis=0, keepdims=True)
    first = group_sum(eight(inner * gain))[0:1]
    second = group_sum(eight(outer * gain))[0:1]
    return rows_of(outer, inner), rows_of(first, second)


def key_kernel(
    side_ref, keys, values, queries_ref, grads_ref, near_hbm, cross_hbm, cot_near_hbm, cot_cross_hbm, query_grad_hbm,
    qk_ref, value_ref, proj_ref, bias_ref,
    totals_own, totals_pair, totals_near, totals_cross, column_ref, row_ref,
    residual_hbm, stats_ref, near_ref, cross_ref, pair_ref, rows_ref,
    key_grad_ref, value_grad_ref, normed_grad_ref, near_out, cross_out, stats_out, sums_out,
    key_sum, value_sum, far, query_grad_ref, residual_ref, arrived,
):
    pixels, channels = keys.shape
    scale = channels ** (-0.5)
    coming = [
        pltpu.make_async_copy(source, target, arrived.at[i])
        for i, (source, target) in enumerate(
            (
                (near_hbm, far.at[0]), (cot_near_hbm, far.at[1]), (cross_hbm, far.at[2]), (cot_cross_hbm, far.at[3]),
                (query_grad_hbm, query_grad_ref), (residual_hbm, residual_ref),
            )
        )
    ]
    for copy in coming:
        copy.start()
    key_sum[...] = jnp.zeros_like(key_sum)
    value_sum[...] = jnp.zeros_like(value_sum)
    chunk = totals_own.shape[2]
    blocks = pixels // chunk

    def add(queries, upstream, totals, i, at):
        scores = nt(keys[...], queries) * scale
        weights = jnp.exp(scores - totals[i, 0:1, :])
        weights = jnp.where(column_ref[:, 0:1] == row_ref[at, 0:1, :], weights, 0.0)
        value_sum[...] += nn(weights.astype(BF16), upstream)
        prob_grad = nt(values[...], upstream)
        score_grad = (weights * (prob_grad - totals[i, 1:2, :])).astype(BF16)
        key_sum[...] += nn(score_grad, queries)

    for group, totals in enumerate((totals_own, totals_pair)):

        def step(i, carry, group=group, totals=totals):
            part = pl.ds(pl.multiple_of(group * pixels + i * chunk, chunk), chunk)
            add(queries_ref[part, :], grads_ref[part, :], totals, i, group * blocks + i)
            return carry

        lax.fori_loop(0, blocks, step, 0)
    for group, totals in enumerate((totals_near, totals_cross)):
        coming[2 * group].wait()
        coming[2 * group + 1].wait()

        def far_step(i, carry, group=group, totals=totals):
            part = pl.ds(pl.multiple_of(i * chunk, chunk), chunk)
            queries = (nn(far[2 * group, part, :], qk_ref[0]) + bias_ref[0:1, :]).astype(BF16)
            upstream = nt(far[2 * group + 1, part, :], proj_ref[...]).astype(BF16)
            add(queries, upstream, totals, i, (group + 2) * blocks + i)
            return carry

        lax.fori_loop(0, blocks, far_step, 0)
    coming[4].wait()
    coming[5].wait()
    key_grad = (key_sum[...] * scale).astype(BF16)
    value_grad = value_sum[...].astype(BF16)
    key_grad_ref[...] = key_grad
    value_grad_ref[...] = value_grad
    normed_grad = nt(query_grad_ref[...], qk_ref[0]) + nt(key_grad, qk_ref[1]) + nt(value_grad, value_ref[...])
    normed_grad_ref[...] = normed_grad
    mean, inverse = joined_stats(stats_ref[...], near_ref[...], cross_ref[...], pair_ref[...], pixels)
    hat = (residual_ref[...] - mean) * inverse
    sums, groups = norm_back_sums(normed_grad, hat, rows_ref[0:1, :])
    sums_out[...] = sums
    stats_out[...] = groups
    edges_out(side_ref, normed_grad_ref, near_out, cross_out, groups)


def scatter_pieces(place_ref, product, tap, keep_ref, send_ref, matrix):
    rows, channels = product.shape
    half, height = channels // 2, rows // PIECES
    matrix[...] = product.astype(BF16)
    for q in range(PIECES):
        into = keep_ref if q < PIECES // 2 else send_ref
        for stream in range(2):
            start = pl.multiple_of((q ^ place_ref[stream]) * height, height)
            into[stream, q % (PIECES // 2), tap] = matrix[pl.ds(start, height), stream * half : (stream + 1) * half]


def tn(left, right):
    return lax.dot_general(left, right, (((0,), (0,)), ((), ())), preferred_element_type=F32)


def matrix_kernel(
    place_ref, normed_ref, query_grad_ref, key_grad_ref, value_grad_ref, attended_ref, cotangent_ref,
    keep_ref, send_ref, sums_ref, turned, matrix,
):
    turned[...] = jnp.transpose(normed_ref[...])
    for tap, ref in enumerate((query_grad_ref, key_grad_ref, value_grad_ref)):
        scatter_pieces(place_ref, nn(turned[...], ref[...]), tap, keep_ref, send_ref, matrix)
    turned[...] = jnp.transpose(attended_ref[...])
    scatter_pieces(place_ref, nn(turned[...], cotangent_ref[...]), 3, keep_ref, send_ref, matrix)
    total = [
        jnp.sum(ref[...].astype(F32), axis=0, keepdims=True)
        for ref in (query_grad_ref, value_grad_ref, cotangent_ref)
    ]
    sums_ref[...] = rows_of(*total)


def weight_grad_kernel(
    with_cotangent, place_ref, side_ref, x_ref, x_near, x_cross, stats_ref, near_ref, cross_ref, pair_ref,
    g_ref, g_near, g_cross, g_pair, g_stats, rows_ref, act_ref, mask_ref, *rest,
):
    if with_cotangent:
        cot_ref, cot_edges, matrix_keep, matrix_send = rest[0], rest[1:5], rest[5], rest[6]
        keep_ref, send_ref, shifted, sums_ref, own_ref, frame, turned, matrix = rest[7:]
    else:
        keep_ref, send_ref, shifted, sums_ref, frame, turned, matrix = rest
    row = pl.program_id(0)
    pixels, channels = x_ref.shape

    @pl.when(row == 0)
    def _():
        mean, inverse = joined_stats(stats_ref[...], near_ref[...], cross_ref[...], pair_ref[...], pixels)
        mean_h, mean_hx = joined_sums(g_stats[...], g_near[...], g_cross[...], g_pair[...], pixels)
        gain = rows_ref[0:1, :]
        side = side_ref[0]

        def back(grad, values):
            hat = (values - mean) * inverse
            return inverse * (grad * gain - mean_h - hat * mean_hx)

        def pick(near, cross):
            return jnp.where(side == 0, cross, near), jnp.where(side == 0, near, cross)

        g_above, g_below = pick(g_near[0:32, :], g_cross[0:32, :])
        x_above, x_below = pick(x_near[0:32, :], x_cross[0:32, :])
        above, below = back(g_above, x_above), back(g_below, x_below)
        own = back(g_ref[...], x_ref[...])
        if with_cotangent:
            near_top, near_bottom, cross_top, cross_bottom = [ref[...].astype(F32) for ref in cot_edges]
            above = above + jnp.where(side == 0, cross_bottom, near_bottom)
            below = below + jnp.where(side == 0, near_top, cross_top)
            own = own + cot_ref[...].astype(F32)
            own_ref[...] = own
            for tap in range(4):
                keep_ref[:, :, 9 + tap] = matrix_keep[:, :, tap]
                send_ref[:, :, 9 + tap] = matrix_send[:, :, tap]
        sums_ref[...] = rows_of(jnp.sum(own, axis=0, keepdims=True))
        frame[0:8, :] = jnp.zeros((8, channels), F32)
        frame[8:40, :] = above
        frame[40 : 40 + pixels, :] = own
        frame[40 + pixels : 72 + pixels, :] = below
        frame[72 + pixels : 80 + pixels, :] = jnp.zeros((8, channels), F32)
        columns_of(frame, shifted, pixels + 64)
        turned[...] = jnp.transpose(act_ref[...])

    for b in range(3):
        block = shifted[b, pl.ds(pl.multiple_of(row * 32, 32), pixels), :]
        block = jnp.concatenate(masked(block, mask_ref[b]), axis=1)
        product = nn(turned[...], block)
        scatter_pieces(place_ref, product, 8 - row * 3 - b, keep_ref, send_ref, matrix)


def conv_back_kernel(
    side_ref, shifted, mask_ref, weight_ref, x_ref, stats_ref, near_ref, cross_ref, pair_ref, rows_ref,
    out_ref, near_out, cross_out, stats_out, sums_out,
):
    row = pl.program_id(0)
    pixels, channels = x_ref.shape

    @pl.when(row == 0)
    def _():
        out_ref[...] = jnp.zeros_like(out_ref)

    weight = jnp.concatenate([weight_ref[2 - b] for b in range(3)], axis=1)
    for i in range(pixels // 256):
        taps = jnp.concatenate(tap_rows(shifted, mask_ref, i * 256, 256, row), axis=1)
        out_ref[i * 256 : (i + 1) * 256, :] += nt(taps, weight)

    @pl.when(row == 2)
    def _():
        mean, inverse = joined_stats(stats_ref[...], near_ref[...], cross_ref[...], pair_ref[...], pixels)
        gain, shift = rows_ref[0:1, :], rows_ref[1:2, :]
        hat = (x_ref[...].astype(F32) - mean) * inverse
        pre = hat * gain + shift
        gate = sigmoid(pre)
        upstream = out_ref[...] * (gate * (1.0 + pre * (1.0 - gate)))
        out_ref[...] = upstream
        sums, groups = norm_back_sums(upstream, hat, gain)
        sums_out[...] = sums
        stats_out[...] = groups
        edges_out(side_ref, out_ref, near_out, cross_out, groups)


def last_kernel(
    g_ref, g_near, g_cross, g_pair, g_stats, x_ref, stats_ref, near_ref, cross_ref, pair_ref, rows_ref, add_ref,
    bias_one, bias_two, sums_one, sums_two, sums_three, matrix_sums, out_ref, small_ref,
):
    pixels = x_ref.shape[0]
    small_ref[...] = jnp.zeros_like(small_ref)
    parts = [bias_one[0:1], bias_two[0:1]]
    parts += [ref[i : i + 1] for i in range(2) for ref in (sums_one, sums_two, sums_three)]
    parts += [matrix_sums[i : i + 1] for i in range(3)]
    for i, part in enumerate(parts):
        small_ref[i : i + 1, :] = part
    mean, inverse = joined_stats(stats_ref[...], near_ref[...], cross_ref[...], pair_ref[...], pixels)
    mean_h, mean_hx = joined_sums(g_stats[...], g_near[...], g_cross[...], g_pair[...], pixels)
    hat = (x_ref[...].astype(F32) - mean) * inverse
    grad = inverse * (g_ref[...] * rows_ref[0:1, :] - mean_h - hat * mean_hx)
    out_ref[...] = (add_ref[...] + grad).astype(BF16)


def unpack_kernel(place_ref, own_ref, other_ref, *rest):
    out_ref = rest[-1]
    height, half = own_ref.shape[3], own_ref.shape[4]
    for tap in range(out_ref.shape[0]):
        for q in range(PIECES):
            pieces = own_ref if q < PIECES // 2 else other_ref
            for stream in range(2):
                start = pl.multiple_of((q ^ place_ref[stream]) * height, height)
                values = pieces[stream, q % (PIECES // 2), tap].astype(F32)
                out_ref[tap, pl.ds(start, height), stream * half : (stream + 1) * half] = values


def body(
    image,
    tile_map,
    out_grad,
    conv_weight,
    conv_bias,
    norm_gain,
    norm_shift,
    qk_weight,
    value_weight,
    proj_weight,
    qv_bias,
    proj_bias,
):
    band, width, channels = image.shape[1], image.shape[2], image.shape[3]
    pixels = band * width
    lanes = lax.axis_size("batch")
    devices = 4 * lanes

    def turned(flat):
        s, b = flat // lanes, flat % lanes
        core, high = b % 2, s // 2
        return (core * 2 + s % 2) * lanes + (b - core + high)

    def xored(flat, bits):
        return flat ^ bits

    def permute(x, to):
        return lax.ppermute(x, ("seq", "batch"), [(i, to(i)) for i in range(devices)])

    near_bit, pair_bit = lanes, 1

    def to_near(i):
        return i ^ near_bit

    def to_pair(i):
        return i ^ pair_bit

    def to_cross(i):
        return i ^ (near_bit | pair_bit)

    def meet(near, cross, stats):
        return permute(near, to_near), permute(cross, to_cross), permute(stats, to_pair)

    seq, lane = lax.axis_index("seq"), lax.axis_index("batch")
    core, low, high = lane % 2, seq % 2, seq // 2
    side = low.astype(jnp.int32).reshape(1)
    spot = jnp.stack([low, ((low == 0) & (core == 0)), ((low == 1) & (core == 1))]).astype(jnp.int32)
    x_bit, y_bit = (lane // 2) % 2, (lane // 4) % 2
    tail = low * 2 + high
    place = jnp.stack(
        [core * 16 + x_bit * 8 + y_bit * 4 + tail, core * 16 + y_bit * 8 + x_bit * 4 + tail]
    ).astype(jnp.int32)

    def block8(*rows):
        rows = [r.astype(F32).reshape(1, channels) for r in rows]
        return jnp.concatenate(rows + [jnp.zeros((8 - len(rows), channels), F32)], axis=0)

    norm_rows = [block8(norm_gain[i], norm_shift[i], conv_bias[min(i, 1)]) for i in range(3)]
    bias_rows = block8(qv_bias[0], qv_bias[1], proj_bias, jnp.zeros((channels,), F32))

    row_f32 = shape((40, channels), F32)
    stat_f32 = shape((8, channels), F32)
    field_f32 = shape((pixels, channels), F32)
    field_b16 = shape((pixels, channels), BF16)
    field = whole(pixels, channels)
    edge = whole(40, channels)
    stat = whole(8, channels)

    def call(kernel, name, operands, in_specs, outs, mib, flops=0, scratch=(), grid=(1,), after=(), aliases=None):
        count = len(operands)

        def run(*refs):
            kernel(*refs[:count], *refs[count + len(after) :])

        moved = sum(o.size * o.dtype.itemsize for o in operands) + sum(o.size * o.dtype.itemsize for _, o in outs)
        return pl.pallas_call(
            run if after else kernel,
            in_specs=list(in_specs) + [pl.BlockSpec(memory_space=pl.ANY)] * len(after),
            out_specs=[spec for spec, _ in outs],
            out_shape=[out for _, out in outs],
            scratch_shapes=list(scratch),
            grid=grid,
            input_output_aliases=aliases or {},
            compiler_params=params(mib),
            cost_estimate=pl.CostEstimate(flops=int(flops), bytes_accessed=int(moved), transcendentals=0),
            name=name,
        )(*operands, *after)

    def behind(x, *deps):
        return lax.optimization_barrier((x,) + deps)[0]

    row_out, stat_out = (edge, row_f32), (stat, stat_f32)
    matmul = 2.0 * pixels * channels * channels

    image_flat = image.reshape(pixels, channels)
    cot_flat = out_grad.reshape(pixels, channels)
    tiles = tile_map.astype(F32).reshape(2, pixels // 2)
    x = permute(image_flat, turned)
    near0, cross0, stats0 = call(
        first_kernel, "first", (image_flat, tiles, side), [field, whole(2, pixels // 2), SMEM],
        [row_out, row_out, stat_out], 16,
    )
    own0 = permute(stats0, turned)
    pair0 = permute(stats0, lambda i: to_pair(turned(i)))
    near0 = permute(near0, lambda i: to_near(turned(i)))
    cross0 = permute(cross0, lambda i: to_cross(turned(i)))
    masks, column_tiles, row_tiles = call(
        mask_kernel, "masks", (spot, own0, near0, cross0, pair0), [SMEM, stat, edge, edge, stat],
        [
            (whole(9, pixels, 128), shape((9, pixels, 128), BF16)),
            (whole(pixels, 128), shape((pixels, 128), F32)),
            (whole(1, 4 * pixels), shape((1, 4 * pixels), F32)),
        ],
        24, scratch=[pltpu.VMEM((pixels + 80, 128), F32)],
    )

    half = pixels // 2
    cot_first = permute(behind(cot_flat[:half], x), turned)

    mask_block = pl.BlockSpec((3, pixels, 128), lambda i: (i, 0, 0))

    def conv(x, met, stats, rows, index, skip, name, after=()):
        near, cross, pair = met
        specs = [
            SMEM, field, edge, edge, stat, stat, stat, mask_block,
            pl.BlockSpec((None, 1, 3, channels, channels), lambda i: (index, i, 0, 0, 0)),
        ]
        operands = [side, x, near, cross, pair, stats, rows, masks, conv_weight]
        kernel = conv_kernel
        if skip is None:

            def kernel(*refs):
                return conv_kernel(*refs[:9], None, *refs[9:])
        else:
            specs.append(field)
            operands.append(skip)
        return call(
            kernel, name, operands, specs,
            [(field, field_f32), (field, field_b16), row_out, row_out, stat_out],
            40, 9 * matmul,
            [pltpu.VMEM((pixels + 80, channels), F32), pltpu.VMEM((3, pixels + 64, channels), BF16)],
            (3,), after,
        )

    met0 = (near0, cross0, pair0)
    middle, act_one, near1, cross1, stats1 = conv(x, met0, own0, norm_rows[0], 0, None, "conv_one")
    met1 = meet(near1, cross1, stats1)
    cot_second = permute(behind(cot_flat[half:], cot_first, met1[0]), turned)
    residual, act_two, near2, cross2, stats2 = conv(
        middle, met1, stats1, norm_rows[1], 1, x, "conv_two", (cot_first,)
    )
    met2 = meet(near2, cross2, stats2)

    (normed,) = call(
        normed_kernel, "normed", (residual, *met2, stats2, norm_rows[2]), [field, edge, edge, stat, stat, stat],
        [(field, field_b16)], 16, after=(cot_second,),
    )
    cotangent = jnp.concatenate([cot_first, cot_second], axis=0)

    normed_near = permute(normed, to_near)
    normed_pair = permute(normed, to_pair)

    block = 512
    anywhere = pl.BlockSpec(memory_space=pl.ANY)
    blocks = pixels // block
    totals_out = (whole(blocks, 8, block), shape((blocks, 8, block), F32))
    square = whole(channels, channels)
    two_fields, two_b16 = whole(2 * pixels, channels), shape((2 * pixels, channels), BF16)
    cot_pair = permute(cotangent, to_pair)
    keys, values, queries, grads = call(
        early_kernel, "early",
        (normed, normed_pair, cotangent, cot_pair, qk_weight, value_weight, proj_weight, bias_rows),
        [field] * 4 + [whole(2, channels, channels), square, square, stat],
        [(two_fields, two_b16)] * 4, 32, 8 * matmul,
    )
    normed_cross = permute(behind(normed_near, keys), to_pair)
    cot_near = permute(behind(cotangent, normed_near), to_near)
    attended, query_grad, totals = call(
        attend_kernel, "attend",
        (normed_near, normed_cross, keys, values, queries, grads, qk_weight, value_weight, bias_rows,
         column_tiles, row_tiles),
        [field] * 2 + [two_fields] * 2 + [field] * 2
        + [whole(2, channels, channels), square, stat, whole(pixels, 128), whole(1, 4 * pixels)],
        [(field, field_b16), (field, field_b16), totals_out],
        58, 4 * matmul + 4 * 4 * matmul * pixels / channels,
        [pltpu.VMEM((2 * pixels, channels), BF16)] * 2,
    )

    totals_pair, totals_near, totals_cross = (permute(totals, to) for to in (to_pair, to_near, to_cross))
    cot_cross = permute(behind(cot_near, attended), to_pair)
    (output,) = call(
        out_kernel, "output", (attended, residual, proj_weight, block8(proj_bias)), [field, field, square, stat],
        [(field, field_b16)], 16, matmul, after=(cot_near,),
    )
    output_there = permute(output, turned)

    key_grad, value_grad, normed_grad, near3, cross3, stats3, sums3 = call(
        key_kernel, "key_value_grad",
        (side, keys, values, queries, grads, normed_near, normed_cross, cot_near, cot_cross,
         query_grad, qk_weight, value_weight, proj_weight, bias_rows,
         totals, totals_pair, totals_near, totals_cross, column_tiles, row_tiles.reshape(4 * blocks, 1, block),
         residual, stats2, *met2, norm_rows[2]),
        [SMEM] + [field] * 2 + [two_fields] * 2 + [anywhere] * 5 + [whole(2, channels, channels), square, square, stat]
        + [totals_out[0]] * 4
        + [whole(pixels, 128), whole(4 * blocks, 1, block), anywhere, stat, edge, edge, stat, stat],
        [(field, field_b16), (field, field_b16), (field, field_f32), row_out, row_out, stat_out, stat_out],
        60, 7 * matmul + 4 * 4 * matmul * pixels / channels,
        [pltpu.VMEM((pixels, channels), F32)] * 2
        + [
            pltpu.VMEM((4, pixels, channels), BF16), pltpu.VMEM((pixels, channels), BF16),
            pltpu.VMEM((pixels, channels), F32), pltpu.SemaphoreType.DMA((6,)),
        ],
        after=(output,),
    )
    met3 = meet(near3, cross3, stats3)

    def pieces(taps):
        dims = (2, PIECES // 2, taps, channels // PIECES, channels // 2)
        return [(whole(*dims), shape(dims, BF16))] * 2

    matrix_keep, matrix_send, matrix_sums = call(
        matrix_kernel, "matrix_grad", (place, normed, query_grad, key_grad, value_grad, attended, cotangent),
        [SMEM] + [field] * 6, pieces(4) + [stat_out], 32, 4 * matmul,
        [pltpu.VMEM((channels, pixels), BF16), pltpu.VMEM((channels, channels), BF16)],
    )

    def weight_grad(x, x_near, x_cross, stats, met, grad, grad_met, grad_stats, rows, act, cot, name, after=()):
        near, cross, pair = met
        g_near, g_cross, g_pair = grad_met
        spread = (3, pixels + 64, channels)
        extra, extra_in, extra_out = [], [], []
        if cot is not None:
            top = pl.BlockSpec((32, channels), lambda i: (0, 0))
            bottom = pl.BlockSpec((32, channels), lambda i: (pixels // 32 - 1, 0))
            extra = [cot, cot_near, cot_near, cot_cross, cot_cross, matrix_keep, matrix_send]
            extra_in = [field, top, bottom, top, bottom] + [spec for spec, _ in pieces(4)]
            extra_out = [(field, field_f32)]
        return call(
            functools.partial(weight_grad_kernel, cot is not None), name,
            [place, side, x, x_near, x_cross, stats, near, cross, pair, grad, g_near, g_cross, g_pair, grad_stats,
             rows, act, masks] + extra,
            [SMEM, SMEM, field, edge, edge, stat, edge, edge, stat, field, edge, edge, stat, stat, stat, field, mask_block]
            + extra_in,
            pieces(9 if cot is None else 13) + [(whole(*spread), shape(spread, BF16)), stat_out] + extra_out,
            58, 9 * matmul,
            [pltpu.VMEM((pixels + 80, channels), F32), pltpu.VMEM((channels, pixels), BF16), pltpu.VMEM((channels, channels), BF16)],
            (3,), after,
        )

    def conv_back(shifted, index, x, stats, met, rows, name, after=()):
        return call(
            conv_back_kernel, name, (side, shifted, masks, conv_weight, x, stats, *met, rows),
            [
                SMEM, whole(3, pixels + 64, channels), mask_block,
                pl.BlockSpec((None, None, 3, channels, channels), lambda i: (index, 2 - i, 0, 0, 0)),
                field, stat, edge, edge, stat, stat,
            ],
            [(field, field_f32), row_out, row_out, stat_out, stat_out],
            40, 9 * matmul, grid=(3,), after=after,
        )

    far_bit = 2 * lanes
    others = []
    bit = 8
    while bit < lanes:
        others.append(bit)
        bit *= 2

    def swap(x, bit):
        return permute(x, lambda i: i ^ bit)

    def added(left, right):
        return (left.astype(F32) + right.astype(F32)).astype(BF16)

    def halve(part, bit, *deps):
        count = part.shape[0] // 2
        return part[:count], swap(part[count:], bit)

    def split(keep, coming):
        total = added(keep, coming)
        return total[0], total[1]

    far_both = near_bit | far_bit

    def z_send(first, second):
        part = jnp.stack([first, second], axis=1)
        return part[0], swap(part[1], far_bit), swap(part[2], near_bit), swap(part[3], far_both)

    def z_sum(own, *coming):
        part = own.astype(F32)
        for other in coming:
            part = part + other.astype(F32)
        part = part.astype(BF16)
        for bit in others:
            part = added(part, swap(part, bit))
        return part

    def z_share(part):
        return part, swap(part, far_bit), swap(part, near_bit), swap(part, far_both)

    def z_join(*parts):
        part = jnp.stack(parts)
        return part[:, 0], part[:, 1]

    def both(first, second, first_bit, second_bit):
        return swap(first, first_bit), swap(second, second_bit)

    def tied(token, *values):
        return lax.optimization_barrier(values + (token,))[:-1]

    def unpack(parts, taps, at_once, start, slots, base, into, name):
        piece = pl.BlockSpec(
            (2, PIECES // 2, at_once, channels // PIECES, channels // 2), lambda i: (0, 0, start // at_once + i, 0, 0)
        )
        operands, specs = [place, *parts], [SMEM, piece, piece]
        if into is not None:
            operands, specs = operands + [into], specs + [anywhere]
        out_spec = pl.BlockSpec((at_once, channels, channels), lambda i: (base // at_once + i, 0, 0))
        (out,) = call(
            unpack_kernel, name, operands, specs, [(out_spec, shape((slots, channels, channels), F32))],
            32, grid=(taps // at_once,), aliases={} if into is None else {3: 0},
        )
        return out

    two_keep, two_send, shifted_two, bias_two, residual_grad = weight_grad(
        residual, met2[0], met2[1], stats2, met2, normed_grad, met3, stats3, norm_rows[2], act_two, cotangent,
        "weight_two_grad",
    )
    two_coming = swap(two_send, 1)
    grad_two, near4, cross4, stats4, sums4 = conv_back(
        shifted_two, 1, middle, stats1, met1, norm_rows[1], "conv_two_back"
    )
    met4 = meet(near4, cross4, stats4)
    two_first, two_second = split(two_keep, behind(two_coming, near4))
    two_first, two_second = halve(two_first, 2), halve(two_second, 4)
    one_keep, one_send, shifted_one, bias_one = weight_grad(
        middle, met1[0], met1[1], stats1, met1, grad_two, met4, stats4, norm_rows[1], act_one, None,
        "weight_one_grad", (output_there,),
    )
    one_coming = swap(behind(one_send, two_first[1], two_second[1]), 1)
    two_first = added(two_first[0], behind(two_first[1], shifted_one))
    two_second = added(two_second[0], behind(two_second[1], shifted_one))
    two_first, two_second = halve(two_first, 4), halve(two_second, 2)
    grad_one, near5, cross5, stats5, sums5 = conv_back(
        shifted_one, 0, x, own0, met0, norm_rows[0], "conv_one_back"
    )
    one_first, one_second = split(one_keep, behind(one_coming, near5))
    token = one_first
    one_first, one_second = halve(one_first, 2), halve(one_second, 4)
    met5 = meet(*tied(token, near5, cross5, stats5))

    two_coming = tied(token, two_first[1], two_second[1])
    two_first, two_second = added(two_first[0], two_coming[0]), added(two_second[0], two_coming[1])
    token = two_first
    two = z_send(two_first, two_second)

    small_rows = shape((16, channels), F32)
    image_grad, small = call(
        last_kernel, "image_grad",
        (grad_one, *met5, stats5, x, own0, *met0, norm_rows[0], residual_grad,
         bias_one, bias_two, sums5, sums4, sums3, matrix_sums),
        [field, edge, edge, stat, stat, field, stat, edge, edge, stat, stat, field] + [stat] * 6,
        [(field, field_b16), (whole(16, channels), small_rows)], 32, after=(token,),
    )
    small = small + swap(small, 1)

    one_coming = tied(small, one_first[1], one_second[1])
    one_first, one_second = added(one_first[0], one_coming[0]), added(one_second[0], one_coming[1])
    token = one_first
    one_first, one_second = halve(one_first, 4), halve(one_second, 2)

    two = z_sum(*tied(token, *two))
    token = two
    two = z_share(two)

    one_coming = tied(token, one_first[1], one_second[1])
    one_first, one_second = added(one_first[0], one_coming[0]), added(one_second[0], one_coming[1])
    token = one_first
    one = z_send(one_first, one_second)

    (small,) = tied(token, small)
    bit = 2
    while bit < near_bit:
        small = small + swap(small, bit)
        bit *= 2

    two_first, two_second = z_join(*tied(small, *two))
    token = two_first
    two_coming = both(two_first, two_second, 4, 2)

    one = z_sum(*tied(token, *one))
    token = one
    one = z_share(one)

    two_coming = tied(token, *two_coming)
    two_first, two_second = jnp.concatenate([two_first, two_coming[0]]), jnp.concatenate([two_second, two_coming[1]])
    token = two_first
    two_coming = both(two_first, two_second, 2, 4)

    (small,) = tied(token, small)
    bit = near_bit
    while bit < devices:
        small = small + swap(small, bit)
        bit *= 2

    one_first, one_second = z_join(*tied(small, *one))
    token = one_first
    one_coming = both(one_first, one_second, 4, 2)
    (image_grad,) = tied(token, image_grad)
    image_there = permute(image_grad, turned)

    two_coming = tied(token, *two_coming)
    two = jnp.stack([jnp.concatenate([two_first, two_coming[0]]), jnp.concatenate([two_second, two_coming[1]])])
    token = two
    two = two, swap(two, 1)

    one_coming = tied(token, *one_coming)
    one_first, one_second = jnp.concatenate([one_first, one_coming[0]]), jnp.concatenate([one_second, one_coming[1]])
    token = one_first
    one_coming = both(one_first, one_second, 2, 4)

    two = tied(token, *two)
    weights = unpack(two, 9, 3, 0, 18, 9, None, "unpack_two")
    qk_grad = unpack(two, 2, 1, 9, 2, 0, None, "unpack_qk")
    value_grad_sum = unpack(two, 1, 1, 11, 1, 0, None, "unpack_value")
    proj_grad = unpack(two, 1, 1, 12, 1, 0, None, "unpack_proj")

    one_coming = tied(weights, *one_coming)
    one_coming = tied(image_there, *one_coming)
    one = jnp.stack([jnp.concatenate([one_first, one_coming[0]]), jnp.concatenate([one_second, one_coming[1]])])
    one = one, swap(one, 1)
    weights = unpack(one, 9, 3, 0, 18, 0, weights, "unpack_one")

    return (
        output_there.reshape(1, band, width, channels),
        image_there.reshape(1, band, width, channels),
        weights.reshape(2, 3, 3, channels, channels),
        small[0:2],
        small[2:5],
        small[5:8],
        qk_grad,
        value_grad_sum[0],
        proj_grad[0],
        small[8:10],
        small[10],
    )


def solution(mesh):
    split = P("batch", "seq", None, None)
    in_specs = (split, P("batch", "seq", None), split) + (P(),) * 9
    out_specs = (split, split) + (P(),) * 9
    return jax.shard_map(body, mesh=mesh, in_specs=in_specs, out_specs=out_specs, check_vma=False)
```

time: 555 us -> 418 us (0.75)
  waiting for transfers between devices: 187 us -> 111 us
  starting transfers between devices: 126 us -> 91.4 us
  Pallas kernels: 178 us -> 163 us
    ppermute x99 -> x70, waiting for transfers between devices: 187 us -> 111 us  [permute(): lax.ppermute(x, ('seq', 'batch'), [(i, to(i)) for i in range(devices)])]
    ppermute x99 -> x70, starting transfers between devices: 126 us -> 91.4 us  [permute(): lax.ppermute(x, ('seq', 'batch'), [(i, to(i)) for i in range(devices)])]
    pallas_call x19 -> x20, Pallas kernels: 178 us -> 163 us  [call(): pl.pallas_call(run if after else kernel, in_specs=list(in_specs) + [pl.Bl...]
    unnamed x190 -> x145, local copies, waits for them, and re-layouts: 27.2 us -> 29.5 us
  transfers between devices with their start and end apart: 99 -> 70, of which waited for: 51 -> 33; matrix products, arithmetic and copies ran while one was open for 5% -> 3% of each run, Pallas kernels for 23% -> 26%
where the time goes in v2:
time: 418 us; the launch traced here: 412 us
  Pallas kernels  163 us (39%)
  waiting for transfers between devices  111 us (27%)
  starting transfers between devices  91.4 us (22%)
  local copies, waits for them, and re-layouts  36 us (9%)
  other arithmetic  9.34 us (2%)
    pallas_call x20, Pallas kernels, call(): pl.pallas_call(run if after else kernel, in_specs=list(in_specs) + [pl.Bl...  163 us
    ppermute x70, waiting for transfers between devices, permute(): lax.ppermute(x, ('seq', 'batch'), [(i, to(i)) for i in range(devices)])  111 us
    ppermute x70, starting transfers between devices, permute(): lax.ppermute(x, ('seq', 'batch'), [(i, to(i)) for i in range(devices)])  91.4 us
    unnamed x145, local copies, waits for them, and re-layouts  29.5 us
  transfers between devices with their start and end apart: 70, of which 33 were waited for; matrix products, arithmetic and copies ran while one was open for 3% of the time, Pallas kernels for 26%

profile of v2, /device:TPU:0, one launch (start us, length us, event | category | flops | bytes accessed | tf_op | source)
XLA Modules:
  0.0 412.2 jit_solution(8221789365737301244)
XLA Ops:
  4.5 5.5 %collective-permute-start.3 = (f32[8,512]{1,0:T(8,128)S(1)}, f32[8,512]{1,0:T(8,128)S(1)}, u32[]{:S(2)}, u32[]{:S(2)}) collective-permute-start(f32[8,512]{1,0:T(8,128)S(1)} %get-tuple-element.117), channel_id=1, source_target_pairs={{0,1},{1,17},{2,3},{3,19},{4,5},{5,21},{6,7},{7,23},{8,9},{9,25},{... | collective-permute-start | bytes 49160 | tf_op jit(solution)/shard_map/ppermute | solution.py:535
  17.9 13.1 %collective-permute-done.2.cross_ref.refs_3_.refs_8_ = f32[40,512]{1,0:T(8,128)S(1)} collective-permute-done((f32[40,512]{1,0:T(8,128)S(1)}, f32[40,512]{1,0:T(8,128)S(1)}, u32[]{:S(2)}, u32[]{:S(2)}) %collective-permute-start.2) | collective-permute-done | bytes 81952 | tf_op jit(solution)/shard_map/ppermute | solution.py:535
  33.6 10.5 %conv_one.1 = (f32[1024,512]{1,0:T(8,128)S(1)}, bf16[1024,512]{1,0:T(8,128)(2,1)S(1)}, f32[40,512]{1,0:T(8,128)S(1)}, f32[40,512]{1,0:T(8,128)S(1)}, f32[8,512]{1,0:T(8,128)S(1)}) custom-call(s32[1]{0:T(128)} %bitcast.side_ref.refs_0_.refs_1_, bf16[1024,512]{1,0:T(8,128)(2,1)S(1)} %collective-permute-done.refs_1_.refs_9_.x_ref.refs_5_, ...), custom_call_target="tpu_custom_call" | custom-call | flops 4831838208 | bytes 16384004 | tf_op jit(solution)/shard_map/conv_one/pallas_call | solution.py:583
  45.1 11.7 %collective-permute-start.5 = (f32[40,512]{1,0:T(8,128)S(1)}, f32[40,512]{1,0:T(8,128)S(1)}, u32[]{:S(2)}, u32[]{:S(2)}) collective-permute-start(f32[40,512]{1,0:T(8,128)S(1)} %get-tuple-element.120), channel_id=1, source_target_pairs={{0,8},{1,9},{2,10},{3,11},{4,12},{5,13},{6,14},{7,15},{8,0},{9,1},... | collective-permute-start | bytes 245768 | tf_op jit(solution)/shard_map/ppermute | solution.py:535
  62.2 10.3 %conv_two.1 = (f32[1024,512]{1,0:T(8,128)S(1)}, bf16[1024,512]{1,0:T(8,128)(2,1)S(1)}, f32[40,512]{1,0:T(8,128)S(1)}, f32[40,512]{1,0:T(8,128)S(1)}, f32[8,512]{1,0:T(8,128)S(1)}) custom-call(s32[1]{0:T(128)} %bitcast.side_ref.refs_0_.refs_1_, f32[1024,512]{1,0:T(8,128)S(1)} %get-tuple-element.119.refs_1_.x_ref.refs_2_, ...), custom_call_target="tpu_custom_call" | custom-call | flops 4831838208 | bytes 18481156 | tf_op jit(solution)/shard_map/conv_two/pallas_call | solution.py:583
  89.2 6.7 %early.1 = (bf16[2048,512]{1,0:T(8,128)(2,1)S(1)}, bf16[2048,512]{1,0:T(8,128)(2,1)S(1)}, bf16[2048,512]{1,0:T(8,128)(2,1)S(1)}, bf16[2048,512]{1,0:T(8,128)(2,1)S(1)}) custom-call(bf16[1024,512]{1,0:T(8,128)(2,1)} %normed.1.own_ref.normed_ref, bf16[1024,512]{1,0:T(8,128)(2,1)} %collective-permute-done.14.pair_ref, ...), custom_call_target="tpu_custom_call" | custom-call | flops 4294967296 | bytes 14696448 | tf_op jit(solution)/shard_map/early/pallas_call | solution.py:583
  101.3 7.5 %collective-permute-done.13.near_ref.refs_5_ = bf16[1024,512]{1,0:T(8,128)(2,1)} collective-permute-done((bf16[1024,512]{1,0:T(8,128)(2,1)}, bf16[1024,512]{1,0:T(8,128)(2,1)}, u32[]{:S(2)}, u32[]{:S(2)}) %collective-permute-start.13) | collective-permute-done | bytes 1048608 | tf_op jit(solution)/shard_map/ppermute | solution.py:535
  112.6 29.0 %attend.1 = (bf16[1024,512]{1,0:T(8,128)(2,1)}, bf16[1024,512]{1,0:T(8,128)(2,1)}, f32[2,8,512]{2,1,0:T(8,128)}) custom-call(bf16[1024,512]{1,0:T(8,128)(2,1)} %collective-permute-done.13.near_ref.refs_5_, bf16[1024,512]{1,0:T(8,128)(2,1)} %copy-done.61, bf16[2048,512]{1,0:T(8,128)(2,1)} %copy-done.49, bf16[2048,512]{1,0:T(8,128)(2,1)} %copy-done.50, ...), custom_call_target="tpu_custom_call" | custom-call | flops 19327352832 | bytes 14745600 | tf_op jit(solution)/shard_map/attend/pallas_call | solution.py:583
  148.6 30.1 %key_value_grad.1 = (bf16[1024,512]{1,0:T(8,128)(2,1)}, bf16[1024,512]{1,0:T(8,128)(2,1)}, f32[1024,512]{1,0:T(8,128)}, f32[40,512]{1,0:T(8,128)}, f32[40,512]{1...) custom-call(s32[1]{0:T(128)} %bitcast.side_ref.refs_0_.refs_1_, bf16[2048,512]{1,0:T(8,128)(2,1)} %copy-done.49, ...), custom_call_target="tpu_custom_call" | custom-call | flops 20937965568 | bytes 23117828 | tf_op jit(solution)/shard_map/key_value_grad/pallas_call | solution.py:583
  190.2 17.2 %weight_two_grad.1 = (bf16[2,16,13,16,256]{4,3,2,1,0:T(8,128)(2,1)}, bf16[2,16,13,16,256]{4,3,2,1,0:T(8,128)(2,1)}, bf16[3,1088,512]{2,1,0:T(8,128)(2,1)}, f32[8,512]{1,0:T(8,128)}, f32[1024,512]{1,0:T(8,128)}) custom-call(s32[2]{0:T(128)} %copy-done.19, s32[1]{0:T(128)} %bitcast.side_ref.refs_0_.refs_1_, f32[1024,512]{1,0:T(8,128)} %copy-done, ...), custom_call_target="tpu_custom_call" | custom-call | flops 4831838208 | bytes 27787276 | tf_op jit(solution)/shard_map/weight_two_grad/pallas_call | solution.py:583
  212.6 9.8 %conv_two_back.1 = (f32[1024,512]{1,0:T(8,128)S(1)}, f32[40,512]{1,0:T(8,128)S(1)}, f32[40,512]{1,0:T(8,128)S(1)}, f32[8,512]{1,0:T(8,128)S(1)}, f32[8,512]{1,0:T(8,128)S(1)}) custom-call(s32[1]{0:T(128)} %bitcast.side_ref.refs_0_.refs_1_, bf16[3,1088,512]{2,1,0:T(8,128)(2,1)S(1)} %copy-done.37, bf16[9,1024,128]{2,1,0:T(8,128)(2,1)S(1)} %copy-done.22, ...), custom_call_target="tpu_custom_call" | custom-call | flops 4831838208 | bytes 19742724 | tf_op jit(solution)/shard_map/conv_two_back/pallas_call | solution.py:583
  230.8 5.8 %collective-permute-start.28 = (f32[8,512]{1,0:T(8,128)S(1)}, f32[8,512]{1,0:T(8,128)S(1)}, u32[]{:S(2)}, u32[]{:S(2)}) collective-permute-start(f32[8,512]{1,0:T(8,128)S(1)} %get-tuple-element.154.refs_13_), channel_id=1, source_target_pairs={{0,1},{1,0},{2,3},{3,2},{4,5},{5,4},{6,7},{7,6},{8,9},{9,8},{10,11... | collective-permute-start | bytes 49160 | tf_op jit(solution)/shard_map/ppermute | solution.py:535
  240.8 14.4 %weight_one_grad.1 = (bf16[2,16,9,16,256]{4,3,2,1,0:T(8,128)(2,1)}, bf16[2,16,9,16,256]{4,3,2,1,0:T(8,128)(2,1)}, bf16[3,1088,512]{2,1,0:T(8,128)(2,1)}, f32[8,512]{1,0:T(8,128)}) custom-call(s32[2]{0:T(128)} %copy-done.19, s32[1]{0:T(128)} %bitcast.side_ref.refs_0_.refs_1_, f32[1024,512]{1,0:T(8,128)} %copy-done.38, f32[40,512]{1,0:T(8,128)} %copy-done.27, ...), custom_call_target="tpu_custom_call" | custom-call | flops 4831838208 | bytes 16252940 | tf_op jit(solution)/shard_map/weight_one_grad/pallas_call | solution.py:583
  257.4 9.8 %conv_one_back.1 = (f32[1024,512]{1,0:T(8,128)S(1)}, f32[40,512]{1,0:T(8,128)S(1)}, f32[40,512]{1,0:T(8,128)S(1)}, f32[8,512]{1,0:T(8,128)S(1)}, f32[8,512]{1,0:T(8,128)S(1)}) custom-call(s32[1]{0:T(128)} %bitcast.side_ref.refs_0_.refs_1_, bf16[3,1088,512]{2,1,0:T(8,128)(2,1)S(1)} %copy-done.41, bf16[9,1024,128]{2,1,0:T(8,128)(2,1)S(1)} %copy-done.23, ...), custom_call_target="tpu_custom_call" | custom-call | flops 4831838208 | bytes 18694148 | tf_op jit(solution)/shard_map/conv_one_back/pallas_call | solution.py:583
  273.1 8.2 %collective-permute-done.36 = bf16[4,13,16,256]{3,2,1,0:T(8,128)(2,1)S(1)} collective-permute-done((bf16[4,13,16,256]{3,2,1,0:T(8,128)(2,1)S(1)}, bf16[4,13,16,256]{3,2,1,0:T(8,128)(2,1)S(1)}, u32[]{:S(2)}, u32[]{:S(2)}) %collective-permute-start.36) | collective-permute-done | bytes 426016 | tf_op jit(solution)/shard_map/ppermute | solution.py:535
  294.6 5.3 %collective-permute-done.39 = bf16[8,9,16,256]{3,2,1,0:T(8,128)(2,1)S(1)} collective-permute-done((bf16[8,9,16,256]{3,2,1,0:T(8,128)(2,1)S(1)}, bf16[8,9,16,256]{3,2,1,0:T(8,128)(2,1)S(1)}, u32[]{:S(2)}, u32[]{:S(2)}) %collective-permute-start.39) | collective-permute-done | bytes 589856 | tf_op jit(solution)/shard_map/ppermute | solution.py:535
  303.6 7.2 %collective-permute-done.43 = bf16[2,13,16,256]{3,2,1,0:T(8,128)(2,1)S(1)} collective-permute-done((bf16[2,13,16,256]{3,2,1,0:T(8,128)(2,1)S(1)}, bf16[2,13,16,256]{3,2,1,0:T(8,128)(2,1)S(1)}, u32[]{:S(2)}, u32[]{:S(2)}) %collective-permute-start.43) | collective-permute-done | bytes 213024 | tf_op jit(solution)/shard_map/ppermute | solution.py:535
  322.7 5.7 %collective-permute-done.50 = bf16[2,13,16,256]{3,2,1,0:T(8,128)(2,1)S(1)} collective-permute-done((bf16[2,13,16,256]{3,2,1,0:T(8,128)(2,1)S(1)}, bf16[2,13,16,256]{3,2,1,0:T(8,128)(2,1)S(1)}, u32[]{:S(2)}, u32[]{:S(2)}) %collective-permute-start.50) | collective-permute-done | bytes 213024 | tf_op jit(solution)/shard_map/ppermute | solution.py:535
  340.5 5.4 %collective-permute-done.46 = bf16[2,9,16,256]{3,2,1,0:T(8,128)(2,1)S(1)} collective-permute-done((bf16[2,9,16,256]{3,2,1,0:T(8,128)(2,1)S(1)}, bf16[2,9,16,256]{3,2,1,0:T(8,128)(2,1)S(1)}, u32[]{:S(2)}, u32[]{:S(2)}) %collective-permute-start.46) | collective-permute-done | bytes 147488 | tf_op jit(solution)/shard_map/ppermute | solution.py:535
  362.3 5.7 %collective-permute-done.54 = bf16[2,9,16,256]{3,2,1,0:T(8,128)(2,1)S(1)} collective-permute-done((bf16[2,9,16,256]{3,2,1,0:T(8,128)(2,1)S(1)}, bf16[2,9,16,256]{3,2,1,0:T(8,128)(2,1)S(1)}, u32[]{:S(2)}, u32[]{:S(2)}) %collective-permute-start.54) | collective-permute-done | bytes 147488 | tf_op jit(solution)/shard_map/ppermute | solution.py:535
  370.9 7.5 %collective-permute-done.63 = bf16[4,9,16,256]{3,2,1,0:T(8,128)(2,1)S(1)} collective-permute-done((bf16[4,9,16,256]{3,2,1,0:T(8,128)(2,1)S(1)}, bf16[4,9,16,256]{3,2,1,0:T(8,128)(2,1)S(1)}, u32[]{:S(2)}, u32[]{:S(2)}) %collective-permute-start.63) | collective-permute-done | bytes 294944 | tf_op jit(solution)/shard_map/ppermute | solution.py:535
  380.8 4.7 %unpack_two.1.rest_0_ = f32[18,512,512]{2,1,0:T(8,128)} custom-call(s32[2]{0:T(128)S(1)} %copy-done.20, bf16[2,16,13,16,256]{4,3,2,1,0:T(8,128)(2,1)S(1)} %pad_maximum_fusion.own_ref, bf16[2,16,13,16,256]{4,3,2,1,0:T(8,128)(2,1)S(1)} %collective-permute-done.68.other_ref), custom_call_target="tpu_custom_call" | custom-call | bytes 25690120 | tf_op jit(solution)/shard_map/unpack_two/pallas_call | solution.py:583
  385.4 8.0 %collective-permute-done.67 = bf16[8,9,16,256]{3,2,1,0:T(8,128)(2,1)S(1)} collective-permute-done((bf16[8,9,16,256]{3,2,1,0:T(8,128)(2,1)S(1)}, bf16[8,9,16,256]{3,2,1,0:T(8,128)(2,1)S(1)}, u32[]{:S(2)}, u32[]{:S(2)}) %collective-permute-start.67) | collective-permute-done | bytes 589856 | tf_op jit(solution)/shard_map/ppermute | solution.py:535
  405.2 4.7 %unpack_one.1 = f32[18,512,512]{2,1,0:T(8,128)} custom-call(s32[2]{0:T(128)S(1)} %copy-done.20, bf16[2,16,9,16,256]{4,3,2,1,0:T(8,128)(2,1)S(1)} %pad_maximum_fusion.1.own_ref, bf16[2,16,9,16,256]{4,3,2,1,0:T(8,128)(2,1)S(1)} %collective-permute-done.69.other_ref, f32[18,512,512]{2,1,0:T(8,128)} %unpack_two.1.rest_0_), custom_call_target="tpu_custom_call", output_to_operand_aliasing={{}: (3, {})} | custom-call | bytes 42467336 | tf_op jit(solution)/shard_map/unpack_one/pallas_call | solution.py:583
  (338 shorter events, 166.3 us)
Async XLA Ops:
  10.0 22.9 %collective-permute-start = (bf16[1024,512]{1,0:T(8,128)(2,1)}, bf16[1024,512]{1,0:T(8,128)(2,1)S(1)}, u32[]{:S(2)}, u32[]{:S(2)}) collective-permute-start(bf16[1024,512]{1,0:T(8,128)(2,1)} %bitcast.1.image_ref), channel_id=1, source_target_pairs={{0,0},{1,16},{2,2},{3,18},{4,4},{5,20},{6,6},{7,22},{8,8},{9,24},{... | collective-permute-start | bytes 3145736 | tf_op jit(solution)/shard_map/ppermute | solution.py:535
  13.4 17.6 %collective-permute-start.2 = (f32[40,512]{1,0:T(8,128)S(1)}, f32[40,512]{1,0:T(8,128)S(1)}, u32[]{:S(2)}, u32[]{:S(2)}) collective-permute-start(f32[40,512]{1,0:T(8,128)S(1)} %get-tuple-element.116), channel_id=1, source_target_pairs={{0,9},{1,25},{2,11},{3,27},{4,13},{5,29},{6,15},{7,31},{8,1},{9,17... | collective-permute-start | bytes 245768 | tf_op jit(solution)/shard_map/ppermute | solution.py:535
  32.9 26.7 %collective-permute-start.8 = (bf16[512,512]{1,0:T(8,128)(2,1)S(1)}, bf16[512,512]{1,0:T(8,128)(2,1)S(1)}, u32[]{:S(2)}, u32[]{:S(2)}) collective-permute-start(bf16[512,512]{1,0:T(8,128)(2,1)S(1)} %bitcast.119), channel_id=1, source_target_pairs={{0,0},{1,16},{2,2},{3,18},{4,4},{5,20},{6,6},{7,22},{8,8},{9,24},{... | collective-permute-start | bytes 1572872 | tf_op jit(solution)/shard_map/ppermute | solution.py:535
  45.1 14.5 %collective-permute-start.5 = (f32[40,512]{1,0:T(8,128)S(1)}, f32[40,512]{1,0:T(8,128)S(1)}, u32[]{:S(2)}, u32[]{:S(2)}) collective-permute-start(f32[40,512]{1,0:T(8,128)S(1)} %get-tuple-element.120), channel_id=1, source_target_pairs={{0,8},{1,9},{2,10},{3,11},{4,12},{5,13},{6,14},{7,15},{8,0},{9,1},... | collective-permute-start | bytes 245768 | tf_op jit(solution)/shard_map/ppermute | solution.py:535
  59.6 18.1 %collective-permute-start.12 = (bf16[512,512]{1,0:T(8,128)(2,1)S(1)}, bf16[512,512]{1,0:T(8,128)(2,1)S(1)}, u32[]{:S(2)}, u32[]{:S(2)}) collective-permute-start(bf16[512,512]{1,0:T(8,128)(2,1)S(1)} %bitcast.118), channel_id=1, source_target_pairs={{0,0},{1,16},{2,2},{3,18},{4,4},{5,20},{6,6},{7,22},{8,8},{9,24},{... | collective-permute-start | bytes 1572872 | tf_op jit(solution)/shard_map/ppermute | solution.py:535
  83.0 25.8 %collective-permute-start.13 = (bf16[1024,512]{1,0:T(8,128)(2,1)}, bf16[1024,512]{1,0:T(8,128)(2,1)}, u32[]{:S(2)}, u32[]{:S(2)}) collective-permute-start(bf16[1024,512]{1,0:T(8,128)(2,1)} %normed.1.own_ref.normed_ref), channel_id=1, source_target_pairs={{0,8},{1,9},{2,10},{3,11},{4,12},{5,13},{6,14},{7,15},{8,0},{9,1},... | collective-permute-start | bytes 3145736 | tf_op jit(solution)/shard_map/ppermute | solution.py:535
  108.8 32.9 %collective-permute-start.17 = (bf16[1024,512]{1,0:T(8,128)(2,1)}, bf16[1024,512]{1,0:T(8,128)(2,1)}, u32[]{:S(2)}, u32[]{:S(2)}) collective-permute-start(bf16[1024,512]{1,0:T(8,128)(2,1)} %constant_dynamic-update-slice_fusion.cot_own.cotangent_ref.rest_0_), channel_id=1, source_target_pairs={{0,8},{1,9},{2,10},{3,11},{4,12},{5,13},{6,14},{7,15},{8,0},{9,1},... | collective-permute-start | bytes 3145736 | tf_op jit(solution)/shard_map/ppermute | solution.py:535
  207.4 14.9 %collective-permute-start.29 = (bf16[2,16,13,16,256]{4,3,2,1,0:T(8,128)(2,1)}, bf16[2,16,13,16,256]{4,3,2,1,0:T(8,128)(2,1)S(1)}, u32[]{:S(2)}, u32[]{:S(2)}) collective-permute-start(bf16[2,16,13,16,256]{4,3,2,1,0:T(8,128)(2,1)} %get-tuple-element.164), channel_id=1, source_target_pairs={{0,1},{1,0},{2,3},{3,2},{4,5},{5,4},{6,7},{7,6},{8,9},{9,8},{10,11... | collective-permute-start | bytes 10223624 | tf_op jit(solution)/shard_map/ppermute | solution.py:535
  208.2 22.6 %collective-permute-start.18 = (bf16[1024,512]{1,0:T(8,128)(2,1)S(1)}, bf16[1024,512]{1,0:T(8,128)(2,1)S(1)}, u32[]{:S(2)}, u32[]{:S(2)}) collective-permute-start(bf16[1024,512]{1,0:T(8,128)(2,1)S(1)} %copy-done.5), channel_id=1, source_target_pairs={{0,0},{1,16},{2,2},{3,18},{4,4},{5,20},{6,6},{7,22},{8,8},{9,24},{... | collective-permute-start | bytes 3145736 | tf_op jit(solution)/shard_map/ppermute | solution.py:535
  225.1 30.1 %collective-permute-start.31 = (bf16[8,13,16,256]{3,2,1,0:T(8,128)(2,1)}, bf16[8,13,16,256]{3,2,1,0:T(8,128)(2,1)S(1)}, u32[]{:S(2)}, u32[]{:S(2)}) collective-permute-start(bf16[8,13,16,256]{3,2,1,0:T(8,128)(2,1)} %get-tuple-element.221), channel_id=1, source_target_pairs={{0,4},{1,5},{2,6},{3,7},{4,0},{5,1},{6,2},{7,3},{8,12},{9,13},{10,... | collective-permute-start | bytes 2555912 | tf_op jit(solution)/shard_map/ppermute | solution.py:535
  226.6 28.6 %collective-permute-start.30 = (bf16[8,13,16,256]{3,2,1,0:T(8,128)(2,1)}, bf16[8,13,16,256]{3,2,1,0:T(8,128)(2,1)}, u32[]{:S(2)}, u32[]{:S(2)}) collective-permute-start(bf16[8,13,16,256]{3,2,1,0:T(8,128)(2,1)} %get-tuple-element.222), channel_id=1, source_target_pairs={{0,2},{1,3},{2,0},{3,1},{4,6},{5,7},{6,4},{7,5},{8,10},{9,11},{10,... | collective-permute-start | bytes 2555912 | tf_op jit(solution)/shard_map/ppermute | solution.py:535
  255.2 17.0 %collective-permute-start.32 = (bf16[2,16,9,16,256]{4,3,2,1,0:T(8,128)(2,1)}, bf16[2,16,9,16,256]{4,3,2,1,0:T(8,128)(2,1)S(1)}, u32[]{:S(2)}, u32[]{:S(2)}) collective-permute-start(bf16[2,16,9,16,256]{4,3,2,1,0:T(8,128)(2,1)} %get-tuple-element.166), channel_id=1, source_target_pairs={{0,1},{1,0},{2,3},{3,2},{4,5},{5,4},{6,7},{7,6},{8,9},{9,8},{10,11... | collective-permute-start | bytes 7077896 | tf_op jit(solution)/shard_map/ppermute | solution.py:535
  284.4 15.5 %collective-permute-start.39 = (bf16[8,9,16,256]{3,2,1,0:T(8,128)(2,1)S(1)}, bf16[8,9,16,256]{3,2,1,0:T(8,128)(2,1)S(1)}, u32[]{:S(2)}, u32[]{:S(2)}) collective-permute-start(bf16[8,9,16,256]{3,2,1,0:T(8,128)(2,1)S(1)} %get-tuple-element.225), channel_id=1, source_target_pairs={{0,4},{1,5},{2,6},{3,7},{4,0},{5,1},{6,2},{7,3},{8,12},{9,13},{10,... | collective-permute-start | bytes 1769480 | tf_op jit(solution)/shard_map/ppermute | solution.py:535
  284.9 15.2 %collective-permute-start.38 = (bf16[8,9,16,256]{3,2,1,0:T(8,128)(2,1)S(1)}, bf16[8,9,16,256]{3,2,1,0:T(8,128)(2,1)S(1)}, u32[]{:S(2)}, u32[]{:S(2)}) collective-permute-start(bf16[8,9,16,256]{3,2,1,0:T(8,128)(2,1)S(1)} %get-tuple-element.226), channel_id=1, source_target_pairs={{0,2},{1,3},{2,0},{3,1},{4,6},{5,7},{6,4},{7,5},{8,10},{9,11},{10,... | collective-permute-start | bytes 1769480 | tf_op jit(solution)/shard_map/ppermute | solution.py:535
  291.2 19.7 %collective-permute-start.43 = (bf16[2,13,16,256]{3,2,1,0:T(8,128)(2,1)S(1)}, bf16[2,13,16,256]{3,2,1,0:T(8,128)(2,1)S(1)}, u32[]{:S(2)}, u32[]{:S(2)}) collective-permute-start(bf16[2,13,16,256]{3,2,1,0:T(8,128)(2,1)S(1)} %get-tuple-element.233), channel_id=1, source_target_pairs={{0,16},{1,17},{2,18},{3,19},{4,20},{5,21},{6,22},{7,23},{8,24},{9,... | collective-permute-start | bytes 638984 | tf_op jit(solution)/shard_map/ppermute | solution.py:535
  291.9 18.9 %collective-permute-start.44 = (bf16[2,13,16,256]{3,2,1,0:T(8,128)(2,1)S(1)}, bf16[2,13,16,256]{3,2,1,0:T(8,128)(2,1)S(1)}, u32[]{:S(2)}, u32[]{:S(2)}) collective-permute-start(bf16[2,13,16,256]{3,2,1,0:T(8,128)(2,1)S(1)} %get-tuple-element.234), channel_id=1, source_target_pairs={{0,8},{1,9},{2,10},{3,11},{4,12},{5,13},{6,14},{7,15},{8,0},{9,1},... | collective-permute-start | bytes 638984 | tf_op jit(solution)/shard_map/ppermute | solution.py:535
  313.8 14.6 %collective-permute-start.50 = (bf16[2,13,16,256]{3,2,1,0:T(8,128)(2,1)S(1)}, bf16[2,13,16,256]{3,2,1,0:T(8,128)(2,1)S(1)}, u32[]{:S(2)}, u32[]{:S(2)}) collective-permute-start(bf16[2,13,16,256]{3,2,1,0:T(8,128)(2,1)S(1)} %add_convert_fusion.6), channel_id=1, source_target_pairs={{0,8},{1,9},{2,10},{3,11},{4,12},{5,13},{6,14},{7,15},{8,0},{9,1},... | collective-permute-start | bytes 638984 | tf_op jit(solution)/shard_map/ppermute | solution.py:535
  313.8 16.6 %collective-permute-start.49 = (bf16[2,13,16,256]{3,2,1,0:T(8,128)(2,1)S(1)}, bf16[2,13,16,256]{3,2,1,0:T(8,128)(2,1)S(1)}, u32[]{:S(2)}, u32[]{:S(2)}) collective-permute-start(bf16[2,13,16,256]{3,2,1,0:T(8,128)(2,1)S(1)} %add_convert_fusion.6), channel_id=1, source_target_pairs={{0,16},{1,17},{2,18},{3,19},{4,20},{5,21},{6,22},{7,23},{8,24},{9,... | collective-permute-start | bytes 638984 | tf_op jit(solution)/shard_map/ppermute | solution.py:535
  330.6 15.3 %collective-permute-start.58 = (bf16[4,13,16,256]{3,2,1,0:T(8,128)(2,1)S(1)}, bf16[4,13,16,256]{3,2,1,0:T(8,128)(2,1)S(1)}, u32[]{:S(2)}, u32[]{:S(2)}) collective-permute-start(bf16[4,13,16,256]{3,2,1,0:T(8,128)(2,1)S(1)} %get-tuple-element.229), channel_id=1, source_target_pairs={{0,2},{1,3},{2,0},{3,1},{4,6},{5,7},{6,4},{7,5},{8,10},{9,11},{10,... | collective-permute-start | bytes 1277960 | tf_op jit(solution)/shard_map/ppermute | solution.py:535
  331.3 14.7 %collective-permute-start.57 = (bf16[4,13,16,256]{3,2,1,0:T(8,128)(2,1)S(1)}, bf16[4,13,16,256]{3,2,1,0:T(8,128)(2,1)S(1)}, u32[]{:S(2)}, u32[]{:S(2)}) collective-permute-start(bf16[4,13,16,256]{3,2,1,0:T(8,128)(2,1)S(1)} %get-tuple-element.230), channel_id=1, source_target_pairs={{0,4},{1,5},{2,6},{3,7},{4,0},{5,1},{6,2},{7,3},{8,12},{9,13},{10,... | collective-permute-start | bytes 1277960 | tf_op jit(solution)/shard_map/ppermute | solution.py:535
  346.2 21.9 %collective-permute-start.65 = (bf16[8,13,16,256]{3,2,1,0:T(8,128)(2,1)S(1)}, bf16[8,13,16,256]{3,2,1,0:T(8,128)(2,1)S(1)}, u32[]{:S(2)}, u32[]{:S(2)}) collective-permute-start(bf16[8,13,16,256]{3,2,1,0:T(8,128)(2,1)S(1)} %pad_maximum_fusion.4), channel_id=1, source_target_pairs={{0,4},{1,5},{2,6},{3,7},{4,0},{5,1},{6,2},{7,3},{8,12},{9,13},{10,... | collective-permute-start | bytes 2555912 | tf_op jit(solution)/shard_map/ppermute | solution.py:535
  347.8 20.4 %collective-permute-start.64 = (bf16[8,13,16,256]{3,2,1,0:T(8,128)(2,1)S(1)}, bf16[8,13,16,256]{3,2,1,0:T(8,128)(2,1)S(1)}, u32[]{:S(2)}, u32[]{:S(2)}) collective-permute-start(bf16[8,13,16,256]{3,2,1,0:T(8,128)(2,1)S(1)} %pad_maximum_fusion.3), channel_id=1, source_target_pairs={{0,2},{1,3},{2,0},{3,1},{4,6},{5,7},{6,4},{7,5},{8,10},{9,11},{10,... | collective-permute-start | bytes 2555912 | tf_op jit(solution)/shard_map/ppermute | solution.py:535
  370.1 23.6 %collective-permute-start.61 = (bf16[1024,512]{1,0:T(8,128)(2,1)S(1)}, bf16[1024,512]{1,0:T(8,128)(2,1)S(1)}, u32[]{:S(2)}, u32[]{:S(2)}) collective-permute-start(bf16[1024,512]{1,0:T(8,128)(2,1)S(1)} %get-tuple-element.207), channel_id=1, source_target_pairs={{0,0},{1,16},{2,2},{3,18},{4,4},{5,20},{6,6},{7,22},{8,8},{9,24},{... | collective-permute-start | bytes 3145736 | tf_op jit(solution)/shard_map/ppermute | solution.py:535
  378.8 14.6 %collective-permute-start.67 = (bf16[8,9,16,256]{3,2,1,0:T(8,128)(2,1)S(1)}, bf16[8,9,16,256]{3,2,1,0:T(8,128)(2,1)S(1)}, u32[]{:S(2)}, u32[]{:S(2)}) collective-permute-start(bf16[8,9,16,256]{3,2,1,0:T(8,128)(2,1)S(1)} %pad_maximum_fusion.7), channel_id=1, source_target_pairs={{0,4},{1,5},{2,6},{3,7},{4,0},{5,1},{6,2},{7,3},{8,12},{9,13},{10,... | collective-permute-start | bytes 1769480 | tf_op jit(solution)/shard_map/ppermute | solution.py:535
  (117 other events, 1177.4 us)

commit v3 on v2

--- a/solution.py
+++ b/solution.py
@@ -14,6 +14,11 @@
 BF16 = jnp.bfloat16
 MIB = 1024 * 1024
 PIECES = 32
+LIMITS = {
+    "conv_one": 46, "conv_two": 46, "weight_two_grad": 24, "weight_one_grad": 20, "conv_two_back": 36, "conv_one_back": 36,
+    "attend": 40, "key_value_grad": 60, "early": 14, "matrix_grad": 16, "unpack_two": 40, "unpack_one": 16,
+    "first": 8, "masks": 12, "normed": 8, "output": 8, "image_grad": 12,
+}
 
 
 def params(mib):
@@ -25,6 +30,7 @@
 
 
 SMEM = pl.BlockSpec(memory_space=pltpu.SMEM)
+IN_HBM = pl.BlockSpec(memory_space=pltpu.HBM)
 
 
 def whole(*dims):
@@ -114,6 +120,27 @@
         block = shifted[b, pl.ds(pl.multiple_of(row * 32 + start, 32), count), :]
         parts += masked(block, mask_ref[b, start : start + count, :])
     return parts
+
+
+def fetch_rows(weights, index, buffer, arrived, row, order):
+    copies = [
+        pltpu.make_async_copy(weights.at[index, r], buffer.at[r], arrived.at[r]) for r in order
+    ]
+
+    @pl.when(row == 0)
+    def _():
+        for copy in copies:
+            copy.start()
+
+    return copies
+
+
+def wait_row(copies, row):
+    for step, copy in enumerate(copies):
+
+        @pl.when(row == step)
+        def _(copy=copy):
+            copy.wait()
 
 
 def first_kernel(image_ref, tiles_ref, side_ref, near_ref, cross_ref, stats_ref):
@@ -160,11 +187,12 @@
 
 
 def conv_kernel(
-    side_ref, x_ref, near_ref, cross_ref, pair_ref, stats_ref, rows_ref, mask_ref, weight_ref, skip_ref,
-    out_ref, act_ref, near_out, cross_out, stats_out, frame, shifted,
+    index, side_ref, x_ref, near_ref, cross_ref, pair_ref, stats_ref, rows_ref, mask_ref, weights, skip_ref,
+    out_ref, act_ref, near_out, cross_out, stats_out, frame, shifted, buffer, arrived,
 ):
     row = pl.program_id(0)
     pixels, channels = x_ref.shape
+    copies = fetch_rows(weights, index, buffer, arrived, row, (0, 1, 2))
 
     @pl.when(row == 0)
     def _():
@@ -189,7 +217,8 @@
             start = start + skip_ref[...].astype(F32)
         out_ref[...] = start
 
-    weight = weight_ref[...].reshape(3 * channels, channels)
+    wait_row(copies, row)
+    weight = buffer[row].reshape(3 * channels, channels)
     for i in range(pixels // 256):
         taps = jnp.concatenate(tap_rows(shifted, mask_ref, i * 256, 256, row), axis=1)
         out_ref[i * 256 : (i + 1) * 256, :] += jnp.dot(taps, weight, preferred_element_type=F32)
@@ -216,22 +245,18 @@
     return lax.dot_general(left, right, (((1,), (1,)), ((), ())), preferred_element_type=F32)
 
 
-def early_kernel(
-    own_ref, pair_ref, cot_own, cot_pair, qk_ref, value_ref, proj_ref, bias_ref, keys_ref, values_ref, queries_ref, grads_ref
-):
-    pixels = own_ref.shape[0]
-    for i, (rows_ref, cot_ref) in enumerate(((own_ref, cot_own), (pair_ref, cot_pair))):
-        part = slice(i * pixels, (i + 1) * pixels)
+def early_kernel(own_ref, pair_ref, cot_own, cot_pair, qk_ref, value_ref, proj_ref, bias_ref, *outs):
+    for rows_ref, cot_ref, (keys, values, queries, grads) in ((own_ref, cot_own, outs[:4]), (pair_ref, cot_pair, outs[4:])):
         rows = rows_ref[...]
-        queries_ref[part, :] = (nn(rows, qk_ref[0]) + bias_ref[0:1, :]).astype(BF16)
-        keys_ref[part, :] = nn(rows, qk_ref[1]).astype(BF16)
-        values_ref[part, :] = (nn(rows, value_ref[...]) + bias_ref[1:2, :]).astype(BF16)
-        grads_ref[part, :] = nt(cot_ref[...], proj_ref[...]).astype(BF16)
+        queries[...] = (nn(rows, qk_ref[0]) + bias_ref[0:1, :]).astype(BF16)
+        keys[...] = nn(rows, qk_ref[1]).astype(BF16)
+        values[...] = (nn(rows, value_ref[...]) + bias_ref[1:2, :]).astype(BF16)
+        grads[...] = nt(cot_ref[...], proj_ref[...]).astype(BF16)
 
 
 def attend_kernel(
-    near_ref, cross_ref, keys_ref, values_ref, queries_ref, grads_ref, qk_ref, value_ref, bias_ref, column_ref, row_ref,
-    attended_ref, query_grad_ref, totals_ref, far_keys, far_values,
+    near_ref, cross_ref, keys_own, values_own, keys_pair, values_pair, queries_ref, grads_ref, qk_ref, value_ref,
+    bias_ref, column_ref, row_ref, attended_ref, query_grad_ref, totals_ref, far_keys, far_values,
 ):
     pixels, channels = near_ref.shape
     scale = channels ** (-0.5)
@@ -241,7 +266,11 @@
         far_keys[part, :] = nn(rows, qk_ref[1]).astype(BF16)
         far_values[part, :] = (nn(rows, value_ref[...]) + bias_ref[1:2, :]).astype(BF16)
     block = totals_ref.shape[2]
-    halves = ((keys_ref, values_ref, slice(0, 2 * pixels)), (far_keys, far_values, slice(2 * pixels, 4 * pixels)))
+    halves = (
+        (keys_own, values_own, slice(0, pixels)),
+        (keys_pair, values_pair, slice(pixels, 2 * pixels)),
+        (far_keys, far_values, slice(2 * pixels, 4 * pixels)),
+    )
 
     def step(i, carry):
         part = pl.ds(pl.multiple_of(i * block, block), block)
@@ -251,7 +280,7 @@
         for keys, _, span in halves:
             product = nt(queries, keys[...]) * scale
             scores.append(jnp.where(column == row_ref[:, span], product, MASKED_SCORE))
-        top = jnp.maximum(*[jnp.max(s, axis=1, keepdims=True) for s in scores])
+        top = functools.reduce(jnp.maximum, [jnp.max(s, axis=1, keepdims=True) for s in scores])
         weights = [jnp.exp(s - top) for s in scores]
         total = sum(jnp.sum(w, axis=1, keepdims=True) for w in weights)
         inverse = 1.0 / total
@@ -287,23 +316,22 @@
 
 
 def key_kernel(
-    side_ref, keys, values, queries_ref, grads_ref, near_hbm, cross_hbm, cot_near_hbm, cot_cross_hbm, query_grad_hbm,
-    qk_ref, value_ref, proj_ref, bias_ref,
+    side_ref, keys, values, queries_own, grads_own, queries_pair, grads_pair, near_hbm, cot_near_hbm, cross_hbm,
+    cot_cross_hbm, query_grad_hbm, qk_ref, value_ref, proj_ref, bias_ref,
     totals_own, totals_pair, totals_near, totals_cross, column_ref, row_ref,
     residual_hbm, stats_ref, near_ref, cross_ref, pair_ref, rows_ref,
     key_grad_ref, value_grad_ref, normed_grad_ref, near_out, cross_out, stats_out, sums_out,
-    key_sum, value_sum, far, query_grad_ref, residual_ref, arrived,
+    key_sum, value_sum, held, query_grad_ref, residual_ref, arrived,
 ):
     pixels, channels = keys.shape
     scale = channels ** (-0.5)
+    sources = (
+        queries_own, grads_own, queries_pair, grads_pair, near_hbm, cot_near_hbm, cross_hbm, cot_cross_hbm,
+        query_grad_hbm, residual_hbm,
+    )
+    targets = [held.at[i] for i in range(8)] + [query_grad_ref, residual_ref]
     coming = [
-        pltpu.make_async_copy(source, target, arrived.at[i])
-        for i, (source, target) in enumerate(
-            (
-                (near_hbm, far.at[0]), (cot_near_hbm, far.at[1]), (cross_hbm, far.at[2]), (cot_cross_hbm, far.at[3]),
-                (query_grad_hbm, query_grad_ref), (residual_hbm, residual_ref),
-            )
-        )
+        pltpu.make_async_copy(source, target, arrived.at[i]) for i, (source, target) in enumerate(zip(sources, targets))
     ]
     for copy in coming:
         copy.start()
@@ -321,28 +349,22 @@
         score_grad = (weights * (prob_grad - totals[i, 1:2, :])).astype(BF16)
         key_sum[...] += nn(score_grad, queries)
 
-    for group, totals in enumerate((totals_own, totals_pair)):
-
-        def step(i, carry, group=group, totals=totals):
-            part = pl.ds(pl.multiple_of(group * pixels + i * chunk, chunk), chunk)
-            add(queries_ref[part, :], grads_ref[part, :], totals, i, group * blocks + i)
-            return carry
-
-        lax.fori_loop(0, blocks, step, 0)
-    for group, totals in enumerate((totals_near, totals_cross)):
+    for group, totals in enumerate((totals_own, totals_pair, totals_near, totals_cross)):
         coming[2 * group].wait()
         coming[2 * group + 1].wait()
 
-        def far_step(i, carry, group=group, totals=totals):
+        def step(i, carry, group=group, totals=totals):
             part = pl.ds(pl.multiple_of(i * chunk, chunk), chunk)
-            queries = (nn(far[2 * group, part, :], qk_ref[0]) + bias_ref[0:1, :]).astype(BF16)
-            upstream = nt(far[2 * group + 1, part, :], proj_ref[...]).astype(BF16)
-            add(queries, upstream, totals, i, (group + 2) * blocks + i)
+            queries, upstream = held[2 * group, part, :], held[2 * group + 1, part, :]
+            if group >= 2:
+                queries = (nn(queries, qk_ref[0]) + bias_ref[0:1, :]).astype(BF16)
+                upstream = nt(upstream, proj_ref[...]).astype(BF16)
+            add(queries, upstream, totals, i, group * blocks + i)
             return carry
 
-        lax.fori_loop(0, blocks, far_step, 0)
-    coming[4].wait()
-    coming[5].wait()
+        lax.fori_loop(0, blocks, step, 0)
+    coming[8].wait()
+    coming[9].wait()
     key_grad = (key_sum[...] * scale).astype(BF16)
     value_grad = value_sum[...].astype(BF16)
     key_grad_ref[...] = key_grad
@@ -444,17 +466,19 @@
 
 
 def conv_back_kernel(
-    side_ref, shifted, mask_ref, weight_ref, x_ref, stats_ref, near_ref, cross_ref, pair_ref, rows_ref,
-    out_ref, near_out, cross_out, stats_out, sums_out,
+    index, side_ref, shifted, mask_ref, weights, x_ref, stats_ref, near_ref, cross_ref, pair_ref, rows_ref,
+    out_ref, near_out, cross_out, stats_out, sums_out, buffer, arrived,
 ):
     row = pl.program_id(0)
     pixels, channels = x_ref.shape
+    copies = fetch_rows(weights, index, buffer, arrived, row, (2, 1, 0))
 
     @pl.when(row == 0)
     def _():
         out_ref[...] = jnp.zeros_like(out_ref)
 
-    weight = jnp.concatenate([weight_ref[2 - b] for b in range(3)], axis=1)
+    wait_row(copies, row)
+    weight = jnp.concatenate([buffer[2 - row, 2 - b] for b in range(3)], axis=1)
     for i in range(pixels // 256):
         taps = jnp.concatenate(tap_rows(shifted, mask_ref, i * 256, 256, row), axis=1)
         out_ref[i * 256 : (i + 1) * 256, :] += nt(taps, weight)
@@ -479,12 +503,19 @@
     bias_one, bias_two, sums_one, sums_two, sums_three, matrix_sums, out_ref, small_ref,
 ):
     pixels = x_ref.shape[0]
-    small_ref[...] = jnp.zeros_like(small_ref)
+    half = x_ref.shape[1] // 2
     parts = [bias_one[0:1], bias_two[0:1]]
     parts += [ref[i : i + 1] for i in range(2) for ref in (sums_one, sums_two, sums_three)]
     parts += [matrix_sums[i : i + 1] for i in range(3)]
+    line = lax.broadcasted_iota(jnp.int32, (16, 2 * half), 0)
+    rows = jnp.zeros((16, 2 * half), F32)
     for i, part in enumerate(parts):
-        small_ref[i : i + 1, :] = part
+        rows = jnp.where(line == i, jnp.broadcast_to(part, rows.shape), rows)
+    high = rows.astype(BF16)
+    low = (rows - high.astype(F32)).astype(BF16)
+    for i, part in enumerate((high, low)):
+        small_ref[2 * i] = part[:, :half]
+        small_ref[2 * i + 1] = part[:, half:]
     mean, inverse = joined_stats(stats_ref[...], near_ref[...], cross_ref[...], pair_ref[...], pixels)
     mean_h, mean_hx = joined_sums(g_stats[...], g_near[...], g_cross[...], g_pair[...], pixels)
     hat = (x_ref[...].astype(F32) - mean) * inverse
@@ -502,6 +533,31 @@
                 start = pl.multiple_of((q ^ place_ref[stream]) * height, height)
                 values = pieces[stream, q % (PIECES // 2), tap].astype(F32)
                 out_ref[tap, pl.ds(start, height), stream * half : (stream + 1) * half] = values
+
+
+def spread_pieces(place_ref, halves, tap, out):
+    height, half = halves[0].shape[2], halves[0].shape[3]
+    for q in range(PIECES):
+        pieces = halves[q // (PIECES // 2)]
+        for stream in range(2):
+            start = pl.multiple_of((q ^ place_ref[stream]) * height, height)
+            values = pieces[q % (PIECES // 2), stream * 17 + tap].astype(F32)
+            out[pl.ds(start, height), stream * half : (stream + 1) * half] = values
+
+
+def unpack_two_kernel(place_ref, own_ref, other_ref, weights_ref, qk_ref, value_ref, proj_ref):
+    step = pl.program_id(0)
+    halves = (own_ref, other_ref)
+
+    @pl.when(step < 3)
+    def _():
+        for tap in range(3):
+            spread_pieces(place_ref, halves, step * 3 + tap, weights_ref.at[tap])
+
+    @pl.when(step == 3)
+    def _():
+        for tap, out in enumerate((qk_ref.at[0], qk_ref.at[1], value_ref, proj_ref)):
+            spread_pieces(place_ref, halves, 9 + tap, out)
 
 
 def body(
@@ -555,7 +611,7 @@
     x_bit, y_bit = (lane // 2) % 2, (lane // 4) % 2
     tail = low * 2 + high
     place = jnp.stack(
-        [core * 16 + x_bit * 8 + y_bit * 4 + tail, core * 16 + y_bit * 8 + x_bit * 4 + tail]
+        [core * 16 + x_bit * 8 + y_bit * 4 + tail, core * 16 + y_bit * 8 + x_bit * 4 + tail, tail]
     ).astype(jnp.int32)
 
     def block8(*rows):
@@ -588,7 +644,7 @@
             scratch_shapes=list(scratch),
             grid=grid,
             input_output_aliases=aliases or {},
-            compiler_params=params(mib),
+            compiler_params=params(LIMITS.get(name, mib)),
             cost_estimate=pl.CostEstimate(flops=int(flops), bytes_accessed=int(moved), transcendentals=0),
             name=name,
         )(*operands, *after)
@@ -626,18 +682,19 @@
 
     mask_block = pl.BlockSpec((3, pixels, 128), lambda i: (i, 0, 0))
 
+    row_buffer = [pltpu.VMEM((3, 3, channels, channels), BF16), pltpu.SemaphoreType.DMA((3,))]
+
     def conv(x, met, stats, rows, index, skip, name, after=()):
         near, cross, pair = met
         specs = [
-            SMEM, field, edge, edge, stat, stat, stat, mask_block,
-            pl.BlockSpec((None, 1, 3, channels, channels), lambda i: (index, i, 0, 0, 0)),
+            SMEM, field, edge, edge, stat, stat, stat, mask_block, IN_HBM,
         ]
         operands = [side, x, near, cross, pair, stats, rows, masks, conv_weight]
-        kernel = conv_kernel
+        kernel = functools.partial(conv_kernel, index)
         if skip is None:
 
             def kernel(*refs):
-                return conv_kernel(*refs[:9], None, *refs[9:])
+                return conv_kernel(index, *refs[:9], None, *refs[9:])
         else:
             specs.append(field)
             operands.append(skip)
@@ -645,14 +702,14 @@
             kernel, name, operands, specs,
             [(field, field_f32), (field, field_b16), row_out, row_out, stat_out],
             40, 9 * matmul,
-            [pltpu.VMEM((pixels + 80, channels), F32), pltpu.VMEM((3, pixels + 64, channels), BF16)],
+            [pltpu.VMEM((pixels + 80, channels), F32), pltpu.VMEM((3, pixels + 64, channels), BF16), *row_buffer],
             (3,), after,
         )
 
     met0 = (near0, cross0, pair0)
     middle, act_one, near1, cross1, stats1 = conv(x, met0, own0, norm_rows[0], 0, None, "conv_one")
     met1 = meet(near1, cross1, stats1)
-    cot_second = permute(behind(cot_flat[half:], cot_first, met1[0]), turned)
+    cot_second = permute(behind(cot_flat[half:], cot_first, met1[2]), turned)
     residual, act_two, near2, cross2, stats2 = conv(
         middle, met1, stats1, norm_rows[1], 1, x, "conv_two", (cot_first,)
     )
@@ -672,22 +729,20 @@
     blocks = pixels // block
     totals_out = (whole(blocks, 8, block), shape((blocks, 8, block), F32))
     square = whole(channels, channels)
-    two_fields, two_b16 = whole(2 * pixels, channels), shape((2 * pixels, channels), BF16)
     cot_pair = permute(cotangent, to_pair)
-    keys, values, queries, grads = call(
+    keys, values, queries, grads, keys_pair, values_pair, queries_pair, grads_pair = call(
         early_kernel, "early",
         (normed, normed_pair, cotangent, cot_pair, qk_weight, value_weight, proj_weight, bias_rows),
         [field] * 4 + [whole(2, channels, channels), square, square, stat],
-        [(two_fields, two_b16)] * 4, 32, 8 * matmul,
+        [(field, field_b16)] * 8, 32, 8 * matmul,
     )
     normed_cross = permute(behind(normed_near, keys), to_pair)
     cot_near = permute(behind(cotangent, normed_near), to_near)
     attended, query_grad, totals = call(
         attend_kernel, "attend",
-        (normed_near, normed_cross, keys, values, queries, grads, qk_weight, value_weight, bias_rows,
+        (normed_near, normed_cross, keys, values, keys_pair, values_pair, queries, grads, qk_weight, value_weight, bias_rows,
          column_tiles, row_tiles),
-        [field] * 2 + [two_fields] * 2 + [field] * 2
-        + [whole(2, channels, channels), square, stat, whole(pixels, 128), whole(1, 4 * pixels)],
+        [field] * 8 + [whole(2, channels, channels), square, stat, whole(pixels, 128), whole(1, 4 * pixels)],
         [(field, field_b16), (field, field_b16), totals_out],
         58, 4 * matmul + 4 * 4 * matmul * pixels / channels,
         [pltpu.VMEM((2 * pixels, channels), BF16)] * 2,
@@ -700,26 +755,25 @@
         [(field, field_b16)], 16, matmul, after=(cot_near,),
     )
     output_there = permute(output, turned)
-
     key_grad, value_grad, normed_grad, near3, cross3, stats3, sums3 = call(
         key_kernel, "key_value_grad",
-        (side, keys, values, queries, grads, normed_near, normed_cross, cot_near, cot_cross,
+        (side, keys, values, queries, grads, queries_pair, grads_pair, normed_near, cot_near, normed_cross, cot_cross,
          query_grad, qk_weight, value_weight, proj_weight, bias_rows,
          totals, totals_pair, totals_near, totals_cross, column_tiles, row_tiles.reshape(4 * blocks, 1, block),
          residual, stats2, *met2, norm_rows[2]),
-        [SMEM] + [field] * 2 + [two_fields] * 2 + [anywhere] * 5 + [whole(2, channels, channels), square, square, stat]
+        [SMEM] + [field] * 2 + [anywhere] * 9 + [whole(2, channels, channels), square, square, stat]
         + [totals_out[0]] * 4
         + [whole(pixels, 128), whole(4 * blocks, 1, block), anywhere, stat, edge, edge, stat, stat],
         [(field, field_b16), (field, field_b16), (field, field_f32), row_out, row_out, stat_out, stat_out],
         60, 7 * matmul + 4 * 4 * matmul * pixels / channels,
         [pltpu.VMEM((pixels, channels), F32)] * 2
         + [
-            pltpu.VMEM((4, pixels, channels), BF16), pltpu.VMEM((pixels, channels), BF16),
-            pltpu.VMEM((pixels, channels), F32), pltpu.SemaphoreType.DMA((6,)),
+            pltpu.VMEM((8, pixels, channels), BF16), pltpu.VMEM((pixels, channels), BF16),
+            pltpu.VMEM((pixels, channels), F32), pltpu.SemaphoreType.DMA((10,)),
         ],
-        after=(output,),
     )
     met3 = meet(near3, cross3, stats3)
+
 
     def pieces(taps):
         dims = (2, PIECES // 2, taps, channels // PIECES, channels // 2)
@@ -728,7 +782,7 @@
     matrix_keep, matrix_send, matrix_sums = call(
         matrix_kernel, "matrix_grad", (place, normed, query_grad, key_grad, value_grad, attended, cotangent),
         [SMEM] + [field] * 6, pieces(4) + [stat_out], 32, 4 * matmul,
-        [pltpu.VMEM((channels, pixels), BF16), pltpu.VMEM((channels, channels), BF16)],
+        [pltpu.VMEM((channels, pixels), BF16), pltpu.VMEM((channels, channels), BF16)], after=(output_there,),
     )
 
     def weight_grad(x, x_near, x_cross, stats, met, grad, grad_met, grad_stats, rows, act, cot, name, after=()):
@@ -756,14 +810,13 @@
 
     def conv_back(shifted, index, x, stats, met, rows, name, after=()):
         return call(
-            conv_back_kernel, name, (side, shifted, masks, conv_weight, x, stats, *met, rows),
+            functools.partial(conv_back_kernel, index), name, (side, shifted, masks, conv_weight, x, stats, *met, rows),
             [
-                SMEM, whole(3, pixels + 64, channels), mask_block,
-                pl.BlockSpec((None, None, 3, channels, channels), lambda i: (index, 2 - i, 0, 0, 0)),
+                SMEM, whole(3, pixels + 64, channels), mask_block, IN_HBM,
                 field, stat, edge, edge, stat, stat,
             ],
             [(field, field_f32), row_out, row_out, stat_out, stat_out],
-            40, 9 * matmul, grid=(3,), after=after,
+            40, 9 * matmul, row_buffer, (3,), after,
         )
 
     far_bit = 2 * lanes
@@ -842,100 +895,111 @@
     two_first, two_second = halve(two_first, 2), halve(two_second, 4)
     one_keep, one_send, shifted_one, bias_one = weight_grad(
         middle, met1[0], met1[1], stats1, met1, grad_two, met4, stats4, norm_rows[1], act_one, None,
-        "weight_one_grad", (output_there,),
-    )
+        "weight_one_grad",
+    )
+    def after_token(token, *values):
+        return lax.optimization_barrier(values + (token,))[:-1]
+
+    def add_halves(token, first, second):
+        one, two = after_token(token, first[1], second[1])
+        return added(first[0], one), added(second[0], two)
+
+    def join_halves(token, first, second, coming):
+        one, two = after_token(token, *coming)
+        return jnp.concatenate([first, one]), jnp.concatenate([second, two])
+
     one_coming = swap(behind(one_send, two_first[1], two_second[1]), 1)
-    two_first = added(two_first[0], behind(two_first[1], shifted_one))
-    two_second = added(two_second[0], behind(two_second[1], shifted_one))
+    two_first, two_second = add_halves(shifted_one, two_first, two_second)
+    token = two_first
     two_first, two_second = halve(two_first, 4), halve(two_second, 2)
     grad_one, near5, cross5, stats5, sums5 = conv_back(
-        shifted_one, 0, x, own0, met0, norm_rows[0], "conv_one_back"
-    )
-    one_first, one_second = split(one_keep, behind(one_coming, near5))
+        shifted_one, 0, x, own0, met0, norm_rows[0], "conv_one_back", (two_first[0], two_second[0])
+    )
+    met5 = meet(near5, cross5, stats5)
+
+    one_first, one_second = split(one_keep, *after_token(near5, one_coming))
     token = one_first
     one_first, one_second = halve(one_first, 2), halve(one_second, 4)
-    met5 = meet(*tied(token, near5, cross5, stats5))
-
-    two_coming = tied(token, two_first[1], two_second[1])
-    two_first, two_second = added(two_first[0], two_coming[0]), added(two_second[0], two_coming[1])
+
+    two_first, two_second = add_halves(token, two_first, two_second)
     token = two_first
     two = z_send(two_first, two_second)
 
-    small_rows = shape((16, channels), F32)
+    piece_dims = (channels // PIECES, channels // 2)
+    small_parts = shape((4,) + piece_dims, BF16)
     image_grad, small = call(
         last_kernel, "image_grad",
         (grad_one, *met5, stats5, x, own0, *met0, norm_rows[0], residual_grad,
          bias_one, bias_two, sums5, sums4, sums3, matrix_sums),
         [field, edge, edge, stat, stat, field, stat, edge, edge, stat, stat, field] + [stat] * 6,
-        [(field, field_b16), (whole(16, channels), small_rows)], 32, after=(token,),
-    )
-    small = small + swap(small, 1)
-
-    one_coming = tied(small, one_first[1], one_second[1])
-    one_first, one_second = added(one_first[0], one_coming[0]), added(one_second[0], one_coming[1])
+        [(field, field_b16), (whole(4, *piece_dims), small_parts)], 32, after=(token,),
+    )
+    for bit in others:
+        small = added(small, swap(small, bit))
+
+    one_first, one_second = add_halves(small, one_first, one_second)
     token = one_first
     one_first, one_second = halve(one_first, 4), halve(one_second, 2)
 
-    two = z_sum(*tied(token, *two))
+    two = z_sum(*after_token(token, *two))
     token = two
-    two = z_share(two)
-
-    one_coming = tied(token, one_first[1], one_second[1])
-    one_first, one_second = added(one_first[0], one_coming[0]), added(one_second[0], one_coming[1])
+    two = z_share(jnp.concatenate([two.reshape((-1,) + piece_dims), small]))
+
+    one_first, one_second = add_halves(token, one_first, one_second)
     token = one_first
     one = z_send(one_first, one_second)
 
-    (small,) = tied(token, small)
-    bit = 2
-    while bit < near_bit:
-        small = small + swap(small, bit)
-        bit *= 2
-
-    two_first, two_second = z_join(*tied(small, *two))
-    token = two_first
+    two = jnp.stack(after_token(token, *two))
+    token = two
+    two_first = jnp.concatenate([two[:, :13], two[:, 26:]], axis=1)
+    two_second = two[:, 13:26]
     two_coming = both(two_first, two_second, 4, 2)
 
-    one = z_sum(*tied(token, *one))
+    one = z_sum(*after_token(token, *one))
     token = one
     one = z_share(one)
 
-    two_coming = tied(token, *two_coming)
-    two_first, two_second = jnp.concatenate([two_first, two_coming[0]]), jnp.concatenate([two_second, two_coming[1]])
+    two_first, two_second = join_halves(token, two_first, two_second, two_coming)
     token = two_first
     two_coming = both(two_first, two_second, 2, 4)
 
-    (small,) = tied(token, small)
-    bit = near_bit
-    while bit < devices:
-        small = small + swap(small, bit)
-        bit *= 2
-
-    one_first, one_second = z_join(*tied(small, *one))
+    one_first, one_second = z_join(*after_token(token, *one))
     token = one_first
     one_coming = both(one_first, one_second, 4, 2)
-    (image_grad,) = tied(token, image_grad)
-    image_there = permute(image_grad, turned)
-
-    two_coming = tied(token, *two_coming)
-    two = jnp.stack([jnp.concatenate([two_first, two_coming[0]]), jnp.concatenate([two_second, two_coming[1]])])
+    image_there = permute(behind(image_grad, token), turned)
+
+    two = jnp.concatenate(join_halves(token, two_first, two_second, two_coming), axis=1)
     token = two
     two = two, swap(two, 1)
 
-    one_coming = tied(token, *one_coming)
-    one_first, one_second = jnp.concatenate([one_first, one_coming[0]]), jnp.concatenate([one_second, one_coming[1]])
+    one_first, one_second = join_halves(token, one_first, one_second, one_coming)
     token = one_first
     one_coming = both(one_first, one_second, 2, 4)
 
-    two = tied(token, *two)
-    weights = unpack(two, 9, 3, 0, 18, 9, None, "unpack_two")
-    qk_grad = unpack(two, 2, 1, 9, 2, 0, None, "unpack_qk")
-    value_grad_sum = unpack(two, 1, 1, 11, 1, 0, None, "unpack_value")
-    proj_grad = unpack(two, 1, 1, 12, 1, 0, None, "unpack_proj")
-
-    one_coming = tied(weights, *one_coming)
-    one_coming = tied(image_there, *one_coming)
-    one = jnp.stack([jnp.concatenate([one_first, one_coming[0]]), jnp.concatenate([one_second, one_coming[1]])])
+    two = after_token(token, *two)
+    weights, qk_grad, value_weight_grad, proj_weight_grad = call(
+        unpack_two_kernel, "unpack_two", (place, *two), [SMEM] + [whole(*two[0].shape)] * 2,
+        [
+            (
+                pl.BlockSpec((3, channels, channels), lambda i: (3 + jnp.minimum(i, 2), 0, 0)),
+                shape((18, channels, channels), F32),
+            ),
+            (whole(2, channels, channels), shape((2, channels, channels), F32)),
+            (square, shape((channels, channels), F32)),
+            (square, shape((channels, channels), F32)),
+        ],
+        40, grid=(4,),
+    )
+    small = jnp.stack(two)[:, :, 13:17].astype(F32)
+    small = jnp.sum(small.reshape((-1, 2, 2) + piece_dims), axis=(0, 1))
+    small = jnp.concatenate([small[0], small[1]], axis=1)
+    token = qk_grad
+
+    one = jnp.stack(join_halves(token, one_first, one_second, one_coming))
+    one, image_there = lax.optimization_barrier((one, image_there))
+    token = one
     one = one, swap(one, 1)
+
     weights = unpack(one, 9, 3, 0, 18, 0, weights, "unpack_one")
 
     return (
@@ -946,8 +1010,8 @@
         small[2:5],
         small[5:8],
         qk_grad,
-        value_grad_sum[0],
-        proj_grad[0],
+        value_weight_grad,
+        proj_weight_grad,
         small[8:10],
         small[10],
     )

time: 418 us -> 385 us (0.921)
  Pallas kernels: 163 us -> 144 us
  local copies, waits for them, and re-layouts: 36 us -> 21.4 us
  starting transfers between devices: 91.4 us -> 78.9 us
  waiting for transfers between devices: 111 us -> 118 us
    pallas_call x20 -> x17, Pallas kernels: 163 us -> 144 us  [call(): pl.pallas_call(run if after else kernel, in_specs=list(in_specs) + [pl.Bl...]
    ppermute x70 -> x65, starting transfers between devices: 91.4 us -> 78.9 us  [permute(): lax.ppermute(x, ('seq', 'batch'), [(i, to(i)) for i in range(devices)])]
    unnamed x145 -> x143, local copies, waits for them, and re-layouts: 29.5 us -> 18.6 us
    ppermute x70 -> x65, waiting for transfers between devices: 111 us -> 118 us  [permute(): lax.ppermute(x, ('seq', 'batch'), [(i, to(i)) for i in range(devices)])]
    concatenate x4 -> x10, other arithmetic: 0.26 us -> 6.22 us  [the longest x1 4.06 us: body(): jnp.concatenate(join_halves(token, two_first, two_second, two_coming), ax...]
  transfers between devices with their start and end apart: 70 -> 65, of which waited for: 33 -> 34; matrix products, arithmetic and copies ran while one was open for 3% -> 3% of each run, Pallas kernels for 26% -> 33%
where the time goes in v3:
time: 385 us; the launch traced here: 378 us
  Pallas kernels  144 us (37%)
  waiting for transfers between devices  118 us (31%)
  starting transfers between devices  78.9 us (20%)
  local copies, waits for them, and re-layouts  21.4 us (6%)
  other arithmetic  13 us (3%)
    pallas_call x17, Pallas kernels, call(): pl.pallas_call(run if after else kernel, in_specs=list(in_specs) + [pl.Bl...  144 us
    ppermute x65, waiting for transfers between devices, permute(): lax.ppermute(x, ('seq', 'batch'), [(i, to(i)) for i in range(devices)])  118 us
    ppermute x65, starting transfers between devices, permute(): lax.ppermute(x, ('seq', 'batch'), [(i, to(i)) for i in range(devices)])  78.9 us
    unnamed x143, local copies, waits for them, and re-layouts  18.6 us
  transfers between devices with their start and end apart: 65, of which 34 were waited for; matrix products, arithmetic and copies ran while one was open for 3% of the time, Pallas kernels for 33%

profile of v3, /device:TPU:0, one launch (start us, length us, event | category | flops | bytes accessed | tf_op | source)
XLA Modules:
  0.0 377.5 jit_solution(6156983686374566071)
XLA Ops:
  4.5 5.5 %collective-permute-start.3 = (f32[8,512]{1,0:T(8,128)S(1)}, f32[8,512]{1,0:T(8,128)S(1)}, u32[]{:S(2)}, u32[]{:S(2)}) collective-permute-start(f32[8,512]{1,0:T(8,128)S(1)} %get-tuple-element.120), channel_id=1, source_target_pairs={{0,1},{1,17},{2,3},{3,19},{4,5},{5,21},{6,7},{7,23},{8,9},{9,25},{... | collective-permute-start | bytes 49160 | tf_op jit(solution)/shard_map/ppermute | solution.py:591
  17.9 13.1 %collective-permute-done.2.cross_ref.refs_3_.refs_7_.refs_8_ = f32[40,512]{1,0:T(8,128)S(1)} collective-permute-done((f32[40,512]{1,0:T(8,128)S(1)}, f32[40,512]{1,0:T(8,128)S(1)}, u32[]{:S(2)}, u32[]{:S(2)}) %collective-permute-start.2) | collective-permute-done | bytes 81952 | tf_op jit(solution)/shard_map/ppermute | solution.py:591
  34.2 9.2 %conv_one.1 = (f32[1024,512]{1,0:T(8,128)S(1)}, bf16[1024,512]{1,0:T(8,128)(2,1)S(1)}, f32[40,512]{1,0:T(8,128)S(1)}, f32[40,512]{1,0:T(8,128)S(1)}, f32[8,512]{1,0:T(8,128)S(1)}) custom-call(s32[1]{0:T(128)} %bitcast.side_ref.refs_0_, bf16[1024,512]{1,0:T(8,128)(2,1)S(1)} %collective-permute-done.refs_1_.refs_9_.refs_4_.refs_5_, ...), custom_call_target="tpu_custom_call" | custom-call | flops 4831838208 | bytes 16384004 | tf_op jit(solution)/shard_map/conv_one/pallas_call | solution.py:639
  44.5 11.7 %collective-permute-start.5 = (f32[40,512]{1,0:T(8,128)S(1)}, f32[40,512]{1,0:T(8,128)S(1)}, u32[]{:S(2)}, u32[]{:S(2)}) collective-permute-start(f32[40,512]{1,0:T(8,128)S(1)} %get-tuple-element.123), channel_id=1, source_target_pairs={{0,8},{1,9},{2,10},{3,11},{4,12},{5,13},{6,14},{7,15},{8,0},{9,1},... | collective-permute-start | bytes 245768 | tf_op jit(solution)/shard_map/ppermute | solution.py:591
  62.4 10.1 %conv_two.1 = (f32[1024,512]{1,0:T(8,128)S(1)}, bf16[1024,512]{1,0:T(8,128)(2,1)S(1)}, f32[40,512]{1,0:T(8,128)S(1)}, f32[40,512]{1,0:T(8,128)S(1)}, f32[8,512]{1,0:T(8,128)S(1)}) custom-call(s32[1]{0:T(128)} %bitcast.side_ref.refs_0_, f32[1024,512]{1,0:T(8,128)S(1)} %get-tuple-element.122.refs_1_.x_ref, ...), custom_call_target="tpu_custom_call" | custom-call | flops 4831838208 | bytes 18481156 | tf_op jit(solution)/shard_map/conv_two/pallas_call | solution.py:639
  86.2 6.5 %early.1 = (bf16[1024,512]{1,0:T(8,128)(2,1)S(1)}, bf16[1024,512]{1,0:T(8,128)(2,1)S(1)}, bf16[1024,512]{1,0:T(8,128)(2,1)S(1)}, bf16[1024,512]{1,0:T(8,128)(2,1...) custom-call(bf16[1024,512]{1,0:T(8,128)(2,1)S(1)} %normed.1.own_ref., ...), custom_call_target="tpu_custom_call" | custom-call | flops 4294967296 | bytes 14696448 | tf_op jit(solution)/shard_map/early/pallas_call | solution.py:639
  94.7 11.0 %collective-permute-done.13.near_ref.near_hbm = bf16[1024,512]{1,0:T(8,128)(2,1)} collective-permute-done((bf16[1024,512]{1,0:T(8,128)(2,1)S(1)}, bf16[1024,512]{1,0:T(8,128)(2,1)}, u32[]{:S(2)}, u32[]{:S(2)}) %collective-permute-start.13) | collective-permute-done | bytes 1048608 | tf_op jit(solution)/shard_map/ppermute | solution.py:591
  108.7 26.1 %attend.1 = (bf16[1024,512]{1,0:T(8,128)(2,1)S(1)}, bf16[1024,512]{1,0:T(8,128)(2,1)S(1)}, f32[2,8,512]{2,1,0:T(8,128)}) custom-call(bf16[1024,512]{1,0:T(8,128)(2,1)} %collective-permute-done.13.near_ref.near_hbm, bf16[1024,512]{1,0:T(8,128)(2,1)S(1)} %collective-permute-done.16.cross_ref.cross_hbm, bf16[1024,512]{1,0:T(8,128)(2,1)S(1)} %get-tuple-element.132.keys_own.keys, ...), custom_call_target="tpu_custom_call" | custom-call | flops 19327352832 | bytes 12648448 | tf_op jit(solution)/shard_map/attend/pallas_call | solution.py:639
  144.3 30.3 %key_value_grad.1 = (bf16[1024,512]{1,0:T(8,128)(2,1)}, bf16[1024,512]{1,0:T(8,128)(2,1)}, f32[1024,512]{1,0:T(8,128)}, f32[40,512]{1,0:T(8,128)}, f32[40,512]{1...) custom-call(s32[1]{0:T(128)} %bitcast.side_ref.refs_0_, bf16[1024,512]{1,0:T(8,128)(2,1)} %copy-done.57, ...), custom_call_target="tpu_custom_call" | custom-call | flops 20937965568 | bytes 21020676 | tf_op jit(solution)/shard_map/key_value_grad/pallas_call | solution.py:639
  185.4 10.1 %weight_two_grad.1 = (bf16[2,16,13,16,256]{4,3,2,1,0:T(8,128)(2,1)S(1)}, bf16[2,16,13,16,256]{4,3,2,1,0:T(8,128)(2,1)S(1)}, bf16[3,1088,512]{2,1,0:T(8,128)(2,1)...) custom-call(s32[3]{0:T(128)S(1)} %pad_add_fusion.1.refs_0_.place_ref, s32[1]{0:T(128)} %bitcast.side_ref.refs_0_, ...), custom_call_target="tpu_custom_call" | custom-call | flops 4831838208 | bytes 27787280 | tf_op jit(solution)/shard_map/weight_two_grad/pallas_call | solution.py:639
  195.9 10.2 %conv_two_back.1 = (f32[1024,512]{1,0:T(8,128)S(1)}, f32[40,512]{1,0:T(8,128)S(1)}, f32[40,512]{1,0:T(8,128)S(1)}, f32[8,512]{1,0:T(8,128)S(1)}, f32[8,512]{1,0:T(8,128)S(1)}) custom-call(s32[1]{0:T(128)} %bitcast.side_ref.refs_0_, bf16[3,1088,512]{2,1,0:T(8,128)(2,1)S(1)} %get-tuple-element.157.shifted, bf16[9,1024,128]{2,1,0:T(8,128)(2,1)S(1)} %copy-done.27, ...), custom_call_target="tpu_custom_call" | custom-call | flops 4831838208 | bytes 19742724 | tf_op jit(solution)/shard_map/conv_two_back/pallas_call | solution.py:639
  217.0 8.6 %weight_one_grad.1 = (bf16[2,16,9,16,256]{4,3,2,1,0:T(8,128)(2,1)S(1)}, bf16[2,16,9,16,256]{4,3,2,1,0:T(8,128)(2,1)S(1)}, bf16[3,1088,512]{2,1,0:T(8,128)(2,1)S(1)}, f32[8,512]{1,0:T(8,128)S(1)}) custom-call(s32[3]{0:T(128)S(1)} %pad_add_fusion.1.refs_0_.place_ref, s32[1]{0:T(128)} %bitcast.side_ref.refs_0_, f32[1024,512]{1,0:T(8,128)S(1)} %copy-done.47, ...), custom_call_target="tpu_custom_call" | custom-call | flops 4831838208 | bytes 16252944 | tf_op jit(solution)/shard_map/weight_one_grad/pallas_call | solution.py:639
  232.5 10.2 %conv_one_back.1 = (f32[1024,512]{1,0:T(8,128)S(1)}, f32[40,512]{1,0:T(8,128)S(1)}, f32[40,512]{1,0:T(8,128)S(1)}, f32[8,512]{1,0:T(8,128)S(1)}, f32[8,512]{1,0:T(8,128)S(1)}) custom-call(s32[1]{0:T(128)} %bitcast.side_ref.refs_0_, bf16[3,1088,512]{2,1,0:T(8,128)(2,1)S(1)} %get-tuple-element.169.refs_1_, bf16[9,1024,128]{2,1,0:T(8,128)(2,1)S(1)} %copy-done.27, ...), custom_call_target="tpu_custom_call" | custom-call | flops 4831838208 | bytes 18694148 | tf_op jit(solution)/shard_map/conv_one_back/pallas_call | solution.py:639
  253.4 7.4 %collective-permute-done.34 = bf16[8,9,16,256]{3,2,1,0:T(8,128)(2,1)S(1)} collective-permute-done((bf16[8,9,16,256]{3,2,1,0:T(8,128)(2,1)S(1)}, bf16[8,9,16,256]{3,2,1,0:T(8,128)(2,1)S(1)}, u32[]{:S(2)}, u32[]{:S(2)}) %collective-permute-start.34) | collective-permute-done | bytes 589856 | tf_op jit(solution)/shard_map/ppermute | solution.py:591
  262.5 7.0 %collective-permute-done.42 = bf16[2,13,16,256]{3,2,1,0:T(8,128)(2,1)S(1)} collective-permute-done((bf16[2,13,16,256]{3,2,1,0:T(8,128)(2,1)S(1)}, bf16[2,13,16,256]{3,2,1,0:T(8,128)(2,1)S(1)}, u32[]{:S(2)}, u32[]{:S(2)}) %collective-permute-start.42) | collective-permute-done | bytes 213024 | tf_op jit(solution)/shard_map/ppermute | solution.py:591
  282.5 6.2 %collective-permute-done.49 = bf16[30,16,256]{2,1,0:T(8,128)(2,1)S(1)} collective-permute-done((bf16[30,16,256]{2,1,0:T(8,128)(2,1)S(1)}, bf16[30,16,256]{2,1,0:T(8,128)(2,1)S(1)}, u32[]{:S(2)}, u32[]{:S(2)}) %collective-permute-start.49) | collective-permute-done | bytes 245792 | tf_op jit(solution)/shard_map/ppermute | solution.py:591
  288.7 4.3 %collective-permute-done.48 = bf16[30,16,256]{2,1,0:T(8,128)(2,1)S(1)} collective-permute-done((bf16[30,16,256]{2,1,0:T(8,128)(2,1)S(1)}, bf16[30,16,256]{2,1,0:T(8,128)(2,1)S(1)}, u32[]{:S(2)}, u32[]{:S(2)}) %collective-permute-start.48) | collective-permute-done | bytes 245792 | tf_op jit(solution)/shard_map/ppermute | solution.py:591
  314.0 4.3 %collective-permute-done.53 = bf16[2,9,16,256]{3,2,1,0:T(8,128)(2,1)S(1)} collective-permute-done((bf16[2,9,16,256]{3,2,1,0:T(8,128)(2,1)S(1)}, bf16[2,9,16,256]{3,2,1,0:T(8,128)(2,1)S(1)}, u32[]{:S(2)}, u32[]{:S(2)}) %collective-permute-start.53) | collective-permute-done | bytes 147488 | tf_op jit(solution)/shard_map/ppermute | solution.py:591
  318.8 4.3 %collective-permute-done.51 = bf16[2,9,16,256]{3,2,1,0:T(8,128)(2,1)S(1)} collective-permute-done((bf16[2,9,16,256]{3,2,1,0:T(8,128)(2,1)S(1)}, bf16[2,9,16,256]{3,2,1,0:T(8,128)(2,1)S(1)}, u32[]{:S(2)}, u32[]{:S(2)}) %collective-permute-start.51) | collective-permute-done | bytes 147488 | tf_op jit(solution)/shard_map/ppermute | solution.py:591
  323.2 5.1 %collective-permute-done.59 = bf16[8,13,16,256]{3,2,1,0:T(8,128)(2,1)S(1)} collective-permute-done((bf16[8,13,16,256]{3,2,1,0:T(8,128)(2,1)S(1)}, bf16[8,13,16,256]{3,2,1,0:T(8,128)(2,1)S(1)}, u32[]{:S(2)}, u32[]{:S(2)}) %collective-permute-start.59) | collective-permute-done | bytes 852000 | tf_op jit(solution)/shard_map/ppermute | solution.py:591
  339.5 6.6 %collective-permute-done.57 = bf16[4,9,16,256]{3,2,1,0:T(8,128)(2,1)S(1)} collective-permute-done((bf16[4,9,16,256]{3,2,1,0:T(8,128)(2,1)S(1)}, bf16[4,9,16,256]{3,2,1,0:T(8,128)(2,1)S(1)}, u32[]{:S(2)}, u32[]{:S(2)}) %collective-permute-start.57) | collective-permute-done | bytes 294944 | tf_op jit(solution)/shard_map/ppermute | solution.py:591
  349.0 6.8 %unpack_two.1 = (f32[18,512,512]{2,1,0:T(8,128)}, f32[2,512,512]{2,1,0:T(8,128)}, f32[512,512]{1,0:T(8,128)}, f32[512,512]{1,0:T(8,128)}) custom-call(s32[3]{0:T(128)S(1)} %pad_add_fusion.1.refs_0_.place_ref, bf16[16,30,16,256]{3,2,1,0:T(8,128)(2,1)S(1)} %maximum_maximum_fusion.own_ref, bf16[16,30,16,256]{3,2,1,0:T(8,128)(2,1)S(1)} %collective-permute-done.62.other_ref), custom_call_target="tpu_custom_call" | custom-call | bytes 30933004 | tf_op jit(solution)/shard_map/unpack_two/pallas_call | solution.py:639
  355.8 6.3 %collective-permute-done.61 = bf16[8,9,16,256]{3,2,1,0:T(8,128)(2,1)S(1)} collective-permute-done((bf16[8,9,16,256]{3,2,1,0:T(8,128)(2,1)S(1)}, bf16[8,9,16,256]{3,2,1,0:T(8,128)(2,1)S(1)}, u32[]{:S(2)}, u32[]{:S(2)}) %collective-permute-start.61) | collective-permute-done | bytes 589856 | tf_op jit(solution)/shard_map/ppermute | solution.py:591
  369.3 5.2 %unpack_one.1 = f32[18,512,512]{2,1,0:T(8,128)} custom-call(s32[3]{0:T(128)S(1)} %pad_add_fusion.1.refs_0_.place_ref, bf16[2,16,9,16,256]{4,3,2,1,0:T(8,128)(2,1)S(1)} %pad_maximum_fusion.own_ref, bf16[2,16,9,16,256]{4,3,2,1,0:T(8,128)(2,1)} %collective-permute-done.64.other_ref, ...), custom_call_target="tpu_custom_call", output_to_operand_aliasing={{}: (3, {})} | custom-call | bytes 42467340 | tf_op jit(solution)/shard_map/unpack_one/pallas_call | solution.py:639
  (322 shorter events, 149.3 us)
Async XLA Ops:
  10.0 23.5 %collective-permute-start = (bf16[1024,512]{1,0:T(8,128)(2,1)}, bf16[1024,512]{1,0:T(8,128)(2,1)S(1)}, u32[]{:S(2)}, u32[]{:S(2)}) collective-permute-start(bf16[1024,512]{1,0:T(8,128)(2,1)} %bitcast.1.image_ref), channel_id=1, source_target_pairs={{0,0},{1,16},{2,2},{3,18},{4,4},{5,20},{6,6},{7,22},{8,8},{9,24},{... | collective-permute-start | bytes 3145736 | tf_op jit(solution)/shard_map/ppermute | solution.py:591
  13.4 17.6 %collective-permute-start.2 = (f32[40,512]{1,0:T(8,128)S(1)}, f32[40,512]{1,0:T(8,128)S(1)}, u32[]{:S(2)}, u32[]{:S(2)}) collective-permute-start(f32[40,512]{1,0:T(8,128)S(1)} %get-tuple-element.119), channel_id=1, source_target_pairs={{0,9},{1,25},{2,11},{3,27},{4,13},{5,29},{6,15},{7,31},{8,1},{9,17... | collective-permute-start | bytes 245768 | tf_op jit(solution)/shard_map/ppermute | solution.py:591
  33.5 25.6 %collective-permute-start.8 = (bf16[512,512]{1,0:T(8,128)(2,1)S(1)}, bf16[512,512]{1,0:T(8,128)(2,1)S(1)}, u32[]{:S(2)}, u32[]{:S(2)}) collective-permute-start(bf16[512,512]{1,0:T(8,128)(2,1)S(1)} %bitcast.115), channel_id=1, source_target_pairs={{0,0},{1,16},{2,2},{3,18},{4,4},{5,20},{6,6},{7,22},{8,8},{9,24},{... | collective-permute-start | bytes 1572872 | tf_op jit(solution)/shard_map/ppermute | solution.py:591
  44.5 15.8 %collective-permute-start.5 = (f32[40,512]{1,0:T(8,128)S(1)}, f32[40,512]{1,0:T(8,128)S(1)}, u32[]{:S(2)}, u32[]{:S(2)}) collective-permute-start(f32[40,512]{1,0:T(8,128)S(1)} %get-tuple-element.123), channel_id=1, source_target_pairs={{0,8},{1,9},{2,10},{3,11},{4,12},{5,13},{6,14},{7,15},{8,0},{9,1},... | collective-permute-start | bytes 245768 | tf_op jit(solution)/shard_map/ppermute | solution.py:591
  59.1 16.2 %collective-permute-start.12 = (bf16[512,512]{1,0:T(8,128)(2,1)S(1)}, bf16[512,512]{1,0:T(8,128)(2,1)S(1)}, u32[]{:S(2)}, u32[]{:S(2)}) collective-permute-start(bf16[512,512]{1,0:T(8,128)(2,1)S(1)} %bitcast.114), channel_id=1, source_target_pairs={{0,0},{1,16},{2,2},{3,18},{4,4},{5,20},{6,6},{7,22},{8,8},{9,24},{... | collective-permute-start | bytes 1572872 | tf_op jit(solution)/shard_map/ppermute | solution.py:591
  80.2 25.6 %collective-permute-start.13 = (bf16[1024,512]{1,0:T(8,128)(2,1)S(1)}, bf16[1024,512]{1,0:T(8,128)(2,1)}, u32[]{:S(2)}, u32[]{:S(2)}) collective-permute-start(bf16[1024,512]{1,0:T(8,128)(2,1)S(1)} %normed.1.own_ref.refs_1_), channel_id=1, source_target_pairs={{0,8},{1,9},{2,10},{3,11},{4,12},{5,13},{6,14},{7,15},{8,0},{9,1},... | collective-permute-start | bytes 3145736 | tf_op jit(solution)/shard_map/ppermute | solution.py:591
  105.8 30.0 %collective-permute-start.17 = (bf16[1024,512]{1,0:T(8,128)(2,1)}, bf16[1024,512]{1,0:T(8,128)(2,1)}, u32[]{:S(2)}, u32[]{:S(2)}) collective-permute-start(bf16[1024,512]{1,0:T(8,128)(2,1)} %constant_dynamic-update-slice_fusion.cot_own.refs_6_.rest_0_), channel_id=1, source_target_pairs={{0,8},{1,9},{2,10},{3,11},{4,12},{5,13},{6,14},{7,15},{8,0},{9,1},... | collective-permute-start | bytes 3145736 | tf_op jit(solution)/shard_map/ppermute | solution.py:591
  141.7 35.5 %collective-permute-start.18 = (bf16[1024,512]{1,0:T(8,128)(2,1)}, bf16[1024,512]{1,0:T(8,128)(2,1)S(1)}, u32[]{:S(2)}, u32[]{:S(2)}) collective-permute-start(bf16[1024,512]{1,0:T(8,128)(2,1)} %output.1), channel_id=1, source_target_pairs={{0,0},{1,16},{2,2},{3,18},{4,4},{5,20},{6,6},{7,22},{8,8},{9,24},{... | collective-permute-start | bytes 3145736 | tf_op jit(solution)/shard_map/ppermute | solution.py:591
  207.4 21.0 %collective-permute-start.31 = (bf16[8,13,16,256]{3,2,1,0:T(8,128)(2,1)S(1)}, bf16[8,13,16,256]{3,2,1,0:T(8,128)(2,1)S(1)}, u32[]{:S(2)}, u32[]{:S(2)}) collective-permute-start(bf16[8,13,16,256]{3,2,1,0:T(8,128)(2,1)S(1)} %get-tuple-element.227), channel_id=1, source_target_pairs={{0,4},{1,5},{2,6},{3,7},{4,0},{5,1},{6,2},{7,3},{8,12},{9,13},{10,... | collective-permute-start | bytes 2555912 | tf_op jit(solution)/shard_map/ppermute | solution.py:591
  208.9 20.7 %collective-permute-start.30 = (bf16[8,13,16,256]{3,2,1,0:T(8,128)(2,1)S(1)}, bf16[8,13,16,256]{3,2,1,0:T(8,128)(2,1)S(1)}, u32[]{:S(2)}, u32[]{:S(2)}) collective-permute-start(bf16[8,13,16,256]{3,2,1,0:T(8,128)(2,1)S(1)} %get-tuple-element.228), channel_id=1, source_target_pairs={{0,2},{1,3},{2,0},{3,1},{4,6},{5,7},{6,4},{7,5},{8,10},{9,11},{10,... | collective-permute-start | bytes 2555912 | tf_op jit(solution)/shard_map/ppermute | solution.py:591
  229.7 15.3 %collective-permute-start.32 = (bf16[2,16,9,16,256]{4,3,2,1,0:T(8,128)(2,1)S(1)}, bf16[2,16,9,16,256]{4,3,2,1,0:T(8,128)(2,1)S(1)}, u32[]{:S(2)}, u32[]{:S(2)}) collective-permute-start(bf16[2,16,9,16,256]{4,3,2,1,0:T(8,128)(2,1)S(1)} %get-tuple-element.168), channel_id=1, source_target_pairs={{0,1},{1,0},{2,3},{3,2},{4,5},{5,4},{6,7},{7,6},{8,9},{9,8},{10,11... | collective-permute-start | bytes 7077896 | tf_op jit(solution)/shard_map/ppermute | solution.py:591
  230.3 14.3 %collective-permute-start.39 = (bf16[4,13,16,256]{3,2,1,0:T(8,128)(2,1)S(1)}, bf16[4,13,16,256]{3,2,1,0:T(8,128)(2,1)S(1)}, u32[]{:S(2)}, u32[]{:S(2)}) collective-permute-start(bf16[4,13,16,256]{3,2,1,0:T(8,128)(2,1)S(1)} %get-tuple-element.241), channel_id=1, source_target_pairs={{0,2},{1,3},{2,0},{3,1},{4,6},{5,7},{6,4},{7,5},{8,10},{9,11},{10,... | collective-permute-start | bytes 1277960 | tf_op jit(solution)/shard_map/ppermute | solution.py:591
  245.8 15.1 %collective-permute-start.34 = (bf16[8,9,16,256]{3,2,1,0:T(8,128)(2,1)S(1)}, bf16[8,9,16,256]{3,2,1,0:T(8,128)(2,1)S(1)}, u32[]{:S(2)}, u32[]{:S(2)}) collective-permute-start(bf16[8,9,16,256]{3,2,1,0:T(8,128)(2,1)S(1)} %get-tuple-element.231), channel_id=1, source_target_pairs={{0,4},{1,5},{2,6},{3,7},{4,0},{5,1},{6,2},{7,3},{8,12},{9,13},{10,... | collective-permute-start | bytes 1769480 | tf_op jit(solution)/shard_map/ppermute | solution.py:591
  247.3 14.7 %collective-permute-start.33 = (bf16[8,9,16,256]{3,2,1,0:T(8,128)(2,1)S(1)}, bf16[8,9,16,256]{3,2,1,0:T(8,128)(2,1)S(1)}, u32[]{:S(2)}, u32[]{:S(2)}) collective-permute-start(bf16[8,9,16,256]{3,2,1,0:T(8,128)(2,1)S(1)} %get-tuple-element.232), channel_id=1, source_target_pairs={{0,2},{1,3},{2,0},{3,1},{4,6},{5,7},{6,4},{7,5},{8,10},{9,11},{10,... | collective-permute-start | bytes 1769480 | tf_op jit(solution)/shard_map/ppermute | solution.py:591
  248.2 14.3 %collective-permute-start.44 = (bf16[2,13,16,256]{3,2,1,0:T(8,128)(2,1)S(1)}, bf16[2,13,16,256]{3,2,1,0:T(8,128)(2,1)S(1)}, u32[]{:S(2)}, u32[]{:S(2)}) collective-permute-start(bf16[2,13,16,256]{3,2,1,0:T(8,128)(2,1)S(1)} %get-tuple-element.237), channel_id=1, source_target_pairs={{0,24},{1,25},{2,26},{3,27},{4,28},{5,29},{6,30},{7,31},{8,16},{9,... | collective-permute-start | bytes 638984 | tf_op jit(solution)/shard_map/ppermute | solution.py:591
  250.4 19.1 %collective-permute-start.42 = (bf16[2,13,16,256]{3,2,1,0:T(8,128)(2,1)S(1)}, bf16[2,13,16,256]{3,2,1,0:T(8,128)(2,1)S(1)}, u32[]{:S(2)}, u32[]{:S(2)}) collective-permute-start(bf16[2,13,16,256]{3,2,1,0:T(8,128)(2,1)S(1)} %get-tuple-element.239), channel_id=1, source_target_pairs={{0,16},{1,17},{2,18},{3,19},{4,20},{5,21},{6,22},{7,23},{8,24},{9,... | collective-permute-start | bytes 638984 | tf_op jit(solution)/shard_map/ppermute | solution.py:591
  251.4 18.0 %collective-permute-start.43 = (bf16[2,13,16,256]{3,2,1,0:T(8,128)(2,1)S(1)}, bf16[2,13,16,256]{3,2,1,0:T(8,128)(2,1)S(1)}, u32[]{:S(2)}, u32[]{:S(2)}) collective-permute-start(bf16[2,13,16,256]{3,2,1,0:T(8,128)(2,1)S(1)} %get-tuple-element.240), channel_id=1, source_target_pairs={{0,8},{1,9},{2,10},{3,11},{4,12},{5,13},{6,14},{7,15},{8,0},{9,1},... | collective-permute-start | bytes 638984 | tf_op jit(solution)/shard_map/ppermute | solution.py:591
  273.9 14.7 %collective-permute-start.49 = (bf16[30,16,256]{2,1,0:T(8,128)(2,1)S(1)}, bf16[30,16,256]{2,1,0:T(8,128)(2,1)S(1)}, u32[]{:S(2)}, u32[]{:S(2)}) collective-permute-start(bf16[30,16,256]{2,1,0:T(8,128)(2,1)S(1)} %pad_maximum_fusion.9), channel_id=1, source_target_pairs={{0,8},{1,9},{2,10},{3,11},{4,12},{5,13},{6,14},{7,15},{8,0},{9,1},... | collective-permute-start | bytes 737288 | tf_op jit(solution)/shard_map/ppermute | solution.py:591
  273.9 19.0 %collective-permute-start.48 = (bf16[30,16,256]{2,1,0:T(8,128)(2,1)S(1)}, bf16[30,16,256]{2,1,0:T(8,128)(2,1)S(1)}, u32[]{:S(2)}, u32[]{:S(2)}) collective-permute-start(bf16[30,16,256]{2,1,0:T(8,128)(2,1)S(1)} %pad_maximum_fusion.9), channel_id=1, source_target_pairs={{0,16},{1,17},{2,18},{3,19},{4,20},{5,21},{6,22},{7,23},{8,24},{9,... | collective-permute-start | bytes 737288 | tf_op jit(solution)/shard_map/ppermute | solution.py:591
  307.4 25.2 %collective-permute-start.58 = (bf16[8,17,16,256]{3,2,1,0:T(8,128)(2,1)S(1)}, bf16[8,17,16,256]{3,2,1,0:T(8,128)(2,1)S(1)}, u32[]{:S(2)}, u32[]{:S(2)}) collective-permute-start(bf16[8,17,16,256]{3,2,1,0:T(8,128)(2,1)S(1)} %pad_maximum_fusion.1), channel_id=1, source_target_pairs={{0,2},{1,3},{2,0},{3,1},{4,6},{5,7},{6,4},{7,5},{8,10},{9,11},{10,... | collective-permute-start | bytes 3342344 | tf_op jit(solution)/shard_map/ppermute | solution.py:591
  309.0 19.3 %collective-permute-start.59 = (bf16[8,13,16,256]{3,2,1,0:T(8,128)(2,1)S(1)}, bf16[8,13,16,256]{3,2,1,0:T(8,128)(2,1)S(1)}, u32[]{:S(2)}, u32[]{:S(2)}) collective-permute-start(bf16[8,13,16,256]{3,2,1,0:T(8,128)(2,1)S(1)} %pad_maximum_fusion.4), channel_id=1, source_target_pairs={{0,4},{1,5},{2,6},{3,7},{4,0},{5,1},{6,2},{7,3},{8,12},{9,13},{10,... | collective-permute-start | bytes 2555912 | tf_op jit(solution)/shard_map/ppermute | solution.py:591
  338.7 24.0 %collective-permute-start.63 = (bf16[1024,512]{1,0:T(8,128)(2,1)S(1)}, bf16[1024,512]{1,0:T(8,128)(2,1)S(1)}, u32[]{:S(2)}, u32[]{:S(2)}) collective-permute-start(bf16[1024,512]{1,0:T(8,128)(2,1)S(1)} %get-tuple-element.219), channel_id=1, source_target_pairs={{0,0},{1,16},{2,2},{3,18},{4,4},{5,20},{6,6},{7,22},{8,8},{9,24},{... | collective-permute-start | bytes 3145736 | tf_op jit(solution)/shard_map/ppermute | solution.py:591
  347.5 14.6 %collective-permute-start.61 = (bf16[8,9,16,256]{3,2,1,0:T(8,128)(2,1)S(1)}, bf16[8,9,16,256]{3,2,1,0:T(8,128)(2,1)S(1)}, u32[]{:S(2)}, u32[]{:S(2)}) collective-permute-start(bf16[8,9,16,256]{3,2,1,0:T(8,128)(2,1)S(1)} %pad_maximum_fusion.7), channel_id=1, source_target_pairs={{0,4},{1,5},{2,6},{3,7},{4,0},{5,1},{6,2},{7,3},{8,12},{9,13},{10,... | collective-permute-start | bytes 1769480 | tf_op jit(solution)/shard_map/ppermute | solution.py:591
  348.0 14.3 %collective-permute-start.60 = (bf16[8,9,16,256]{3,2,1,0:T(8,128)(2,1)S(1)}, bf16[8,9,16,256]{3,2,1,0:T(8,128)(2,1)S(1)}, u32[]{:S(2)}, u32[]{:S(2)}) collective-permute-start(bf16[8,9,16,256]{3,2,1,0:T(8,128)(2,1)S(1)} %pad_maximum_fusion.6), channel_id=1, source_target_pairs={{0,2},{1,3},{2,0},{3,1},{4,6},{5,7},{6,4},{7,5},{8,10},{9,11},{10,... | collective-permute-start | bytes 1769480 | tf_op jit(solution)/shard_map/ppermute | solution.py:591
  (111 other events, 1245.2 us)

commit v4 on v3

--- a/solution.py
+++ b/solution.py
@@ -16,7 +16,7 @@
 PIECES = 32
 LIMITS = {
     "conv_one": 46, "conv_two": 46, "weight_two_grad": 24, "weight_one_grad": 20, "conv_two_back": 36, "conv_one_back": 36,
-    "attend": 40, "key_value_grad": 60, "early": 14, "matrix_grad": 16, "unpack_two": 40, "unpack_one": 16,
+    "attend": 40, "attend_first": 32, "key_value_grad": 60, "early": 14, "matrix_grad": 16, "unpack_two": 40, "unpack_one": 16,
     "first": 8, "masks": 12, "normed": 8, "output": 8, "image_grad": 12,
 }
 
@@ -254,9 +254,42 @@
         grads[...] = nt(cot_ref[...], proj_ref[...]).astype(BF16)
 
 
+def attend_first_kernel(
+    keys_own, values_own, keys_pair, values_pair, queries_ref, column_ref, row_ref,
+    weights_ref, top_ref, total_ref, sum_ref,
+):
+    pixels, channels = queries_ref.shape
+    scale = channels ** (-0.5)
+    block = 512
+
+    def step(i, carry):
+        part = pl.ds(pl.multiple_of(i * block, block), block)
+        queries = queries_ref[part, :]
+        column = column_ref[part, 0:1]
+        scores = []
+        for j, keys in enumerate((keys_own, keys_pair)):
+            product = nt(queries, keys[...]) * scale
+            scores.append(jnp.where(column == row_ref[:, j * pixels : (j + 1) * pixels], product, MASKED_SCORE))
+        top = jnp.maximum(*[jnp.max(s, axis=1, keepdims=True) for s in scores])
+        total, summed = 0.0, 0.0
+        for j, (score, values) in enumerate(zip(scores, (values_own, values_pair))):
+            weights = jnp.exp(score - top)
+            total = total + jnp.sum(weights, axis=1, keepdims=True)
+            rounded = weights.astype(BF16)
+            weights_ref[part, j * pixels : (j + 1) * pixels] = rounded
+            summed = summed + nn(rounded, values[...])
+        top_ref[part, :] = jnp.broadcast_to(top, (block, 128))
+        total_ref[part, :] = jnp.broadcast_to(total, (block, 128))
+        sum_ref[part, :] = summed
+        return carry
+
+    lax.fori_loop(0, pixels // block, step, 0)
+
+
 def attend_kernel(
-    near_ref, cross_ref, keys_own, values_own, keys_pair, values_pair, queries_ref, grads_ref, qk_ref, value_ref,
-    bias_ref, column_ref, row_ref, attended_ref, query_grad_ref, totals_ref, far_keys, far_values,
+    near_ref, cross_ref, keys_own, values_own, keys_pair, values_pair, queries_ref, grads_ref,
+    weights_ref, top_ref, total_ref, sum_ref, qk_ref, value_ref, bias_ref, column_ref, row_ref,
+    attended_ref, query_grad_ref, totals_ref, far_keys, far_values,
 ):
     pixels, channels = near_ref.shape
     scale = channels ** (-0.5)
@@ -266,31 +299,27 @@
         far_keys[part, :] = nn(rows, qk_ref[1]).astype(BF16)
         far_values[part, :] = (nn(rows, value_ref[...]) + bias_ref[1:2, :]).astype(BF16)
     block = totals_ref.shape[2]
-    halves = (
-        (keys_own, values_own, slice(0, pixels)),
-        (keys_pair, values_pair, slice(pixels, 2 * pixels)),
-        (far_keys, far_values, slice(2 * pixels, 4 * pixels)),
-    )
 
     def step(i, carry):
         part = pl.ds(pl.multiple_of(i * block, block), block)
         queries, upstream = queries_ref[part, :], grads_ref[part, :]
-        column = column_ref[part, 0:1]
-        scores = []
-        for keys, _, span in halves:
-            product = nt(queries, keys[...]) * scale
-            scores.append(jnp.where(column == row_ref[:, span], product, MASKED_SCORE))
-        top = functools.reduce(jnp.maximum, [jnp.max(s, axis=1, keepdims=True) for s in scores])
-        weights = [jnp.exp(s - top) for s in scores]
-        total = sum(jnp.sum(w, axis=1, keepdims=True) for w in weights)
+        product = nt(queries, far_keys[...]) * scale
+        scores = jnp.where(column_ref[part, 0:1] == row_ref[:, 2 * pixels :], product, MASKED_SCORE)
+        first_top = top_ref[part, 0:1]
+        top = jnp.maximum(first_top, jnp.max(scores, axis=1, keepdims=True))
+        shrink = jnp.exp(first_top - top)
+        weights = jnp.exp(scores - top)
+        total = total_ref[part, 0:1] * shrink + jnp.sum(weights, axis=1, keepdims=True)
         inverse = 1.0 / total
-        attended = sum(nn(w.astype(BF16), values[...]) for w, (_, values, _) in zip(weights, halves)) * inverse
+        attended = (sum_ref[part, :] * shrink + nn(weights.astype(BF16), far_values[...])) * inverse
         attended_ref[part, :] = attended.astype(BF16)
         delta = jnp.sum(attended * upstream.astype(F32), axis=1, keepdims=True)
-        query_grad = 0.0
-        for w, (keys, values, _) in zip(weights, halves):
-            prob_grad = nt(upstream, values[...])
-            score_grad = (w * inverse * (prob_grad - delta)).astype(BF16)
+        score_grad = (weights * inverse * (nt(upstream, far_values[...]) - delta)).astype(BF16)
+        query_grad = nn(score_grad, far_keys[...])
+        factor = shrink * inverse
+        for j, (keys, values) in enumerate(((keys_own, values_own), (keys_pair, values_pair))):
+            held = weights_ref[part, j * pixels : (j + 1) * pixels].astype(F32)
+            score_grad = (held * factor * (nt(upstream, values[...]) - delta)).astype(BF16)
             query_grad = query_grad + nn(score_grad, keys[...])
         query_grad_ref[part, :] = (query_grad * scale).astype(BF16)
         log_total = jnp.transpose(jnp.broadcast_to(top + jnp.log(total), (block, 128)))
@@ -661,7 +690,7 @@
     x = permute(image_flat, turned)
     near0, cross0, stats0 = call(
         first_kernel, "first", (image_flat, tiles, side), [field, whole(2, pixels // 2), SMEM],
-        [row_out, row_out, stat_out], 16,
+        [row_out, row_out, stat_out], 16, after=(permute(block8(norm_gain[0]), to_pair),),
     )
     own0 = permute(stats0, turned)
     pair0 = permute(stats0, lambda i: to_pair(turned(i)))
@@ -736,13 +765,20 @@
         [field] * 4 + [whole(2, channels, channels), square, square, stat],
         [(field, field_b16)] * 8, 32, 8 * matmul,
     )
-    normed_cross = permute(behind(normed_near, keys), to_pair)
+    lane_field = (whole(pixels, 128), shape((pixels, 128), F32))
+    weights, tops, sums, products = call(
+        attend_first_kernel, "attend_first", (keys, values, keys_pair, values_pair, queries, column_tiles, row_tiles),
+        [field] * 5 + [whole(pixels, 128), whole(1, 4 * pixels)],
+        [(whole(pixels, 2 * pixels), shape((pixels, 2 * pixels), BF16)), lane_field, lane_field, (field, field_f32)],
+        32, 2 * 2 * matmul * pixels / channels,
+    )
+    normed_cross = permute(behind(normed_near, products), to_pair)
     cot_near = permute(behind(cotangent, normed_near), to_near)
     attended, query_grad, totals = call(
         attend_kernel, "attend",
-        (normed_near, normed_cross, keys, values, keys_pair, values_pair, queries, grads, qk_weight, value_weight, bias_rows,
+        (normed_near, normed_cross, keys, values, keys_pair, values_pair, queries, grads, weights, tops, sums, products, qk_weight, value_weight, bias_rows,
          column_tiles, row_tiles),
-        [field] * 8 + [whole(2, channels, channels), square, stat, whole(pixels, 128), whole(1, 4 * pixels)],
+        [field] * 8 + [whole(pixels, 2 * pixels), whole(pixels, 128), whole(pixels, 128), field] + [whole(2, channels, channels), square, stat, whole(pixels, 128), whole(1, 4 * pixels)],
         [(field, field_b16), (field, field_b16), totals_out],
         58, 4 * matmul + 4 * 4 * matmul * pixels / channels,
         [pltpu.VMEM((2 * pixels, channels), BF16)] * 2,
@@ -754,7 +790,7 @@
         out_kernel, "output", (attended, residual, proj_weight, block8(proj_bias)), [field, field, square, stat],
         [(field, field_b16)], 16, matmul, after=(cot_near,),
     )
-    output_there = permute(output, turned)
+    output_there = permute(output.reshape(1, band, width, channels), turned)
     key_grad, value_grad, normed_grad, near3, cross3, stats3, sums3 = call(
         key_kernel, "key_value_grad",
         (side, keys, values, queries, grads, queries_pair, grads_pair, normed_near, cot_near, normed_cross, cot_cross,
@@ -966,7 +1002,7 @@
     one_first, one_second = z_join(*after_token(token, *one))
     token = one_first
     one_coming = both(one_first, one_second, 4, 2)
-    image_there = permute(behind(image_grad, token), turned)
+    image_there = permute(behind(image_grad, token).reshape(1, band, width, channels), turned)
 
     two = jnp.concatenate(join_halves(token, two_first, two_second, two_coming), axis=1)
     token = two
@@ -1003,8 +1039,8 @@
     weights = unpack(one, 9, 3, 0, 18, 0, weights, "unpack_one")
 
     return (
-        output_there.reshape(1, band, width, channels),
-        image_there.reshape(1, band, width, channels),
+        output_there,
+        image_there,
         weights.reshape(2, 3, 3, channels, channels),
         small[0:2],
         small[2:5],

time: 385 us -> 376 us (0.977)
  waiting for transfers between devices: 118 us -> 112 us
  starting transfers between devices: 78.9 us -> 73.9 us
    ppermute x65 -> x66, waiting for transfers between devices: 118 us -> 112 us  [permute(): lax.ppermute(x, ('seq', 'batch'), [(i, to(i)) for i in range(devices)])]
    ppermute x65 -> x66, starting transfers between devices: 78.9 us -> 73.9 us  [permute(): lax.ppermute(x, ('seq', 'batch'), [(i, to(i)) for i in range(devices)])]
    unnamed x143 -> x149, local copies, waits for them, and re-layouts: 18.6 us -> 20.2 us
    pallas_call x17 -> x18, Pallas kernels: 144 us -> 145 us  [call(): pl.pallas_call(run if after else kernel, in_specs=list(in_specs) + [pl.Bl...]
  transfers between devices with their start and end apart: 65 -> 66, of which waited for: 34 -> 34; matrix products, arithmetic and copies ran while one was open for 3% -> 3% of each run, Pallas kernels for 33% -> 35%
where the time goes in v4:
time: 376 us; the launch traced here: 370 us
  Pallas kernels  145 us (39%)
  waiting for transfers between devices  112 us (30%)
  starting transfers between devices  73.9 us (20%)
  local copies, waits for them, and re-layouts  23.8 us (6%)
  other arithmetic  13 us (3%)
    pallas_call x18, Pallas kernels, call(): pl.pallas_call(run if after else kernel, in_specs=list(in_specs) + [pl.Bl...  145 us
    ppermute x66, waiting for transfers between devices, permute(): lax.ppermute(x, ('seq', 'batch'), [(i, to(i)) for i in range(devices)])  112 us
    ppermute x66, starting transfers between devices, permute(): lax.ppermute(x, ('seq', 'batch'), [(i, to(i)) for i in range(devices)])  73.9 us
    unnamed x149, local copies, waits for them, and re-layouts  20.2 us
  transfers between devices with their start and end apart: 66, of which 34 were waited for; matrix products, arithmetic and copies ran while one was open for 3% of the time, Pallas kernels for 35%

profile of v4, /device:TPU:0, one launch (start us, length us, event | category | flops | bytes accessed | tf_op | source)
XLA Modules:
  0.0 369.9 jit_solution(3250742618603971705)
XLA Ops:
  4.4 4.2 %collective-permute-start.1 = (f32[8,512]{1,0:T(8,128)S(1)}, f32[8,512]{1,0:T(8,128)S(1)}, u32[]{:S(2)}, u32[]{:S(2)}) collective-permute-start(f32[8,512]{1,0:T(8,128)S(1)} %get-tuple-element.279), channel_id=1, source_target_pairs={{0,1},{1,0},{2,3},{3,2},{4,5},{5,4},{6,7},{7,6},{8,9},{9,8},{10,11... | collective-permute-start | bytes 49160 | tf_op jit(solution)/shard_map/ppermute | solution.py:620
  17.7 15.8 %collective-permute-done.4.pair_ref.refs_4_.refs_8_.refs_9_ = f32[8,512]{1,0:T(8,128)S(1)} collective-permute-done((f32[8,512]{1,0:T(8,128)S(1)}, f32[8,512]{1,0:T(8,128)S(1)}, u32[]{:S(2)}, u32[]{:S(2)}) %collective-permute-start.4) | collective-permute-done | bytes 16416 | tf_op jit(solution)/shard_map/ppermute | solution.py:620
  36.1 9.2 %conv_one.1 = (f32[1024,512]{1,0:T(8,128)S(1)}, bf16[1024,512]{1,0:T(8,128)(2,1)S(1)}, f32[40,512]{1,0:T(8,128)S(1)}, f32[40,512]{1,0:T(8,128)S(1)}, f32[8,512]{1,0:T(8,128)S(1)}) custom-call(s32[1]{0:T(128)} %bitcast.refs_2_.refs_0_.side_ref, bf16[1024,512]{1,0:T(8,128)(2,1)S(1)} %collective-permute-done.refs_1_.refs_9_.refs_4_.refs_5_, ...), custom_call_target="tpu_custom_call" | custom-call | flops 4831838208 | bytes 16384004 | tf_op jit(solution)/shard_map/conv_one/pallas_call | solution.py:668
  56.7 10.1 %conv_two.1 = (f32[1024,512]{1,0:T(8,128)S(1)}, bf16[1024,512]{1,0:T(8,128)(2,1)S(1)}, f32[40,512]{1,0:T(8,128)S(1)}, f32[40,512]{1,0:T(8,128)S(1)}, f32[8,512]{1,0:T(8,128)S(1)}) custom-call(s32[1]{0:T(128)} %bitcast.refs_2_.refs_0_.side_ref, f32[1024,512]{1,0:T(8,128)S(1)} %get-tuple-element.126.refs_1_.x_ref, ...), custom_call_target="tpu_custom_call" | custom-call | flops 4831838208 | bytes 18481156 | tf_op jit(solution)/shard_map/conv_two/pallas_call | solution.py:668
  80.8 6.4 %early.1 = (bf16[1024,512]{1,0:T(8,128)(2,1)S(1)}, bf16[1024,512]{1,0:T(8,128)(2,1)S(1)}, bf16[1024,512]{1,0:T(8,128)(2,1)S(1)}, bf16[1024,512]{1,0:T(8,128)(2,1...) custom-call(bf16[1024,512]{1,0:T(8,128)(2,1)S(1)} %normed.1.own_ref., ...), custom_call_target="tpu_custom_call" | custom-call | flops 4294967296 | bytes 14696448 | tf_op jit(solution)/shard_map/early/pallas_call | solution.py:668
  89.2 6.7 %attend_first.1 = (bf16[1024,2048]{1,0:T(8,128)(2,1)S(1)}, f32[1024,128]{1,0:T(8,128)S(1)}, f32[1024,128]{1,0:T(8,128)S(1)}, f32[1024,512]{1,0:T(8,128)S(1)}) custom-call(bf16[1024,512]{1,0:T(8,128)(2,1)S(1)} %get-tuple-element.136.keys_own.keys, bf16[1024,512]{1,0:T(8,128)(2,1)S(1)} %get-tuple-element.137.values_own.values, ...), custom_call_target="tpu_custom_call" | custom-call | flops 4294967296 | bytes 13123584 | tf_op jit(solution)/shard_map/attend_first/pallas_call | solution.py:668
  103.3 21.8 %attend.1 = (bf16[1024,512]{1,0:T(8,128)(2,1)S(1)}, bf16[1024,512]{1,0:T(8,128)(2,1)S(1)}, f32[2,8,512]{2,1,0:T(8,128)}) custom-call(bf16[1024,512]{1,0:T(8,128)(2,1)} %collective-permute-done.14.near_ref.near_hbm, bf16[1024,512]{1,0:T(8,128)(2,1)S(1)} %collective-permute-done.17.cross_ref.cross_hbm, bf16[1024,512]{1,0:T(8,128)(2,1)S(1)} %get-tuple-element.136.keys_own.keys, ...), custom_call_target="tpu_custom_call" | custom-call | flops 19327352832 | bytes 19988480 | tf_op jit(solution)/shard_map/attend/pallas_call | solution.py:668
  133.7 30.2 %key_value_grad.1 = (bf16[1024,512]{1,0:T(8,128)(2,1)}, bf16[1024,512]{1,0:T(8,128)(2,1)}, f32[1024,512]{1,0:T(8,128)}, f32[40,512]{1,0:T(8,128)}, f32[40,512]{1...) custom-call(s32[1]{0:T(128)} %bitcast.refs_2_.refs_0_.side_ref, bf16[1024,512]{1,0:T(8,128)(2,1)} %copy-done.60, ...), custom_call_target="tpu_custom_call" | custom-call | flops 20937965568 | bytes 21020676 | tf_op jit(solution)/shard_map/key_value_grad/pallas_call | solution.py:668
  174.1 10.1 %weight_two_grad.1 = (bf16[2,16,13,16,256]{4,3,2,1,0:T(8,128)(2,1)S(1)}, bf16[2,16,13,16,256]{4,3,2,1,0:T(8,128)(2,1)S(1)}, bf16[3,1088,512]{2,1,0:T(8,128)(2,1)...) custom-call(s32[3]{0:T(128)S(1)} %pad_add_fusion.1.refs_0_.place_ref, s32[1]{0:T(128)} %bitcast.refs_2_.refs_0_.side_ref, ...), custom_call_target="tpu_custom_call" | custom-call | flops 4831838208 | bytes 27787280 | tf_op jit(solution)/shard_map/weight_two_grad/pallas_call | solution.py:668
  185.0 10.2 %conv_two_back.1 = (f32[1024,512]{1,0:T(8,128)S(1)}, f32[40,512]{1,0:T(8,128)S(1)}, f32[40,512]{1,0:T(8,128)S(1)}, f32[8,512]{1,0:T(8,128)S(1)}, f32[8,512]{1,0:T(8,128)S(1)}) custom-call(s32[1]{0:T(128)} %bitcast.refs_2_.refs_0_.side_ref, bf16[3,1088,512]{2,1,0:T(8,128)(2,1)S(1)} %get-tuple-element.165.shifted, bf16[9,1024,128]{2,1,0:T(8,128)(2,1)S(1)} %copy-done.28, ...), custom_call_target="tpu_custom_call" | custom-call | flops 4831838208 | bytes 19742724 | tf_op jit(solution)/shard_map/conv_two_back/pallas_call | solution.py:668
  205.5 8.6 %weight_one_grad.1 = (bf16[2,16,9,16,256]{4,3,2,1,0:T(8,128)(2,1)S(1)}, bf16[2,16,9,16,256]{4,3,2,1,0:T(8,128)(2,1)S(1)}, bf16[3,1088,512]{2,1,0:T(8,128)(2,1)S(1)}, f32[8,512]{1,0:T(8,128)S(1)}) custom-call(s32[3]{0:T(128)S(1)} %pad_add_fusion.1.refs_0_.place_ref, s32[1]{0:T(128)} %bitcast.refs_2_.refs_0_.side_ref, f32[1024,512]{1,0:T(8,128)S(1)} %copy-done.48, ...), custom_call_target="tpu_custom_call" | custom-call | flops 4831838208 | bytes 16252944 | tf_op jit(solution)/shard_map/weight_one_grad/pallas_call | solution.py:668
  221.5 10.2 %conv_one_back.1 = (f32[1024,512]{1,0:T(8,128)S(1)}, f32[40,512]{1,0:T(8,128)S(1)}, f32[40,512]{1,0:T(8,128)S(1)}, f32[8,512]{1,0:T(8,128)S(1)}, f32[8,512]{1,0:T(8,128)S(1)}) custom-call(s32[1]{0:T(128)} %bitcast.refs_2_.refs_0_.side_ref, bf16[3,1088,512]{2,1,0:T(8,128)(2,1)S(1)} %get-tuple-element.177.refs_1_, bf16[9,1024,128]{2,1,0:T(8,128)(2,1)S(1)} %copy-done.28, ...), custom_call_target="tpu_custom_call" | custom-call | flops 4831838208 | bytes 18694148 | tf_op jit(solution)/shard_map/conv_one_back/pallas_call | solution.py:668
  242.4 7.4 %collective-permute-done.35 = bf16[8,9,16,256]{3,2,1,0:T(8,128)(2,1)S(1)} collective-permute-done((bf16[8,9,16,256]{3,2,1,0:T(8,128)(2,1)S(1)}, bf16[8,9,16,256]{3,2,1,0:T(8,128)(2,1)S(1)}, u32[]{:S(2)}, u32[]{:S(2)}) %collective-permute-start.35) | collective-permute-done | bytes 589856 | tf_op jit(solution)/shard_map/ppermute | solution.py:620
  251.5 6.8 %collective-permute-done.43 = bf16[2,13,16,256]{3,2,1,0:T(8,128)(2,1)S(1)} collective-permute-done((bf16[2,13,16,256]{3,2,1,0:T(8,128)(2,1)S(1)}, bf16[2,13,16,256]{3,2,1,0:T(8,128)(2,1)S(1)}, u32[]{:S(2)}, u32[]{:S(2)}) %collective-permute-start.43) | collective-permute-done | bytes 213024 | tf_op jit(solution)/shard_map/ppermute | solution.py:620
  271.4 5.3 %collective-permute-done.50 = bf16[30,16,256]{2,1,0:T(8,128)(2,1)S(1)} collective-permute-done((bf16[30,16,256]{2,1,0:T(8,128)(2,1)S(1)}, bf16[30,16,256]{2,1,0:T(8,128)(2,1)S(1)}, u32[]{:S(2)}, u32[]{:S(2)}) %collective-permute-start.50) | collective-permute-done | bytes 245792 | tf_op jit(solution)/shard_map/ppermute | solution.py:620
  276.7 5.6 %collective-permute-done.49 = bf16[30,16,256]{2,1,0:T(8,128)(2,1)S(1)} collective-permute-done((bf16[30,16,256]{2,1,0:T(8,128)(2,1)S(1)}, bf16[30,16,256]{2,1,0:T(8,128)(2,1)S(1)}, u32[]{:S(2)}, u32[]{:S(2)}) %collective-permute-start.49) | collective-permute-done | bytes 245792 | tf_op jit(solution)/shard_map/ppermute | solution.py:620
  293.1 4.3 %collective-permute-done.46 = bf16[2,9,16,256]{3,2,1,0:T(8,128)(2,1)S(1)} collective-permute-done((bf16[2,9,16,256]{3,2,1,0:T(8,128)(2,1)S(1)}, bf16[2,9,16,256]{3,2,1,0:T(8,128)(2,1)S(1)}, u32[]{:S(2)}, u32[]{:S(2)}) %collective-permute-start.46) | collective-permute-done | bytes 147488 | tf_op jit(solution)/shard_map/ppermute | solution.py:620
  304.2 4.3 %collective-permute-done.54 = bf16[2,9,16,256]{3,2,1,0:T(8,128)(2,1)S(1)} collective-permute-done((bf16[2,9,16,256]{3,2,1,0:T(8,128)(2,1)S(1)}, bf16[2,9,16,256]{3,2,1,0:T(8,128)(2,1)S(1)}, u32[]{:S(2)}, u32[]{:S(2)}) %collective-permute-start.54) | collective-permute-done | bytes 147488 | tf_op jit(solution)/shard_map/ppermute | solution.py:620
  313.8 5.0 %collective-permute-done.60 = bf16[8,13,16,256]{3,2,1,0:T(8,128)(2,1)S(1)} collective-permute-done((bf16[8,13,16,256]{3,2,1,0:T(8,128)(2,1)S(1)}, bf16[8,13,16,256]{3,2,1,0:T(8,128)(2,1)S(1)}, u32[]{:S(2)}, u32[]{:S(2)}) %collective-permute-start.60) | collective-permute-done | bytes 852000 | tf_op jit(solution)/shard_map/ppermute | solution.py:620
  318.8 4.3 %collective-permute-done.59 = bf16[8,17,16,256]{3,2,1,0:T(8,128)(2,1)S(1)} collective-permute-done((bf16[8,17,16,256]{3,2,1,0:T(8,128)(2,1)S(1)}, bf16[8,17,16,256]{3,2,1,0:T(8,128)(2,1)S(1)}, u32[]{:S(2)}, u32[]{:S(2)}) %collective-permute-start.59) | collective-permute-done | bytes 1114144 | tf_op jit(solution)/shard_map/ppermute | solution.py:620
  330.0 6.6 %collective-permute-done.58 = bf16[4,9,16,256]{3,2,1,0:T(8,128)(2,1)S(1)} collective-permute-done((bf16[4,9,16,256]{3,2,1,0:T(8,128)(2,1)S(1)}, bf16[4,9,16,256]{3,2,1,0:T(8,128)(2,1)S(1)}, u32[]{:S(2)}, u32[]{:S(2)}) %collective-permute-start.58) | collective-permute-done | bytes 294944 | tf_op jit(solution)/shard_map/ppermute | solution.py:620
  339.6 6.8 %unpack_two.1 = (f32[18,512,512]{2,1,0:T(8,128)}, f32[2,512,512]{2,1,0:T(8,128)}, f32[512,512]{1,0:T(8,128)}, f32[512,512]{1,0:T(8,128)}) custom-call(s32[3]{0:T(128)S(1)} %pad_add_fusion.1.refs_0_.place_ref, bf16[16,30,16,256]{3,2,1,0:T(8,128)(2,1)S(1)} %maximum_maximum_fusion.own_ref, bf16[16,30,16,256]{3,2,1,0:T(8,128)(2,1)S(1)} %collective-permute-done.63.other_ref), custom_call_target="tpu_custom_call" | custom-call | bytes 30933004 | tf_op jit(solution)/shard_map/unpack_two/pallas_call | solution.py:668
  346.4 6.2 %collective-permute-done.62 = bf16[8,9,16,256]{3,2,1,0:T(8,128)(2,1)S(1)} collective-permute-done((bf16[8,9,16,256]{3,2,1,0:T(8,128)(2,1)S(1)}, bf16[8,9,16,256]{3,2,1,0:T(8,128)(2,1)S(1)}, u32[]{:S(2)}, u32[]{:S(2)}) %collective-permute-start.62) | collective-permute-done | bytes 589856 | tf_op jit(solution)/shard_map/ppermute | solution.py:620
  361.7 5.2 %unpack_one.1 = f32[18,512,512]{2,1,0:T(8,128)} custom-call(s32[3]{0:T(128)S(1)} %pad_add_fusion.1.refs_0_.place_ref, bf16[2,16,9,16,256]{4,3,2,1,0:T(8,128)(2,1)S(1)} %pad_maximum_fusion.own_ref, bf16[2,16,9,16,256]{4,3,2,1,0:T(8,128)(2,1)} %collective-permute-done.65.other_ref, ...), custom_call_target="tpu_custom_call", output_to_operand_aliasing={{}: (3, {})} | custom-call | bytes 42467340 | tf_op jit(solution)/shard_map/unpack_one/pallas_call | solution.py:668
  (331 shorter events, 156.2 us)
Async XLA Ops:
  0.7 34.8 %collective-permute-start = (bf16[1024,512]{1,0:T(8,128)(2,1)}, bf16[1024,512]{1,0:T(8,128)(2,1)S(1)}, u32[]{:S(2)}, u32[]{:S(2)}) collective-permute-start(bf16[1024,512]{1,0:T(8,128)(2,1)} %bitcast.106), channel_id=1, source_target_pairs={{0,0},{1,16},{2,2},{3,18},{4,4},{5,20},{6,6},{7,22},{8,8},{9,24},{... | collective-permute-start | bytes 3145736 | tf_op jit(solution)/shard_map/ppermute | solution.py:620
  13.4 20.1 %collective-permute-start.4 = (f32[8,512]{1,0:T(8,128)S(1)}, f32[8,512]{1,0:T(8,128)S(1)}, u32[]{:S(2)}, u32[]{:S(2)}) collective-permute-start(f32[8,512]{1,0:T(8,128)S(1)} %get-tuple-element.124), channel_id=1, source_target_pairs={{0,1},{1,17},{2,3},{3,19},{4,5},{5,21},{6,7},{7,23},{8,9},{9,25},{... | collective-permute-start | bytes 49160 | tf_op jit(solution)/shard_map/ppermute | solution.py:620
  14.7 18.8 %collective-permute-start.2 = (f32[40,512]{1,0:T(8,128)S(1)}, f32[40,512]{1,0:T(8,128)S(1)}, u32[]{:S(2)}, u32[]{:S(2)}) collective-permute-start(f32[40,512]{1,0:T(8,128)S(1)} %get-tuple-element.122), channel_id=1, source_target_pairs={{0,8},{1,24},{2,10},{3,26},{4,12},{5,28},{6,14},{7,30},{8,0},{9,16... | collective-permute-start | bytes 245768 | tf_op jit(solution)/shard_map/ppermute | solution.py:620
  16.3 17.2 %collective-permute-start.3 = (f32[40,512]{1,0:T(8,128)S(1)}, f32[40,512]{1,0:T(8,128)S(1)}, u32[]{:S(2)}, u32[]{:S(2)}) collective-permute-start(f32[40,512]{1,0:T(8,128)S(1)} %get-tuple-element.123), channel_id=1, source_target_pairs={{0,9},{1,25},{2,11},{3,27},{4,13},{5,29},{6,15},{7,31},{8,1},{9,17... | collective-permute-start | bytes 245768 | tf_op jit(solution)/shard_map/ppermute | solution.py:620
  35.4 17.9 %collective-permute-start.9 = (bf16[512,512]{1,0:T(8,128)(2,1)S(1)}, bf16[512,512]{1,0:T(8,128)(2,1)S(1)}, u32[]{:S(2)}, u32[]{:S(2)}) collective-permute-start(bf16[512,512]{1,0:T(8,128)(2,1)S(1)} %bitcast.115), channel_id=1, source_target_pairs={{0,0},{1,16},{2,2},{3,18},{4,4},{5,20},{6,6},{7,22},{8,8},{9,24},{... | collective-permute-start | bytes 1572872 | tf_op jit(solution)/shard_map/ppermute | solution.py:620
  53.4 16.3 %collective-permute-start.13 = (bf16[512,512]{1,0:T(8,128)(2,1)}, bf16[512,512]{1,0:T(8,128)(2,1)S(1)}, u32[]{:S(2)}, u32[]{:S(2)}) collective-permute-start(bf16[512,512]{1,0:T(8,128)(2,1)} %bitcast.5), channel_id=1, source_target_pairs={{0,0},{1,16},{2,2},{3,18},{4,4},{5,20},{6,6},{7,22},{8,8},{9,24},{... | collective-permute-start | bytes 1572872 | tf_op jit(solution)/shard_map/ppermute | solution.py:620
  74.8 25.6 %collective-permute-start.14 = (bf16[1024,512]{1,0:T(8,128)(2,1)S(1)}, bf16[1024,512]{1,0:T(8,128)(2,1)}, u32[]{:S(2)}, u32[]{:S(2)}) collective-permute-start(bf16[1024,512]{1,0:T(8,128)(2,1)S(1)} %normed.1.own_ref.refs_1_), channel_id=1, source_target_pairs={{0,8},{1,9},{2,10},{3,11},{4,12},{5,13},{6,14},{7,15},{8,0},{9,1},... | collective-permute-start | bytes 3145736 | tf_op jit(solution)/shard_map/ppermute | solution.py:620
  100.4 25.9 %collective-permute-start.18 = (bf16[1024,512]{1,0:T(8,128)(2,1)}, bf16[1024,512]{1,0:T(8,128)(2,1)}, u32[]{:S(2)}, u32[]{:S(2)}) collective-permute-start(bf16[1024,512]{1,0:T(8,128)(2,1)} %constant_dynamic-update-slice_fusion.cot_own.refs_6_.rest_0_), channel_id=1, source_target_pairs={{0,8},{1,9},{2,10},{3,11},{4,12},{5,13},{6,14},{7,15},{8,0},{9,1},... | collective-permute-start | bytes 3145736 | tf_op jit(solution)/shard_map/ppermute | solution.py:620
  131.2 34.8 %collective-permute-start.19 = (bf16[1,32,32,512]{3,2,1,0:T(8,128)(2,1)}, bf16[1,32,32,512]{3,2,1,0:T(8,128)(2,1)S(1)}, u32[]{:S(2)}, u32[]{:S(2)}) collective-permute-start(bf16[1,32,32,512]{3,2,1,0:T(8,128)(2,1)} %bitcast.7), channel_id=1, source_target_pairs={{0,0},{1,16},{2,2},{3,18},{4,4},{5,20},{6,6},{7,22},{8,8},{9,24},{... | collective-permute-start | bytes 3145736 | tf_op jit(solution)/shard_map/ppermute | solution.py:620
  196.5 21.0 %collective-permute-start.32 = (bf16[8,13,16,256]{3,2,1,0:T(8,128)(2,1)S(1)}, bf16[8,13,16,256]{3,2,1,0:T(8,128)(2,1)S(1)}, u32[]{:S(2)}, u32[]{:S(2)}) collective-permute-start(bf16[8,13,16,256]{3,2,1,0:T(8,128)(2,1)S(1)} %get-tuple-element.235), channel_id=1, source_target_pairs={{0,4},{1,5},{2,6},{3,7},{4,0},{5,1},{6,2},{7,3},{8,12},{9,13},{10,... | collective-permute-start | bytes 2555912 | tf_op jit(solution)/shard_map/ppermute | solution.py:620
  198.1 20.6 %collective-permute-start.31 = (bf16[8,13,16,256]{3,2,1,0:T(8,128)(2,1)S(1)}, bf16[8,13,16,256]{3,2,1,0:T(8,128)(2,1)S(1)}, u32[]{:S(2)}, u32[]{:S(2)}) collective-permute-start(bf16[8,13,16,256]{3,2,1,0:T(8,128)(2,1)S(1)} %get-tuple-element.236), channel_id=1, source_target_pairs={{0,2},{1,3},{2,0},{3,1},{4,6},{5,7},{6,4},{7,5},{8,10},{9,11},{10,... | collective-permute-start | bytes 2555912 | tf_op jit(solution)/shard_map/ppermute | solution.py:620
  218.7 15.3 %collective-permute-start.33 = (bf16[2,16,9,16,256]{4,3,2,1,0:T(8,128)(2,1)S(1)}, bf16[2,16,9,16,256]{4,3,2,1,0:T(8,128)(2,1)S(1)}, u32[]{:S(2)}, u32[]{:S(2)}) collective-permute-start(bf16[2,16,9,16,256]{4,3,2,1,0:T(8,128)(2,1)S(1)} %get-tuple-element.176), channel_id=1, source_target_pairs={{0,1},{1,0},{2,3},{3,2},{4,5},{5,4},{6,7},{7,6},{8,9},{9,8},{10,11... | collective-permute-start | bytes 7077896 | tf_op jit(solution)/shard_map/ppermute | solution.py:620
  234.8 15.1 %collective-permute-start.35 = (bf16[8,9,16,256]{3,2,1,0:T(8,128)(2,1)S(1)}, bf16[8,9,16,256]{3,2,1,0:T(8,128)(2,1)S(1)}, u32[]{:S(2)}, u32[]{:S(2)}) collective-permute-start(bf16[8,9,16,256]{3,2,1,0:T(8,128)(2,1)S(1)} %get-tuple-element.239), channel_id=1, source_target_pairs={{0,4},{1,5},{2,6},{3,7},{4,0},{5,1},{6,2},{7,3},{8,12},{9,13},{10,... | collective-permute-start | bytes 1769480 | tf_op jit(solution)/shard_map/ppermute | solution.py:620
  236.4 14.7 %collective-permute-start.34 = (bf16[8,9,16,256]{3,2,1,0:T(8,128)(2,1)S(1)}, bf16[8,9,16,256]{3,2,1,0:T(8,128)(2,1)S(1)}, u32[]{:S(2)}, u32[]{:S(2)}) collective-permute-start(bf16[8,9,16,256]{3,2,1,0:T(8,128)(2,1)S(1)} %get-tuple-element.240), channel_id=1, source_target_pairs={{0,2},{1,3},{2,0},{3,1},{4,6},{5,7},{6,4},{7,5},{8,10},{9,11},{10,... | collective-permute-start | bytes 1769480 | tf_op jit(solution)/shard_map/ppermute | solution.py:620
  237.2 14.3 %collective-permute-start.45 = (bf16[2,13,16,256]{3,2,1,0:T(8,128)(2,1)S(1)}, bf16[2,13,16,256]{3,2,1,0:T(8,128)(2,1)S(1)}, u32[]{:S(2)}, u32[]{:S(2)}) collective-permute-start(bf16[2,13,16,256]{3,2,1,0:T(8,128)(2,1)S(1)} %get-tuple-element.245), channel_id=1, source_target_pairs={{0,24},{1,25},{2,26},{3,27},{4,28},{5,29},{6,30},{7,31},{8,16},{9,... | collective-permute-start | bytes 638984 | tf_op jit(solution)/shard_map/ppermute | solution.py:620
  239.8 18.6 %collective-permute-start.43 = (bf16[2,13,16,256]{3,2,1,0:T(8,128)(2,1)S(1)}, bf16[2,13,16,256]{3,2,1,0:T(8,128)(2,1)S(1)}, u32[]{:S(2)}, u32[]{:S(2)}) collective-permute-start(bf16[2,13,16,256]{3,2,1,0:T(8,128)(2,1)S(1)} %get-tuple-element.247), channel_id=1, source_target_pairs={{0,16},{1,17},{2,18},{3,19},{4,20},{5,21},{6,22},{7,23},{8,24},{9,... | collective-permute-start | bytes 638984 | tf_op jit(solution)/shard_map/ppermute | solution.py:620
  240.1 18.2 %collective-permute-start.44 = (bf16[2,13,16,256]{3,2,1,0:T(8,128)(2,1)S(1)}, bf16[2,13,16,256]{3,2,1,0:T(8,128)(2,1)S(1)}, u32[]{:S(2)}, u32[]{:S(2)}) collective-permute-start(bf16[2,13,16,256]{3,2,1,0:T(8,128)(2,1)S(1)} %get-tuple-element.248), channel_id=1, source_target_pairs={{0,8},{1,9},{2,10},{3,11},{4,12},{5,13},{6,14},{7,15},{8,0},{9,1},... | collective-permute-start | bytes 638984 | tf_op jit(solution)/shard_map/ppermute | solution.py:620
  263.3 19.0 %collective-permute-start.49 = (bf16[30,16,256]{2,1,0:T(8,128)(2,1)S(1)}, bf16[30,16,256]{2,1,0:T(8,128)(2,1)S(1)}, u32[]{:S(2)}, u32[]{:S(2)}) collective-permute-start(bf16[30,16,256]{2,1,0:T(8,128)(2,1)S(1)} %pad_maximum_fusion.9), channel_id=1, source_target_pairs={{0,16},{1,17},{2,18},{3,19},{4,20},{5,21},{6,22},{7,23},{8,24},{9,... | collective-permute-start | bytes 737288 | tf_op jit(solution)/shard_map/ppermute | solution.py:620
  282.6 14.9 %collective-permute-start.55 = (bf16[4,17,16,256]{3,2,1,0:T(8,128)(2,1)S(1)}, bf16[4,17,16,256]{3,2,1,0:T(8,128)(2,1)S(1)}, u32[]{:S(2)}, u32[]{:S(2)}) collective-permute-start(bf16[4,17,16,256]{3,2,1,0:T(8,128)(2,1)S(1)} %pad_maximum_fusion.8), channel_id=1, source_target_pairs={{0,4},{1,5},{2,6},{3,7},{4,0},{5,1},{6,2},{7,3},{8,12},{9,13},{10,... | collective-permute-start | bytes 1671176 | tf_op jit(solution)/shard_map/ppermute | solution.py:620
  297.6 25.5 %collective-permute-start.59 = (bf16[8,17,16,256]{3,2,1,0:T(8,128)(2,1)S(1)}, bf16[8,17,16,256]{3,2,1,0:T(8,128)(2,1)S(1)}, u32[]{:S(2)}, u32[]{:S(2)}) collective-permute-start(bf16[8,17,16,256]{3,2,1,0:T(8,128)(2,1)S(1)} %pad_maximum_fusion.1), channel_id=1, source_target_pairs={{0,2},{1,3},{2,0},{3,1},{4,6},{5,7},{6,4},{7,5},{8,10},{9,11},{10,... | collective-permute-start | bytes 3342344 | tf_op jit(solution)/shard_map/ppermute | solution.py:620
  299.3 19.5 %collective-permute-start.60 = (bf16[8,13,16,256]{3,2,1,0:T(8,128)(2,1)S(1)}, bf16[8,13,16,256]{3,2,1,0:T(8,128)(2,1)S(1)}, u32[]{:S(2)}, u32[]{:S(2)}) collective-permute-start(bf16[8,13,16,256]{3,2,1,0:T(8,128)(2,1)S(1)} %pad_maximum_fusion.4), channel_id=1, source_target_pairs={{0,4},{1,5},{2,6},{3,7},{4,0},{5,1},{6,2},{7,3},{8,12},{9,13},{10,... | collective-permute-start | bytes 2555912 | tf_op jit(solution)/shard_map/ppermute | solution.py:620
  329.3 24.0 %collective-permute-start.64 = (bf16[1,32,32,512]{3,2,1,0:T(8,128)(2,1)S(1)}, bf16[1,32,32,512]{3,2,1,0:T(8,128)(2,1)S(1)}, u32[]{:S(2)}, u32[]{:S(2)}) collective-permute-start(bf16[1,32,32,512]{3,2,1,0:T(8,128)(2,1)S(1)} %bitcast.108), channel_id=1, source_target_pairs={{0,0},{1,16},{2,2},{3,18},{4,4},{5,20},{6,6},{7,22},{8,8},{9,24},{... | collective-permute-start | bytes 3145736 | tf_op jit(solution)/shard_map/ppermute | solution.py:620
  337.9 14.6 %collective-permute-start.62 = (bf16[8,9,16,256]{3,2,1,0:T(8,128)(2,1)S(1)}, bf16[8,9,16,256]{3,2,1,0:T(8,128)(2,1)S(1)}, u32[]{:S(2)}, u32[]{:S(2)}) collective-permute-start(bf16[8,9,16,256]{3,2,1,0:T(8,128)(2,1)S(1)} %pad_maximum_fusion.7), channel_id=1, source_target_pairs={{0,4},{1,5},{2,6},{3,7},{4,0},{5,1},{6,2},{7,3},{8,12},{9,13},{10,... | collective-permute-start | bytes 1769480 | tf_op jit(solution)/shard_map/ppermute | solution.py:620
  338.6 14.3 %collective-permute-start.61 = (bf16[8,9,16,256]{3,2,1,0:T(8,128)(2,1)S(1)}, bf16[8,9,16,256]{3,2,1,0:T(8,128)(2,1)S(1)}, u32[]{:S(2)}, u32[]{:S(2)}) collective-permute-start(bf16[8,9,16,256]{3,2,1,0:T(8,128)(2,1)S(1)} %pad_maximum_fusion.6), channel_id=1, source_target_pairs={{0,2},{1,3},{2,0},{3,1},{4,6},{5,7},{6,4},{7,5},{8,10},{9,11},{10,... | collective-permute-start | bytes 1769480 | tf_op jit(solution)/shard_map/ppermute | solution.py:620
  (115 other events, 1115.7 us)

commit v5 on v4

--- a/solution.py
+++ b/solution.py
@@ -16,7 +16,7 @@
 PIECES = 32
 LIMITS = {
     "conv_one": 46, "conv_two": 46, "weight_two_grad": 24, "weight_one_grad": 20, "conv_two_back": 36, "conv_one_back": 36,
-    "attend": 40, "attend_first": 32, "key_value_grad": 60, "early": 14, "matrix_grad": 16, "unpack_two": 40, "unpack_one": 16,
+    "attend": 40, "attend_first": 32, "key_value_grad": 46, "early": 14, "matrix_grad": 16, "unpack_two": 40, "unpack_one": 16,
     "first": 8, "masks": 12, "normed": 8, "output": 8, "image_grad": 12,
 }
 

time: 376 us -> 369 us (0.981)
    unnamed x149 -> x155, local copies, waits for them, and re-layouts: 20.2 us -> 16.7 us
where the time goes in v5:
time: 369 us; the launch traced here: 363 us
  Pallas kernels  142 us (38%)
  waiting for transfers between devices  112 us (30%)
  starting transfers between devices  72.9 us (20%)
  local copies, waits for them, and re-layouts  20.3 us (6%)
  other arithmetic  13.1 us (4%)
    pallas_call x18, Pallas kernels, call(): pl.pallas_call(run if after else kernel, in_specs=list(in_specs) + [pl.Bl...  142 us
    ppermute x66, waiting for transfers between devices, permute(): lax.ppermute(x, ('seq', 'batch'), [(i, to(i)) for i in range(devices)])  112 us
    ppermute x66, starting transfers between devices, permute(): lax.ppermute(x, ('seq', 'batch'), [(i, to(i)) for i in range(devices)])  72.9 us
    unnamed x155, local copies, waits for them, and re-layouts  16.7 us
  transfers between devices with their start and end apart: 66, of which 34 were waited for; matrix products, arithmetic and copies ran while one was open for 3% of the time, Pallas kernels for 35%

profile of v5, /device:TPU:0, one launch (start us, length us, event | category | flops | bytes accessed | tf_op | source)
XLA Modules:
  0.0 362.7 jit_solution(9561553619212366206)
XLA Ops:
  4.4 4.2 %collective-permute-start.1 = (f32[8,512]{1,0:T(8,128)S(1)}, f32[8,512]{1,0:T(8,128)S(1)}, u32[]{:S(2)}, u32[]{:S(2)}) collective-permute-start(f32[8,512]{1,0:T(8,128)S(1)} %get-tuple-element.279), channel_id=1, source_target_pairs={{0,1},{1,0},{2,3},{3,2},{4,5},{5,4},{6,7},{7,6},{8,9},{9,8},{10,11... | collective-permute-start | bytes 49160 | tf_op jit(solution)/shard_map/ppermute | solution.py:620
  17.7 15.8 %collective-permute-done.4.pair_ref.refs_4_.refs_8_.refs_9_ = f32[8,512]{1,0:T(8,128)S(1)} collective-permute-done((f32[8,512]{1,0:T(8,128)S(1)}, f32[8,512]{1,0:T(8,128)S(1)}, u32[]{:S(2)}, u32[]{:S(2)}) %collective-permute-start.4) | collective-permute-done | bytes 16416 | tf_op jit(solution)/shard_map/ppermute | solution.py:620
  36.1 9.2 %conv_one.1 = (f32[1024,512]{1,0:T(8,128)S(1)}, bf16[1024,512]{1,0:T(8,128)(2,1)S(1)}, f32[40,512]{1,0:T(8,128)S(1)}, f32[40,512]{1,0:T(8,128)S(1)}, f32[8,512]{1,0:T(8,128)S(1)}) custom-call(s32[1]{0:T(128)} %bitcast.refs_2_.refs_0_.side_ref, bf16[1024,512]{1,0:T(8,128)(2,1)S(1)} %collective-permute-done.refs_1_.refs_9_.refs_4_.refs_5_, ...), custom_call_target="tpu_custom_call" | custom-call | flops 4831838208 | bytes 16384004 | tf_op jit(solution)/shard_map/conv_one/pallas_call | solution.py:668
  56.7 10.1 %conv_two.1 = (f32[1024,512]{1,0:T(8,128)S(1)}, bf16[1024,512]{1,0:T(8,128)(2,1)S(1)}, f32[40,512]{1,0:T(8,128)S(1)}, f32[40,512]{1,0:T(8,128)S(1)}, f32[8,512]{1,0:T(8,128)S(1)}) custom-call(s32[1]{0:T(128)} %bitcast.refs_2_.refs_0_.side_ref, f32[1024,512]{1,0:T(8,128)S(1)} %get-tuple-element.126.refs_1_.x_ref, ...), custom_call_target="tpu_custom_call" | custom-call | flops 4831838208 | bytes 18481156 | tf_op jit(solution)/shard_map/conv_two/pallas_call | solution.py:668
  80.7 6.4 %early.1 = (bf16[1024,512]{1,0:T(8,128)(2,1)S(1)}, bf16[1024,512]{1,0:T(8,128)(2,1)S(1)}, bf16[1024,512]{1,0:T(8,128)(2,1)S(1)}, bf16[1024,512]{1,0:T(8,128)(2,1...) custom-call(bf16[1024,512]{1,0:T(8,128)(2,1)S(1)} %normed.1.own_ref., ...), custom_call_target="tpu_custom_call" | custom-call | flops 4294967296 | bytes 14696448 | tf_op jit(solution)/shard_map/early/pallas_call | solution.py:668
  89.3 6.7 %attend_first.1 = (bf16[1024,2048]{1,0:T(8,128)(2,1)S(1)}, f32[1024,128]{1,0:T(8,128)S(1)}, f32[1024,128]{1,0:T(8,128)S(1)}, f32[1024,512]{1,0:T(8,128)S(1)}) custom-call(bf16[1024,512]{1,0:T(8,128)(2,1)S(1)} %get-tuple-element.136.keys_own.keys, bf16[1024,512]{1,0:T(8,128)(2,1)S(1)} %get-tuple-element.137.values_own.values, ...), custom_call_target="tpu_custom_call" | custom-call | flops 4294967296 | bytes 13123584 | tf_op jit(solution)/shard_map/attend_first/pallas_call | solution.py:668
  103.2 21.8 %attend.1 = (bf16[1024,512]{1,0:T(8,128)(2,1)S(1)}, bf16[1024,512]{1,0:T(8,128)(2,1)S(1)}, f32[2,8,512]{2,1,0:T(8,128)}) custom-call(bf16[1024,512]{1,0:T(8,128)(2,1)} %collective-permute-done.14.near_ref.near_hbm, bf16[1024,512]{1,0:T(8,128)(2,1)S(1)} %collective-permute-done.17.cross_ref.cross_hbm, bf16[1024,512]{1,0:T(8,128)(2,1)S(1)} %get-tuple-element.136.keys_own.keys, ...), custom_call_target="tpu_custom_call" | custom-call | flops 19327352832 | bytes 19988480 | tf_op jit(solution)/shard_map/attend/pallas_call | solution.py:668
  132.0 28.6 %key_value_grad.1 = (bf16[1024,512]{1,0:T(8,128)(2,1)S(1)}, bf16[1024,512]{1,0:T(8,128)(2,1)S(1)}, f32[1024,512]{1,0:T(8,128)}, f32[40,512]{1,0:T(8,128)S(1)}, f...) custom-call(s32[1]{0:T(128)} %bitcast.refs_2_.refs_0_.side_ref, ...), custom_call_target="tpu_custom_call" | custom-call | flops 20937965568 | bytes 21020676 | tf_op jit(solution)/shard_map/key_value_grad/pallas_call | solution.py:668
  163.3 4.2 %matrix_grad.1 = (bf16[2,16,4,16,256]{4,3,2,1,0:T(8,128)(2,1)S(1)}, bf16[2,16,4,16,256]{4,3,2,1,0:T(8,128)(2,1)S(1)}, f32[8,512]{1,0:T(8,128)S(1)}) custom-call(s32[3]{0:T(128)S(1)} %pad_add_fusion.1.refs_0_.place_ref, bf16[1024,512]{1,0:T(8,128)(2,1)S(1)} %copy-done.6, bf16[1024,512]{1,0:T(8,128)(2,1)S(1)} %copy-done.53, ...), custom_call_target="tpu_custom_call" | custom-call | flops 2147483648 | bytes 8405004 | tf_op jit(solution)/shard_map/matrix_grad/pallas_call | solution.py:668
  167.7 10.1 %weight_two_grad.1 = (bf16[2,16,13,16,256]{4,3,2,1,0:T(8,128)(2,1)S(1)}, bf16[2,16,13,16,256]{4,3,2,1,0:T(8,128)(2,1)S(1)}, bf16[3,1088,512]{2,1,0:T(8,128)(2,1)...) custom-call(s32[3]{0:T(128)S(1)} %pad_add_fusion.1.refs_0_.place_ref, s32[1]{0:T(128)} %bitcast.refs_2_.refs_0_.side_ref, ...), custom_call_target="tpu_custom_call" | custom-call | flops 4831838208 | bytes 27787280 | tf_op jit(solution)/shard_map/weight_two_grad/pallas_call | solution.py:668
  178.6 10.2 %conv_two_back.1 = (f32[1024,512]{1,0:T(8,128)S(1)}, f32[40,512]{1,0:T(8,128)S(1)}, f32[40,512]{1,0:T(8,128)S(1)}, f32[8,512]{1,0:T(8,128)S(1)}, f32[8,512]{1,0:T(8,128)S(1)}) custom-call(s32[1]{0:T(128)} %bitcast.refs_2_.refs_0_.side_ref, bf16[3,1088,512]{2,1,0:T(8,128)(2,1)S(1)} %get-tuple-element.165.shifted, bf16[9,1024,128]{2,1,0:T(8,128)(2,1)S(1)} %copy-done.29, ...), custom_call_target="tpu_custom_call" | custom-call | flops 4831838208 | bytes 19742724 | tf_op jit(solution)/shard_map/conv_two_back/pallas_call | solution.py:668
  199.0 8.5 %weight_one_grad.1 = (bf16[2,16,9,16,256]{4,3,2,1,0:T(8,128)(2,1)S(1)}, bf16[2,16,9,16,256]{4,3,2,1,0:T(8,128)(2,1)S(1)}, bf16[3,1088,512]{2,1,0:T(8,128)(2,1)S(1)}, f32[8,512]{1,0:T(8,128)S(1)}) custom-call(s32[3]{0:T(128)S(1)} %pad_add_fusion.1.refs_0_.place_ref, s32[1]{0:T(128)} %bitcast.refs_2_.refs_0_.side_ref, f32[1024,512]{1,0:T(8,128)S(1)} %copy-done.51, ...), custom_call_target="tpu_custom_call" | custom-call | flops 4831838208 | bytes 16252944 | tf_op jit(solution)/shard_map/weight_one_grad/pallas_call | solution.py:668
  215.1 9.9 %conv_one_back.1 = (f32[1024,512]{1,0:T(8,128)S(1)}, f32[40,512]{1,0:T(8,128)S(1)}, f32[40,512]{1,0:T(8,128)S(1)}, f32[8,512]{1,0:T(8,128)S(1)}, f32[8,512]{1,0:T(8,128)S(1)}) custom-call(s32[1]{0:T(128)} %bitcast.refs_2_.refs_0_.side_ref, bf16[3,1088,512]{2,1,0:T(8,128)(2,1)S(1)} %get-tuple-element.177.refs_1_, bf16[9,1024,128]{2,1,0:T(8,128)(2,1)S(1)} %copy-done.29, ...), custom_call_target="tpu_custom_call" | custom-call | flops 4831838208 | bytes 18694148 | tf_op jit(solution)/shard_map/conv_one_back/pallas_call | solution.py:668
  235.7 7.4 %collective-permute-done.35 = bf16[8,9,16,256]{3,2,1,0:T(8,128)(2,1)S(1)} collective-permute-done((bf16[8,9,16,256]{3,2,1,0:T(8,128)(2,1)S(1)}, bf16[8,9,16,256]{3,2,1,0:T(8,128)(2,1)S(1)}, u32[]{:S(2)}, u32[]{:S(2)}) %collective-permute-start.35) | collective-permute-done | bytes 589856 | tf_op jit(solution)/shard_map/ppermute | solution.py:620
  244.7 6.8 %collective-permute-done.43 = bf16[2,13,16,256]{3,2,1,0:T(8,128)(2,1)S(1)} collective-permute-done((bf16[2,13,16,256]{3,2,1,0:T(8,128)(2,1)S(1)}, bf16[2,13,16,256]{3,2,1,0:T(8,128)(2,1)S(1)}, u32[]{:S(2)}, u32[]{:S(2)}) %collective-permute-start.43) | collective-permute-done | bytes 213024 | tf_op jit(solution)/shard_map/ppermute | solution.py:620
  264.6 5.4 %collective-permute-done.50 = bf16[30,16,256]{2,1,0:T(8,128)(2,1)S(1)} collective-permute-done((bf16[30,16,256]{2,1,0:T(8,128)(2,1)S(1)}, bf16[30,16,256]{2,1,0:T(8,128)(2,1)S(1)}, u32[]{:S(2)}, u32[]{:S(2)}) %collective-permute-start.50) | collective-permute-done | bytes 245792 | tf_op jit(solution)/shard_map/ppermute | solution.py:620
  270.0 5.7 %collective-permute-done.49 = bf16[30,16,256]{2,1,0:T(8,128)(2,1)S(1)} collective-permute-done((bf16[30,16,256]{2,1,0:T(8,128)(2,1)S(1)}, bf16[30,16,256]{2,1,0:T(8,128)(2,1)S(1)}, u32[]{:S(2)}, u32[]{:S(2)}) %collective-permute-start.49) | collective-permute-done | bytes 245792 | tf_op jit(solution)/shard_map/ppermute | solution.py:620
  286.2 4.4 %collective-permute-done.46 = bf16[2,9,16,256]{3,2,1,0:T(8,128)(2,1)S(1)} collective-permute-done((bf16[2,9,16,256]{3,2,1,0:T(8,128)(2,1)S(1)}, bf16[2,9,16,256]{3,2,1,0:T(8,128)(2,1)S(1)}, u32[]{:S(2)}, u32[]{:S(2)}) %collective-permute-start.46) | collective-permute-done | bytes 147488 | tf_op jit(solution)/shard_map/ppermute | solution.py:620
  297.4 4.3 %collective-permute-done.54 = bf16[2,9,16,256]{3,2,1,0:T(8,128)(2,1)S(1)} collective-permute-done((bf16[2,9,16,256]{3,2,1,0:T(8,128)(2,1)S(1)}, bf16[2,9,16,256]{3,2,1,0:T(8,128)(2,1)S(1)}, u32[]{:S(2)}, u32[]{:S(2)}) %collective-permute-start.54) | collective-permute-done | bytes 147488 | tf_op jit(solution)/shard_map/ppermute | solution.py:620
  306.8 5.1 %collective-permute-done.60 = bf16[8,13,16,256]{3,2,1,0:T(8,128)(2,1)S(1)} collective-permute-done((bf16[8,13,16,256]{3,2,1,0:T(8,128)(2,1)S(1)}, bf16[8,13,16,256]{3,2,1,0:T(8,128)(2,1)S(1)}, u32[]{:S(2)}, u32[]{:S(2)}) %collective-permute-start.60) | collective-permute-done | bytes 852000 | tf_op jit(solution)/shard_map/ppermute | solution.py:620
  323.1 6.6 %collective-permute-done.58 = bf16[4,9,16,256]{3,2,1,0:T(8,128)(2,1)S(1)} collective-permute-done((bf16[4,9,16,256]{3,2,1,0:T(8,128)(2,1)S(1)}, bf16[4,9,16,256]{3,2,1,0:T(8,128)(2,1)S(1)}, u32[]{:S(2)}, u32[]{:S(2)}) %collective-permute-start.58) | collective-permute-done | bytes 294944 | tf_op jit(solution)/shard_map/ppermute | solution.py:620
  332.6 6.8 %unpack_two.1 = (f32[18,512,512]{2,1,0:T(8,128)}, f32[2,512,512]{2,1,0:T(8,128)}, f32[512,512]{1,0:T(8,128)}, f32[512,512]{1,0:T(8,128)}) custom-call(s32[3]{0:T(128)S(1)} %pad_add_fusion.1.refs_0_.place_ref, bf16[16,30,16,256]{3,2,1,0:T(8,128)(2,1)S(1)} %maximum_maximum_fusion.own_ref, bf16[16,30,16,256]{3,2,1,0:T(8,128)(2,1)S(1)} %collective-permute-done.63.other_ref), custom_call_target="tpu_custom_call" | custom-call | bytes 30933004 | tf_op jit(solution)/shard_map/unpack_two/pallas_call | solution.py:668
  339.4 6.3 %collective-permute-done.62 = bf16[8,9,16,256]{3,2,1,0:T(8,128)(2,1)S(1)} collective-permute-done((bf16[8,9,16,256]{3,2,1,0:T(8,128)(2,1)S(1)}, bf16[8,9,16,256]{3,2,1,0:T(8,128)(2,1)S(1)}, u32[]{:S(2)}, u32[]{:S(2)}) %collective-permute-start.62) | collective-permute-done | bytes 589856 | tf_op jit(solution)/shard_map/ppermute | solution.py:620
  354.5 5.2 %unpack_one.1 = f32[18,512,512]{2,1,0:T(8,128)} custom-call(s32[3]{0:T(128)S(1)} %copy-done.27, bf16[2,16,9,16,256]{4,3,2,1,0:T(8,128)(2,1)S(1)} %pad_maximum_fusion.own_ref, bf16[2,16,9,16,256]{4,3,2,1,0:T(8,128)(2,1)} %collective-permute-done.65.other_ref, f32[18,512,512]{2,1,0:T(8,128)} %get-tuple-element.230.rest_0_), custom_call_target="tpu_custom_call", output_to_operand_aliasing={{}: (3, {})} | custom-call | bytes 42467340 | tf_op jit(solution)/shard_map/unpack_one/pallas_call | solution.py:668
  (337 shorter events, 150.6 us)
Async XLA Ops:
  0.7 34.7 %collective-permute-start = (bf16[1024,512]{1,0:T(8,128)(2,1)}, bf16[1024,512]{1,0:T(8,128)(2,1)S(1)}, u32[]{:S(2)}, u32[]{:S(2)}) collective-permute-start(bf16[1024,512]{1,0:T(8,128)(2,1)} %bitcast.106), channel_id=1, source_target_pairs={{0,0},{1,16},{2,2},{3,18},{4,4},{5,20},{6,6},{7,22},{8,8},{9,24},{... | collective-permute-start | bytes 3145736 | tf_op jit(solution)/shard_map/ppermute | solution.py:620
  13.4 20.1 %collective-permute-start.4 = (f32[8,512]{1,0:T(8,128)S(1)}, f32[8,512]{1,0:T(8,128)S(1)}, u32[]{:S(2)}, u32[]{:S(2)}) collective-permute-start(f32[8,512]{1,0:T(8,128)S(1)} %get-tuple-element.124), channel_id=1, source_target_pairs={{0,1},{1,17},{2,3},{3,19},{4,5},{5,21},{6,7},{7,23},{8,9},{9,25},{... | collective-permute-start | bytes 49160 | tf_op jit(solution)/shard_map/ppermute | solution.py:620
  14.7 18.8 %collective-permute-start.2 = (f32[40,512]{1,0:T(8,128)S(1)}, f32[40,512]{1,0:T(8,128)S(1)}, u32[]{:S(2)}, u32[]{:S(2)}) collective-permute-start(f32[40,512]{1,0:T(8,128)S(1)} %get-tuple-element.122), channel_id=1, source_target_pairs={{0,8},{1,24},{2,10},{3,26},{4,12},{5,28},{6,14},{7,30},{8,0},{9,16... | collective-permute-start | bytes 245768 | tf_op jit(solution)/shard_map/ppermute | solution.py:620
  16.3 17.2 %collective-permute-start.3 = (f32[40,512]{1,0:T(8,128)S(1)}, f32[40,512]{1,0:T(8,128)S(1)}, u32[]{:S(2)}, u32[]{:S(2)}) collective-permute-start(f32[40,512]{1,0:T(8,128)S(1)} %get-tuple-element.123), channel_id=1, source_target_pairs={{0,9},{1,25},{2,11},{3,27},{4,13},{5,29},{6,15},{7,31},{8,1},{9,17... | collective-permute-start | bytes 245768 | tf_op jit(solution)/shard_map/ppermute | solution.py:620
  35.4 17.9 %collective-permute-start.9 = (bf16[512,512]{1,0:T(8,128)(2,1)S(1)}, bf16[512,512]{1,0:T(8,128)(2,1)S(1)}, u32[]{:S(2)}, u32[]{:S(2)}) collective-permute-start(bf16[512,512]{1,0:T(8,128)(2,1)S(1)} %bitcast.116), channel_id=1, source_target_pairs={{0,0},{1,16},{2,2},{3,18},{4,4},{5,20},{6,6},{7,22},{8,8},{9,24},{... | collective-permute-start | bytes 1572872 | tf_op jit(solution)/shard_map/ppermute | solution.py:620
  53.3 16.3 %collective-permute-start.13 = (bf16[512,512]{1,0:T(8,128)(2,1)}, bf16[512,512]{1,0:T(8,128)(2,1)S(1)}, u32[]{:S(2)}, u32[]{:S(2)}) collective-permute-start(bf16[512,512]{1,0:T(8,128)(2,1)} %bitcast.5), channel_id=1, source_target_pairs={{0,0},{1,16},{2,2},{3,18},{4,4},{5,20},{6,6},{7,22},{8,8},{9,24},{... | collective-permute-start | bytes 1572872 | tf_op jit(solution)/shard_map/ppermute | solution.py:620
  74.8 25.6 %collective-permute-start.14 = (bf16[1024,512]{1,0:T(8,128)(2,1)S(1)}, bf16[1024,512]{1,0:T(8,128)(2,1)}, u32[]{:S(2)}, u32[]{:S(2)}) collective-permute-start(bf16[1024,512]{1,0:T(8,128)(2,1)S(1)} %normed.1.own_ref.refs_1_), channel_id=1, source_target_pairs={{0,8},{1,9},{2,10},{3,11},{4,12},{5,13},{6,14},{7,15},{8,0},{9,1},... | collective-permute-start | bytes 3145736 | tf_op jit(solution)/shard_map/ppermute | solution.py:620
  100.3 25.9 %collective-permute-start.18 = (bf16[1024,512]{1,0:T(8,128)(2,1)}, bf16[1024,512]{1,0:T(8,128)(2,1)}, u32[]{:S(2)}, u32[]{:S(2)}) collective-permute-start(bf16[1024,512]{1,0:T(8,128)(2,1)} %constant_dynamic-update-slice_fusion.cot_own.refs_6_.rest_0_), channel_id=1, source_target_pairs={{0,8},{1,9},{2,10},{3,11},{4,12},{5,13},{6,14},{7,15},{8,0},{9,1},... | collective-permute-start | bytes 3145736 | tf_op jit(solution)/shard_map/ppermute | solution.py:620
  130.3 32.9 %collective-permute-start.19 = (bf16[1,32,32,512]{3,2,1,0:T(8,128)(2,1)S(1)}, bf16[1,32,32,512]{3,2,1,0:T(8,128)(2,1)S(1)}, u32[]{:S(2)}, u32[]{:S(2)}) collective-permute-start(bf16[1,32,32,512]{3,2,1,0:T(8,128)(2,1)S(1)} %bitcast.108), channel_id=1, source_target_pairs={{0,0},{1,16},{2,2},{3,18},{4,4},{5,20},{6,6},{7,22},{8,8},{9,24},{... | collective-permute-start | bytes 3145736 | tf_op jit(solution)/shard_map/ppermute | solution.py:620
  190.0 21.0 %collective-permute-start.32 = (bf16[8,13,16,256]{3,2,1,0:T(8,128)(2,1)S(1)}, bf16[8,13,16,256]{3,2,1,0:T(8,128)(2,1)S(1)}, u32[]{:S(2)}, u32[]{:S(2)}) collective-permute-start(bf16[8,13,16,256]{3,2,1,0:T(8,128)(2,1)S(1)} %get-tuple-element.235), channel_id=1, source_target_pairs={{0,4},{1,5},{2,6},{3,7},{4,0},{5,1},{6,2},{7,3},{8,12},{9,13},{10,... | collective-permute-start | bytes 2555912 | tf_op jit(solution)/shard_map/ppermute | solution.py:620
  191.6 20.6 %collective-permute-start.31 = (bf16[8,13,16,256]{3,2,1,0:T(8,128)(2,1)S(1)}, bf16[8,13,16,256]{3,2,1,0:T(8,128)(2,1)S(1)}, u32[]{:S(2)}, u32[]{:S(2)}) collective-permute-start(bf16[8,13,16,256]{3,2,1,0:T(8,128)(2,1)S(1)} %get-tuple-element.236), channel_id=1, source_target_pairs={{0,2},{1,3},{2,0},{3,1},{4,6},{5,7},{6,4},{7,5},{8,10},{9,11},{10,... | collective-permute-start | bytes 2555912 | tf_op jit(solution)/shard_map/ppermute | solution.py:620
  212.2 14.9 %collective-permute-start.33 = (bf16[2,16,9,16,256]{4,3,2,1,0:T(8,128)(2,1)S(1)}, bf16[2,16,9,16,256]{4,3,2,1,0:T(8,128)(2,1)S(1)}, u32[]{:S(2)}, u32[]{:S(2)}) collective-permute-start(bf16[2,16,9,16,256]{4,3,2,1,0:T(8,128)(2,1)S(1)} %get-tuple-element.176), channel_id=1, source_target_pairs={{0,1},{1,0},{2,3},{3,2},{4,5},{5,4},{6,7},{7,6},{8,9},{9,8},{10,11... | collective-permute-start | bytes 7077896 | tf_op jit(solution)/shard_map/ppermute | solution.py:620
  228.0 15.1 %collective-permute-start.35 = (bf16[8,9,16,256]{3,2,1,0:T(8,128)(2,1)S(1)}, bf16[8,9,16,256]{3,2,1,0:T(8,128)(2,1)S(1)}, u32[]{:S(2)}, u32[]{:S(2)}) collective-permute-start(bf16[8,9,16,256]{3,2,1,0:T(8,128)(2,1)S(1)} %get-tuple-element.239), channel_id=1, source_target_pairs={{0,4},{1,5},{2,6},{3,7},{4,0},{5,1},{6,2},{7,3},{8,12},{9,13},{10,... | collective-permute-start | bytes 1769480 | tf_op jit(solution)/shard_map/ppermute | solution.py:620
  229.6 14.7 %collective-permute-start.34 = (bf16[8,9,16,256]{3,2,1,0:T(8,128)(2,1)S(1)}, bf16[8,9,16,256]{3,2,1,0:T(8,128)(2,1)S(1)}, u32[]{:S(2)}, u32[]{:S(2)}) collective-permute-start(bf16[8,9,16,256]{3,2,1,0:T(8,128)(2,1)S(1)} %get-tuple-element.240), channel_id=1, source_target_pairs={{0,2},{1,3},{2,0},{3,1},{4,6},{5,7},{6,4},{7,5},{8,10},{9,11},{10,... | collective-permute-start | bytes 1769480 | tf_op jit(solution)/shard_map/ppermute | solution.py:620
  230.5 14.2 %collective-permute-start.45 = (bf16[2,13,16,256]{3,2,1,0:T(8,128)(2,1)S(1)}, bf16[2,13,16,256]{3,2,1,0:T(8,128)(2,1)S(1)}, u32[]{:S(2)}, u32[]{:S(2)}) collective-permute-start(bf16[2,13,16,256]{3,2,1,0:T(8,128)(2,1)S(1)} %get-tuple-element.245), channel_id=1, source_target_pairs={{0,24},{1,25},{2,26},{3,27},{4,28},{5,29},{6,30},{7,31},{8,16},{9,... | collective-permute-start | bytes 638984 | tf_op jit(solution)/shard_map/ppermute | solution.py:620
  233.1 18.5 %collective-permute-start.43 = (bf16[2,13,16,256]{3,2,1,0:T(8,128)(2,1)S(1)}, bf16[2,13,16,256]{3,2,1,0:T(8,128)(2,1)S(1)}, u32[]{:S(2)}, u32[]{:S(2)}) collective-permute-start(bf16[2,13,16,256]{3,2,1,0:T(8,128)(2,1)S(1)} %get-tuple-element.247), channel_id=1, source_target_pairs={{0,16},{1,17},{2,18},{3,19},{4,20},{5,21},{6,22},{7,23},{8,24},{9,... | collective-permute-start | bytes 638984 | tf_op jit(solution)/shard_map/ppermute | solution.py:620
  233.4 18.2 %collective-permute-start.44 = (bf16[2,13,16,256]{3,2,1,0:T(8,128)(2,1)S(1)}, bf16[2,13,16,256]{3,2,1,0:T(8,128)(2,1)S(1)}, u32[]{:S(2)}, u32[]{:S(2)}) collective-permute-start(bf16[2,13,16,256]{3,2,1,0:T(8,128)(2,1)S(1)} %get-tuple-element.248), channel_id=1, source_target_pairs={{0,8},{1,9},{2,10},{3,11},{4,12},{5,13},{6,14},{7,15},{8,0},{9,1},... | collective-permute-start | bytes 638984 | tf_op jit(solution)/shard_map/ppermute | solution.py:620
  256.6 19.1 %collective-permute-start.49 = (bf16[30,16,256]{2,1,0:T(8,128)(2,1)S(1)}, bf16[30,16,256]{2,1,0:T(8,128)(2,1)S(1)}, u32[]{:S(2)}, u32[]{:S(2)}) collective-permute-start(bf16[30,16,256]{2,1,0:T(8,128)(2,1)S(1)} %pad_maximum_fusion.9), channel_id=1, source_target_pairs={{0,16},{1,17},{2,18},{3,19},{4,20},{5,21},{6,22},{7,23},{8,24},{9,... | collective-permute-start | bytes 737288 | tf_op jit(solution)/shard_map/ppermute | solution.py:620
  275.9 14.7 %collective-permute-start.55 = (bf16[4,17,16,256]{3,2,1,0:T(8,128)(2,1)S(1)}, bf16[4,17,16,256]{3,2,1,0:T(8,128)(2,1)S(1)}, u32[]{:S(2)}, u32[]{:S(2)}) collective-permute-start(bf16[4,17,16,256]{3,2,1,0:T(8,128)(2,1)S(1)} %pad_maximum_fusion.8), channel_id=1, source_target_pairs={{0,4},{1,5},{2,6},{3,7},{4,0},{5,1},{6,2},{7,3},{8,12},{9,13},{10,... | collective-permute-start | bytes 1671176 | tf_op jit(solution)/shard_map/ppermute | solution.py:620
  290.8 25.3 %collective-permute-start.59 = (bf16[8,17,16,256]{3,2,1,0:T(8,128)(2,1)S(1)}, bf16[8,17,16,256]{3,2,1,0:T(8,128)(2,1)S(1)}, u32[]{:S(2)}, u32[]{:S(2)}) collective-permute-start(bf16[8,17,16,256]{3,2,1,0:T(8,128)(2,1)S(1)} %pad_maximum_fusion.1), channel_id=1, source_target_pairs={{0,2},{1,3},{2,0},{3,1},{4,6},{5,7},{6,4},{7,5},{8,10},{9,11},{10,... | collective-permute-start | bytes 3342344 | tf_op jit(solution)/shard_map/ppermute | solution.py:620
  292.6 19.3 %collective-permute-start.60 = (bf16[8,13,16,256]{3,2,1,0:T(8,128)(2,1)S(1)}, bf16[8,13,16,256]{3,2,1,0:T(8,128)(2,1)S(1)}, u32[]{:S(2)}, u32[]{:S(2)}) collective-permute-start(bf16[8,13,16,256]{3,2,1,0:T(8,128)(2,1)S(1)} %pad_maximum_fusion.4), channel_id=1, source_target_pairs={{0,4},{1,5},{2,6},{3,7},{4,0},{5,1},{6,2},{7,3},{8,12},{9,13},{10,... | collective-permute-start | bytes 2555912 | tf_op jit(solution)/shard_map/ppermute | solution.py:620
  322.4 24.0 %collective-permute-start.64 = (bf16[1,32,32,512]{3,2,1,0:T(8,128)(2,1)S(1)}, bf16[1,32,32,512]{3,2,1,0:T(8,128)(2,1)S(1)}, u32[]{:S(2)}, u32[]{:S(2)}) collective-permute-start(bf16[1,32,32,512]{3,2,1,0:T(8,128)(2,1)S(1)} %bitcast.109), channel_id=1, source_target_pairs={{0,0},{1,16},{2,2},{3,18},{4,4},{5,20},{6,6},{7,22},{8,8},{9,24},{... | collective-permute-start | bytes 3145736 | tf_op jit(solution)/shard_map/ppermute | solution.py:620
  331.1 14.6 %collective-permute-start.62 = (bf16[8,9,16,256]{3,2,1,0:T(8,128)(2,1)S(1)}, bf16[8,9,16,256]{3,2,1,0:T(8,128)(2,1)S(1)}, u32[]{:S(2)}, u32[]{:S(2)}) collective-permute-start(bf16[8,9,16,256]{3,2,1,0:T(8,128)(2,1)S(1)} %pad_maximum_fusion.7), channel_id=1, source_target_pairs={{0,4},{1,5},{2,6},{3,7},{4,0},{5,1},{6,2},{7,3},{8,12},{9,13},{10,... | collective-permute-start | bytes 1769480 | tf_op jit(solution)/shard_map/ppermute | solution.py:620
  331.6 14.3 %collective-permute-start.61 = (bf16[8,9,16,256]{3,2,1,0:T(8,128)(2,1)S(1)}, bf16[8,9,16,256]{3,2,1,0:T(8,128)(2,1)S(1)}, u32[]{:S(2)}, u32[]{:S(2)}) collective-permute-start(bf16[8,9,16,256]{3,2,1,0:T(8,128)(2,1)S(1)} %pad_maximum_fusion.6), channel_id=1, source_target_pairs={{0,2},{1,3},{2,0},{3,1},{4,6},{5,7},{6,4},{7,5},{8,10},{9,11},{10,... | collective-permute-start | bytes 1769480 | tf_op jit(solution)/shard_map/ppermute | solution.py:620
  (118 other events, 1271.0 us)

commit v6 on v5

--- a/solution.py
+++ b/solution.py
@@ -188,10 +188,11 @@
 
 def conv_kernel(
     index, side_ref, x_ref, near_ref, cross_ref, pair_ref, stats_ref, rows_ref, mask_ref, weights, skip_ref,
-    out_ref, act_ref, near_out, cross_out, stats_out, frame, shifted, buffer, arrived,
+    out_ref, act_hbm, near_out, cross_out, stats_out, frame, shifted, buffer, arrived, stored,
 ):
     row = pl.program_id(0)
     pixels, channels = x_ref.shape
+    store_act = pltpu.make_async_copy(shifted.at[1, pl.ds(32, pixels), :], act_hbm, stored)
     copies = fetch_rows(weights, index, buffer, arrived, row, (0, 1, 2))
 
     @pl.when(row == 0)
@@ -211,7 +212,7 @@
         frame[40 + pixels : 72 + pixels, :] = act(jnp.where(side == 0, near, cross))
         frame[72 + pixels : 80 + pixels, :] = jnp.zeros((8, channels), F32)
         columns_of(frame, shifted, pixels + 64)
-        act_ref[...] = shifted[1, 32 : 32 + pixels, :]
+        store_act.start()
         start = jnp.broadcast_to(bias, (pixels, channels))
         if skip_ref is not None:
             start = start + skip_ref[...].astype(F32)
@@ -229,6 +230,7 @@
         stats = rows_of(mean, square)
         stats_out[...] = stats
         edges_out(side_ref, out_ref, near_out, cross_out, stats)
+        store_act.wait()
 
 
 def normed_kernel(x_ref, near_ref, cross_ref, pair_ref, stats_ref, rows_ref, out_ref):
@@ -729,9 +731,12 @@
             operands.append(skip)
         return call(
             kernel, name, operands, specs,
-            [(field, field_f32), (field, field_b16), row_out, row_out, stat_out],
+            [(field, field_f32), (IN_HBM, field_b16), row_out, row_out, stat_out],
             40, 9 * matmul,
-            [pltpu.VMEM((pixels + 80, channels), F32), pltpu.VMEM((3, pixels + 64, channels), BF16), *row_buffer],
+            [
+                pltpu.VMEM((pixels + 80, channels), F32), pltpu.VMEM((3, pixels + 64, channels), BF16), *row_buffer,
+                pltpu.SemaphoreType.DMA,
+            ],
             (3,), after,
         )
 

time: 369 us -> 369 us (level)
  no operation moved by 1% of the time
where the time goes in v6:
time: 369 us; the launch traced here: 363 us
  Pallas kernels  142 us (38%)
  waiting for transfers between devices  112 us (30%)
  starting transfers between devices  73.4 us (20%)
  local copies, waits for them, and re-layouts  20.3 us (6%)
  other arithmetic  13 us (4%)
    pallas_call x18, Pallas kernels, call(): pl.pallas_call(run if after else kernel, in_specs=list(in_specs) + [pl.Bl...  142 us
    ppermute x66, waiting for transfers between devices, permute(): lax.ppermute(x, ('seq', 'batch'), [(i, to(i)) for i in range(devices)])  112 us
    ppermute x66, starting transfers between devices, permute(): lax.ppermute(x, ('seq', 'batch'), [(i, to(i)) for i in range(devices)])  73.4 us
    unnamed x155, local copies, waits for them, and re-layouts  16.7 us
  transfers between devices with their start and end apart: 66, of which 34 were waited for; matrix products, arithmetic and copies ran while one was open for 3% of the time, Pallas kernels for 35%

profile of v6, /device:TPU:0, one launch (start us, length us, event | category | flops | bytes accessed | tf_op | source)
XLA Modules:
  0.0 363.1 jit_solution(11093247376675210041)
XLA Ops:
  17.7 15.8 %collective-permute-done.4.pair_ref.refs_4_.refs_8_.refs_9_ = f32[8,512]{1,0:T(8,128)S(1)} collective-permute-done((f32[8,512]{1,0:T(8,128)S(1)}, f32[8,512]{1,0:T(8,128)S(1)}, u32[]{:S(2)}, u32[]{:S(2)}) %collective-permute-start.4) | collective-permute-done | bytes 16416 | tf_op jit(solution)/shard_map/ppermute | solution.py:622
  36.1 9.3 %conv_one.1 = (f32[1024,512]{1,0:T(8,128)S(1)}, bf16[1024,512]{1,0:T(8,128)(2,1)S(1)}, f32[40,512]{1,0:T(8,128)S(1)}, f32[40,512]{1,0:T(8,128)S(1)}, f32[8,512]{1,0:T(8,128)S(1)}) custom-call(s32[1]{0:T(128)} %bitcast.refs_2_.refs_0_.side_ref, bf16[1024,512]{1,0:T(8,128)(2,1)S(1)} %collective-permute-done.refs_1_.refs_9_.refs_4_.refs_5_, ...), custom_call_target="tpu_custom_call" | custom-call | flops 4831838208 | bytes 16384004 | tf_op jit(solution)/shard_map/conv_one/pallas_call | solution.py:670
  56.7 10.0 %conv_two.1 = (f32[1024,512]{1,0:T(8,128)S(1)}, bf16[1024,512]{1,0:T(8,128)(2,1)S(1)}, f32[40,512]{1,0:T(8,128)S(1)}, f32[40,512]{1,0:T(8,128)S(1)}, f32[8,512]{1,0:T(8,128)S(1)}) custom-call(s32[1]{0:T(128)} %bitcast.refs_2_.refs_0_.side_ref, f32[1024,512]{1,0:T(8,128)S(1)} %get-tuple-element.126.refs_1_.x_ref, ...), custom_call_target="tpu_custom_call" | custom-call | flops 4831838208 | bytes 18481156 | tf_op jit(solution)/shard_map/conv_two/pallas_call | solution.py:670
  80.8 6.4 %early.1 = (bf16[1024,512]{1,0:T(8,128)(2,1)S(1)}, bf16[1024,512]{1,0:T(8,128)(2,1)S(1)}, bf16[1024,512]{1,0:T(8,128)(2,1)S(1)}, bf16[1024,512]{1,0:T(8,128)(2,1...) custom-call(bf16[1024,512]{1,0:T(8,128)(2,1)S(1)} %normed.1.own_ref., ...), custom_call_target="tpu_custom_call" | custom-call | flops 4294967296 | bytes 14696448 | tf_op jit(solution)/shard_map/early/pallas_call | solution.py:670
  89.3 6.7 %attend_first.1 = (bf16[1024,2048]{1,0:T(8,128)(2,1)S(1)}, f32[1024,128]{1,0:T(8,128)S(1)}, f32[1024,128]{1,0:T(8,128)S(1)}, f32[1024,512]{1,0:T(8,128)S(1)}) custom-call(bf16[1024,512]{1,0:T(8,128)(2,1)S(1)} %get-tuple-element.136.keys_own.keys, bf16[1024,512]{1,0:T(8,128)(2,1)S(1)} %get-tuple-element.137.values_own.values, ...), custom_call_target="tpu_custom_call" | custom-call | flops 4294967296 | bytes 13123584 | tf_op jit(solution)/shard_map/attend_first/pallas_call | solution.py:670
  103.3 21.8 %attend.1 = (bf16[1024,512]{1,0:T(8,128)(2,1)S(1)}, bf16[1024,512]{1,0:T(8,128)(2,1)S(1)}, f32[2,8,512]{2,1,0:T(8,128)}) custom-call(bf16[1024,512]{1,0:T(8,128)(2,1)} %collective-permute-done.14.near_ref.near_hbm, bf16[1024,512]{1,0:T(8,128)(2,1)S(1)} %collective-permute-done.17.cross_ref.cross_hbm, bf16[1024,512]{1,0:T(8,128)(2,1)S(1)} %get-tuple-element.136.keys_own.keys, ...), custom_call_target="tpu_custom_call" | custom-call | flops 19327352832 | bytes 19988480 | tf_op jit(solution)/shard_map/attend/pallas_call | solution.py:670
  132.0 28.6 %key_value_grad.1 = (bf16[1024,512]{1,0:T(8,128)(2,1)S(1)}, bf16[1024,512]{1,0:T(8,128)(2,1)S(1)}, f32[1024,512]{1,0:T(8,128)}, f32[40,512]{1,0:T(8,128)S(1)}, f...) custom-call(s32[1]{0:T(128)} %bitcast.refs_2_.refs_0_.side_ref, ...), custom_call_target="tpu_custom_call" | custom-call | flops 20937965568 | bytes 21020676 | tf_op jit(solution)/shard_map/key_value_grad/pallas_call | solution.py:670
  167.7 10.1 %weight_two_grad.1 = (bf16[2,16,13,16,256]{4,3,2,1,0:T(8,128)(2,1)S(1)}, bf16[2,16,13,16,256]{4,3,2,1,0:T(8,128)(2,1)S(1)}, bf16[3,1088,512]{2,1,0:T(8,128)(2,1)...) custom-call(s32[3]{0:T(128)S(1)} %pad_add_fusion.1.refs_0_.place_ref, s32[1]{0:T(128)} %bitcast.refs_2_.refs_0_.side_ref, ...), custom_call_target="tpu_custom_call" | custom-call | flops 4831838208 | bytes 27787280 | tf_op jit(solution)/shard_map/weight_two_grad/pallas_call | solution.py:670
  178.6 10.2 %conv_two_back.1 = (f32[1024,512]{1,0:T(8,128)S(1)}, f32[40,512]{1,0:T(8,128)S(1)}, f32[40,512]{1,0:T(8,128)S(1)}, f32[8,512]{1,0:T(8,128)S(1)}, f32[8,512]{1,0:T(8,128)S(1)}) custom-call(s32[1]{0:T(128)} %bitcast.refs_2_.refs_0_.side_ref, bf16[3,1088,512]{2,1,0:T(8,128)(2,1)S(1)} %get-tuple-element.165.shifted, bf16[9,1024,128]{2,1,0:T(8,128)(2,1)S(1)} %copy-done.29, ...), custom_call_target="tpu_custom_call" | custom-call | flops 4831838208 | bytes 19742724 | tf_op jit(solution)/shard_map/conv_two_back/pallas_call | solution.py:670
  199.0 8.5 %weight_one_grad.1 = (bf16[2,16,9,16,256]{4,3,2,1,0:T(8,128)(2,1)S(1)}, bf16[2,16,9,16,256]{4,3,2,1,0:T(8,128)(2,1)S(1)}, bf16[3,1088,512]{2,1,0:T(8,128)(2,1)S(1)}, f32[8,512]{1,0:T(8,128)S(1)}) custom-call(s32[3]{0:T(128)S(1)} %pad_add_fusion.1.refs_0_.place_ref, s32[1]{0:T(128)} %bitcast.refs_2_.refs_0_.side_ref, f32[1024,512]{1,0:T(8,128)S(1)} %copy-done.51, ...), custom_call_target="tpu_custom_call" | custom-call | flops 4831838208 | bytes 16252944 | tf_op jit(solution)/shard_map/weight_one_grad/pallas_call | solution.py:670
  215.1 9.9 %conv_one_back.1 = (f32[1024,512]{1,0:T(8,128)S(1)}, f32[40,512]{1,0:T(8,128)S(1)}, f32[40,512]{1,0:T(8,128)S(1)}, f32[8,512]{1,0:T(8,128)S(1)}, f32[8,512]{1,0:T(8,128)S(1)}) custom-call(s32[1]{0:T(128)} %bitcast.refs_2_.refs_0_.side_ref, bf16[3,1088,512]{2,1,0:T(8,128)(2,1)S(1)} %get-tuple-element.177.refs_1_, bf16[9,1024,128]{2,1,0:T(8,128)(2,1)S(1)} %copy-done.29, ...), custom_call_target="tpu_custom_call" | custom-call | flops 4831838208 | bytes 18694148 | tf_op jit(solution)/shard_map/conv_one_back/pallas_call | solution.py:670
  235.7 7.4 %collective-permute-done.35 = bf16[8,9,16,256]{3,2,1,0:T(8,128)(2,1)S(1)} collective-permute-done((bf16[8,9,16,256]{3,2,1,0:T(8,128)(2,1)S(1)}, bf16[8,9,16,256]{3,2,1,0:T(8,128)(2,1)S(1)}, u32[]{:S(2)}, u32[]{:S(2)}) %collective-permute-start.35) | collective-permute-done | bytes 589856 | tf_op jit(solution)/shard_map/ppermute | solution.py:622
  244.8 6.9 %collective-permute-done.43 = bf16[2,13,16,256]{3,2,1,0:T(8,128)(2,1)S(1)} collective-permute-done((bf16[2,13,16,256]{3,2,1,0:T(8,128)(2,1)S(1)}, bf16[2,13,16,256]{3,2,1,0:T(8,128)(2,1)S(1)}, u32[]{:S(2)}, u32[]{:S(2)}) %collective-permute-start.43) | collective-permute-done | bytes 213024 | tf_op jit(solution)/shard_map/ppermute | solution.py:622
  260.4 4.3 %collective-permute-done.51 = bf16[30,16,256]{2,1,0:T(8,128)(2,1)S(1)} collective-permute-done((bf16[30,16,256]{2,1,0:T(8,128)(2,1)S(1)}, bf16[30,16,256]{2,1,0:T(8,128)(2,1)S(1)}, u32[]{:S(2)}, u32[]{:S(2)}) %collective-permute-start.51) | collective-permute-done | bytes 245792 | tf_op jit(solution)/shard_map/ppermute | solution.py:622
  264.7 5.6 %collective-permute-done.50 = bf16[30,16,256]{2,1,0:T(8,128)(2,1)S(1)} collective-permute-done((bf16[30,16,256]{2,1,0:T(8,128)(2,1)S(1)}, bf16[30,16,256]{2,1,0:T(8,128)(2,1)S(1)}, u32[]{:S(2)}, u32[]{:S(2)}) %collective-permute-start.50) | collective-permute-done | bytes 245792 | tf_op jit(solution)/shard_map/ppermute | solution.py:622
  270.3 5.4 %collective-permute-done.49 = bf16[30,16,256]{2,1,0:T(8,128)(2,1)S(1)} collective-permute-done((bf16[30,16,256]{2,1,0:T(8,128)(2,1)S(1)}, bf16[30,16,256]{2,1,0:T(8,128)(2,1)S(1)}, u32[]{:S(2)}, u32[]{:S(2)}) %collective-permute-start.49) | collective-permute-done | bytes 245792 | tf_op jit(solution)/shard_map/ppermute | solution.py:622
  286.4 4.3 %collective-permute-done.46 = bf16[2,9,16,256]{3,2,1,0:T(8,128)(2,1)S(1)} collective-permute-done((bf16[2,9,16,256]{3,2,1,0:T(8,128)(2,1)S(1)}, bf16[2,9,16,256]{3,2,1,0:T(8,128)(2,1)S(1)}, u32[]{:S(2)}, u32[]{:S(2)}) %collective-permute-start.46) | collective-permute-done | bytes 147488 | tf_op jit(solution)/shard_map/ppermute | solution.py:622
  297.5 4.3 %collective-permute-done.54 = bf16[2,9,16,256]{3,2,1,0:T(8,128)(2,1)S(1)} collective-permute-done((bf16[2,9,16,256]{3,2,1,0:T(8,128)(2,1)S(1)}, bf16[2,9,16,256]{3,2,1,0:T(8,128)(2,1)S(1)}, u32[]{:S(2)}, u32[]{:S(2)}) %collective-permute-start.54) | collective-permute-done | bytes 147488 | tf_op jit(solution)/shard_map/ppermute | solution.py:622
  306.9 5.0 %collective-permute-done.60 = bf16[8,13,16,256]{3,2,1,0:T(8,128)(2,1)S(1)} collective-permute-done((bf16[8,13,16,256]{3,2,1,0:T(8,128)(2,1)S(1)}, bf16[8,13,16,256]{3,2,1,0:T(8,128)(2,1)S(1)}, u32[]{:S(2)}, u32[]{:S(2)}) %collective-permute-start.60) | collective-permute-done | bytes 852000 | tf_op jit(solution)/shard_map/ppermute | solution.py:622
  312.0 4.4 %collective-permute-done.59 = bf16[8,17,16,256]{3,2,1,0:T(8,128)(2,1)S(1)} collective-permute-done((bf16[8,17,16,256]{3,2,1,0:T(8,128)(2,1)S(1)}, bf16[8,17,16,256]{3,2,1,0:T(8,128)(2,1)S(1)}, u32[]{:S(2)}, u32[]{:S(2)}) %collective-permute-start.59) | collective-permute-done | bytes 1114144 | tf_op jit(solution)/shard_map/ppermute | solution.py:622
  323.2 6.7 %collective-permute-done.58 = bf16[4,9,16,256]{3,2,1,0:T(8,128)(2,1)S(1)} collective-permute-done((bf16[4,9,16,256]{3,2,1,0:T(8,128)(2,1)S(1)}, bf16[4,9,16,256]{3,2,1,0:T(8,128)(2,1)S(1)}, u32[]{:S(2)}, u32[]{:S(2)}) %collective-permute-start.58) | collective-permute-done | bytes 294944 | tf_op jit(solution)/shard_map/ppermute | solution.py:622
  332.6 6.8 %unpack_two.1 = (f32[18,512,512]{2,1,0:T(8,128)}, f32[2,512,512]{2,1,0:T(8,128)}, f32[512,512]{1,0:T(8,128)}, f32[512,512]{1,0:T(8,128)}) custom-call(s32[3]{0:T(128)S(1)} %pad_add_fusion.1.refs_0_.place_ref, bf16[16,30,16,256]{3,2,1,0:T(8,128)(2,1)S(1)} %maximum_maximum_fusion.own_ref, bf16[16,30,16,256]{3,2,1,0:T(8,128)(2,1)S(1)} %collective-permute-done.63.other_ref), custom_call_target="tpu_custom_call" | custom-call | bytes 30933004 | tf_op jit(solution)/shard_map/unpack_two/pallas_call | solution.py:670
  339.4 6.4 %collective-permute-done.62 = bf16[8,9,16,256]{3,2,1,0:T(8,128)(2,1)S(1)} collective-permute-done((bf16[8,9,16,256]{3,2,1,0:T(8,128)(2,1)S(1)}, bf16[8,9,16,256]{3,2,1,0:T(8,128)(2,1)S(1)}, u32[]{:S(2)}, u32[]{:S(2)}) %collective-permute-start.62) | collective-permute-done | bytes 589856 | tf_op jit(solution)/shard_map/ppermute | solution.py:622
  354.9 5.2 %unpack_one.1 = f32[18,512,512]{2,1,0:T(8,128)} custom-call(s32[3]{0:T(128)S(1)} %copy-done.27, bf16[2,16,9,16,256]{4,3,2,1,0:T(8,128)(2,1)S(1)} %pad_maximum_fusion.own_ref, bf16[2,16,9,16,256]{4,3,2,1,0:T(8,128)(2,1)} %collective-permute-done.65.other_ref, f32[18,512,512]{2,1,0:T(8,128)} %get-tuple-element.230.rest_0_), custom_call_target="tpu_custom_call", output_to_operand_aliasing={{}: (3, {})} | custom-call | bytes 42467340 | tf_op jit(solution)/shard_map/unpack_one/pallas_call | solution.py:670
  (337 shorter events, 150.8 us)
Async XLA Ops:
  0.7 34.7 %collective-permute-start = (bf16[1024,512]{1,0:T(8,128)(2,1)}, bf16[1024,512]{1,0:T(8,128)(2,1)S(1)}, u32[]{:S(2)}, u32[]{:S(2)}) collective-permute-start(bf16[1024,512]{1,0:T(8,128)(2,1)} %bitcast.106), channel_id=1, source_target_pairs={{0,0},{1,16},{2,2},{3,18},{4,4},{5,20},{6,6},{7,22},{8,8},{9,24},{... | collective-permute-start | bytes 3145736 | tf_op jit(solution)/shard_map/ppermute | solution.py:622
  13.4 20.1 %collective-permute-start.4 = (f32[8,512]{1,0:T(8,128)S(1)}, f32[8,512]{1,0:T(8,128)S(1)}, u32[]{:S(2)}, u32[]{:S(2)}) collective-permute-start(f32[8,512]{1,0:T(8,128)S(1)} %get-tuple-element.124), channel_id=1, source_target_pairs={{0,1},{1,17},{2,3},{3,19},{4,5},{5,21},{6,7},{7,23},{8,9},{9,25},{... | collective-permute-start | bytes 49160 | tf_op jit(solution)/shard_map/ppermute | solution.py:622
  14.7 18.8 %collective-permute-start.2 = (f32[40,512]{1,0:T(8,128)S(1)}, f32[40,512]{1,0:T(8,128)S(1)}, u32[]{:S(2)}, u32[]{:S(2)}) collective-permute-start(f32[40,512]{1,0:T(8,128)S(1)} %get-tuple-element.122), channel_id=1, source_target_pairs={{0,8},{1,24},{2,10},{3,26},{4,12},{5,28},{6,14},{7,30},{8,0},{9,16... | collective-permute-start | bytes 245768 | tf_op jit(solution)/shard_map/ppermute | solution.py:622
  16.3 17.2 %collective-permute-start.3 = (f32[40,512]{1,0:T(8,128)S(1)}, f32[40,512]{1,0:T(8,128)S(1)}, u32[]{:S(2)}, u32[]{:S(2)}) collective-permute-start(f32[40,512]{1,0:T(8,128)S(1)} %get-tuple-element.123), channel_id=1, source_target_pairs={{0,9},{1,25},{2,11},{3,27},{4,13},{5,29},{6,15},{7,31},{8,1},{9,17... | collective-permute-start | bytes 245768 | tf_op jit(solution)/shard_map/ppermute | solution.py:622
  35.4 18.0 %collective-permute-start.9 = (bf16[512,512]{1,0:T(8,128)(2,1)S(1)}, bf16[512,512]{1,0:T(8,128)(2,1)S(1)}, u32[]{:S(2)}, u32[]{:S(2)}) collective-permute-start(bf16[512,512]{1,0:T(8,128)(2,1)S(1)} %bitcast.116), channel_id=1, source_target_pairs={{0,0},{1,16},{2,2},{3,18},{4,4},{5,20},{6,6},{7,22},{8,8},{9,24},{... | collective-permute-start | bytes 1572872 | tf_op jit(solution)/shard_map/ppermute | solution.py:622
  53.4 16.2 %collective-permute-start.13 = (bf16[512,512]{1,0:T(8,128)(2,1)}, bf16[512,512]{1,0:T(8,128)(2,1)S(1)}, u32[]{:S(2)}, u32[]{:S(2)}) collective-permute-start(bf16[512,512]{1,0:T(8,128)(2,1)} %bitcast.5), channel_id=1, source_target_pairs={{0,0},{1,16},{2,2},{3,18},{4,4},{5,20},{6,6},{7,22},{8,8},{9,24},{... | collective-permute-start | bytes 1572872 | tf_op jit(solution)/shard_map/ppermute | solution.py:622
  74.8 25.6 %collective-permute-start.14 = (bf16[1024,512]{1,0:T(8,128)(2,1)S(1)}, bf16[1024,512]{1,0:T(8,128)(2,1)}, u32[]{:S(2)}, u32[]{:S(2)}) collective-permute-start(bf16[1024,512]{1,0:T(8,128)(2,1)S(1)} %normed.1.own_ref.refs_1_), channel_id=1, source_target_pairs={{0,8},{1,9},{2,10},{3,11},{4,12},{5,13},{6,14},{7,15},{8,0},{9,1},... | collective-permute-start | bytes 3145736 | tf_op jit(solution)/shard_map/ppermute | solution.py:622
  100.4 25.9 %collective-permute-start.18 = (bf16[1024,512]{1,0:T(8,128)(2,1)}, bf16[1024,512]{1,0:T(8,128)(2,1)}, u32[]{:S(2)}, u32[]{:S(2)}) collective-permute-start(bf16[1024,512]{1,0:T(8,128)(2,1)} %constant_dynamic-update-slice_fusion.cot_own.refs_6_.rest_0_), channel_id=1, source_target_pairs={{0,8},{1,9},{2,10},{3,11},{4,12},{5,13},{6,14},{7,15},{8,0},{9,1},... | collective-permute-start | bytes 3145736 | tf_op jit(solution)/shard_map/ppermute | solution.py:622
  130.4 32.9 %collective-permute-start.19 = (bf16[1,32,32,512]{3,2,1,0:T(8,128)(2,1)S(1)}, bf16[1,32,32,512]{3,2,1,0:T(8,128)(2,1)S(1)}, u32[]{:S(2)}, u32[]{:S(2)}) collective-permute-start(bf16[1,32,32,512]{3,2,1,0:T(8,128)(2,1)S(1)} %bitcast.108), channel_id=1, source_target_pairs={{0,0},{1,16},{2,2},{3,18},{4,4},{5,20},{6,6},{7,22},{8,8},{9,24},{... | collective-permute-start | bytes 3145736 | tf_op jit(solution)/shard_map/ppermute | solution.py:622
  190.1 21.0 %collective-permute-start.32 = (bf16[8,13,16,256]{3,2,1,0:T(8,128)(2,1)S(1)}, bf16[8,13,16,256]{3,2,1,0:T(8,128)(2,1)S(1)}, u32[]{:S(2)}, u32[]{:S(2)}) collective-permute-start(bf16[8,13,16,256]{3,2,1,0:T(8,128)(2,1)S(1)} %get-tuple-element.235), channel_id=1, source_target_pairs={{0,4},{1,5},{2,6},{3,7},{4,0},{5,1},{6,2},{7,3},{8,12},{9,13},{10,... | collective-permute-start | bytes 2555912 | tf_op jit(solution)/shard_map/ppermute | solution.py:622
  191.7 20.6 %collective-permute-start.31 = (bf16[8,13,16,256]{3,2,1,0:T(8,128)(2,1)S(1)}, bf16[8,13,16,256]{3,2,1,0:T(8,128)(2,1)S(1)}, u32[]{:S(2)}, u32[]{:S(2)}) collective-permute-start(bf16[8,13,16,256]{3,2,1,0:T(8,128)(2,1)S(1)} %get-tuple-element.236), channel_id=1, source_target_pairs={{0,2},{1,3},{2,0},{3,1},{4,6},{5,7},{6,4},{7,5},{8,10},{9,11},{10,... | collective-permute-start | bytes 2555912 | tf_op jit(solution)/shard_map/ppermute | solution.py:622
  212.3 14.9 %collective-permute-start.33 = (bf16[2,16,9,16,256]{4,3,2,1,0:T(8,128)(2,1)S(1)}, bf16[2,16,9,16,256]{4,3,2,1,0:T(8,128)(2,1)S(1)}, u32[]{:S(2)}, u32[]{:S(2)}) collective-permute-start(bf16[2,16,9,16,256]{4,3,2,1,0:T(8,128)(2,1)S(1)} %get-tuple-element.176), channel_id=1, source_target_pairs={{0,1},{1,0},{2,3},{3,2},{4,5},{5,4},{6,7},{7,6},{8,9},{9,8},{10,11... | collective-permute-start | bytes 7077896 | tf_op jit(solution)/shard_map/ppermute | solution.py:622
  228.1 15.1 %collective-permute-start.35 = (bf16[8,9,16,256]{3,2,1,0:T(8,128)(2,1)S(1)}, bf16[8,9,16,256]{3,2,1,0:T(8,128)(2,1)S(1)}, u32[]{:S(2)}, u32[]{:S(2)}) collective-permute-start(bf16[8,9,16,256]{3,2,1,0:T(8,128)(2,1)S(1)} %get-tuple-element.239), channel_id=1, source_target_pairs={{0,4},{1,5},{2,6},{3,7},{4,0},{5,1},{6,2},{7,3},{8,12},{9,13},{10,... | collective-permute-start | bytes 1769480 | tf_op jit(solution)/shard_map/ppermute | solution.py:622
  229.7 14.7 %collective-permute-start.34 = (bf16[8,9,16,256]{3,2,1,0:T(8,128)(2,1)S(1)}, bf16[8,9,16,256]{3,2,1,0:T(8,128)(2,1)S(1)}, u32[]{:S(2)}, u32[]{:S(2)}) collective-permute-start(bf16[8,9,16,256]{3,2,1,0:T(8,128)(2,1)S(1)} %get-tuple-element.240), channel_id=1, source_target_pairs={{0,2},{1,3},{2,0},{3,1},{4,6},{5,7},{6,4},{7,5},{8,10},{9,11},{10,... | collective-permute-start | bytes 1769480 | tf_op jit(solution)/shard_map/ppermute | solution.py:622
  230.6 14.3 %collective-permute-start.45 = (bf16[2,13,16,256]{3,2,1,0:T(8,128)(2,1)S(1)}, bf16[2,13,16,256]{3,2,1,0:T(8,128)(2,1)S(1)}, u32[]{:S(2)}, u32[]{:S(2)}) collective-permute-start(bf16[2,13,16,256]{3,2,1,0:T(8,128)(2,1)S(1)} %get-tuple-element.245), channel_id=1, source_target_pairs={{0,24},{1,25},{2,26},{3,27},{4,28},{5,29},{6,30},{7,31},{8,16},{9,... | collective-permute-start | bytes 638984 | tf_op jit(solution)/shard_map/ppermute | solution.py:622
  233.2 18.5 %collective-permute-start.43 = (bf16[2,13,16,256]{3,2,1,0:T(8,128)(2,1)S(1)}, bf16[2,13,16,256]{3,2,1,0:T(8,128)(2,1)S(1)}, u32[]{:S(2)}, u32[]{:S(2)}) collective-permute-start(bf16[2,13,16,256]{3,2,1,0:T(8,128)(2,1)S(1)} %get-tuple-element.247), channel_id=1, source_target_pairs={{0,16},{1,17},{2,18},{3,19},{4,20},{5,21},{6,22},{7,23},{8,24},{9,... | collective-permute-start | bytes 638984 | tf_op jit(solution)/shard_map/ppermute | solution.py:622
  233.4 18.2 %collective-permute-start.44 = (bf16[2,13,16,256]{3,2,1,0:T(8,128)(2,1)S(1)}, bf16[2,13,16,256]{3,2,1,0:T(8,128)(2,1)S(1)}, u32[]{:S(2)}, u32[]{:S(2)}) collective-permute-start(bf16[2,13,16,256]{3,2,1,0:T(8,128)(2,1)S(1)} %get-tuple-element.248), channel_id=1, source_target_pairs={{0,8},{1,9},{2,10},{3,11},{4,12},{5,13},{6,14},{7,15},{8,0},{9,1},... | collective-permute-start | bytes 638984 | tf_op jit(solution)/shard_map/ppermute | solution.py:622
  256.6 19.0 %collective-permute-start.49 = (bf16[30,16,256]{2,1,0:T(8,128)(2,1)S(1)}, bf16[30,16,256]{2,1,0:T(8,128)(2,1)S(1)}, u32[]{:S(2)}, u32[]{:S(2)}) collective-permute-start(bf16[30,16,256]{2,1,0:T(8,128)(2,1)S(1)} %pad_maximum_fusion.9), channel_id=1, source_target_pairs={{0,16},{1,17},{2,18},{3,19},{4,20},{5,21},{6,22},{7,23},{8,24},{9,... | collective-permute-start | bytes 737288 | tf_op jit(solution)/shard_map/ppermute | solution.py:622
  275.9 14.9 %collective-permute-start.55 = (bf16[4,17,16,256]{3,2,1,0:T(8,128)(2,1)S(1)}, bf16[4,17,16,256]{3,2,1,0:T(8,128)(2,1)S(1)}, u32[]{:S(2)}, u32[]{:S(2)}) collective-permute-start(bf16[4,17,16,256]{3,2,1,0:T(8,128)(2,1)S(1)} %pad_maximum_fusion.8), channel_id=1, source_target_pairs={{0,4},{1,5},{2,6},{3,7},{4,0},{5,1},{6,2},{7,3},{8,12},{9,13},{10,... | collective-permute-start | bytes 1671176 | tf_op jit(solution)/shard_map/ppermute | solution.py:622
  290.9 25.4 %collective-permute-start.59 = (bf16[8,17,16,256]{3,2,1,0:T(8,128)(2,1)S(1)}, bf16[8,17,16,256]{3,2,1,0:T(8,128)(2,1)S(1)}, u32[]{:S(2)}, u32[]{:S(2)}) collective-permute-start(bf16[8,17,16,256]{3,2,1,0:T(8,128)(2,1)S(1)} %pad_maximum_fusion.1), channel_id=1, source_target_pairs={{0,2},{1,3},{2,0},{3,1},{4,6},{5,7},{6,4},{7,5},{8,10},{9,11},{10,... | collective-permute-start | bytes 3342344 | tf_op jit(solution)/shard_map/ppermute | solution.py:622
  292.7 19.3 %collective-permute-start.60 = (bf16[8,13,16,256]{3,2,1,0:T(8,128)(2,1)S(1)}, bf16[8,13,16,256]{3,2,1,0:T(8,128)(2,1)S(1)}, u32[]{:S(2)}, u32[]{:S(2)}) collective-permute-start(bf16[8,13,16,256]{3,2,1,0:T(8,128)(2,1)S(1)} %pad_maximum_fusion.4), channel_id=1, source_target_pairs={{0,4},{1,5},{2,6},{3,7},{4,0},{5,1},{6,2},{7,3},{8,12},{9,13},{10,... | collective-permute-start | bytes 2555912 | tf_op jit(solution)/shard_map/ppermute | solution.py:622
  322.5 24.0 %collective-permute-start.64 = (bf16[1,32,32,512]{3,2,1,0:T(8,128)(2,1)S(1)}, bf16[1,32,32,512]{3,2,1,0:T(8,128)(2,1)S(1)}, u32[]{:S(2)}, u32[]{:S(2)}) collective-permute-start(bf16[1,32,32,512]{3,2,1,0:T(8,128)(2,1)S(1)} %bitcast.109), channel_id=1, source_target_pairs={{0,0},{1,16},{2,2},{3,18},{4,4},{5,20},{6,6},{7,22},{8,8},{9,24},{... | collective-permute-start | bytes 3145736 | tf_op jit(solution)/shard_map/ppermute | solution.py:622
  331.1 14.6 %collective-permute-start.62 = (bf16[8,9,16,256]{3,2,1,0:T(8,128)(2,1)S(1)}, bf16[8,9,16,256]{3,2,1,0:T(8,128)(2,1)S(1)}, u32[]{:S(2)}, u32[]{:S(2)}) collective-permute-start(bf16[8,9,16,256]{3,2,1,0:T(8,128)(2,1)S(1)} %pad_maximum_fusion.7), channel_id=1, source_target_pairs={{0,4},{1,5},{2,6},{3,7},{4,0},{5,1},{6,2},{7,3},{8,12},{9,13},{10,... | collective-permute-start | bytes 1769480 | tf_op jit(solution)/shard_map/ppermute | solution.py:622
  331.7 14.3 %collective-permute-start.61 = (bf16[8,9,16,256]{3,2,1,0:T(8,128)(2,1)S(1)}, bf16[8,9,16,256]{3,2,1,0:T(8,128)(2,1)S(1)}, u32[]{:S(2)}, u32[]{:S(2)}) collective-permute-start(bf16[8,9,16,256]{3,2,1,0:T(8,128)(2,1)S(1)} %pad_maximum_fusion.6), channel_id=1, source_target_pairs={{0,2},{1,3},{2,0},{3,1},{4,6},{5,7},{6,4},{7,5},{8,10},{9,11},{10,... | collective-permute-start | bytes 1769480 | tf_op jit(solution)/shard_map/ppermute | solution.py:622
  (118 other events, 1271.8 us)
